TPU v7x, 32 devices: a whole 2x2x4 slice. The times are simulated.
32 devices in a mesh: row: 8 (over z, core), col: 4 (over y, x).
Axes of the slice: x: 2, y: 2, z: 4, core: 2. Of those that a mesh axis runs over, the one named last changes fastest.
Arguments:
- front_blocks: bfloat16 [32, 5, 512, 512], P('row'), may hold values from -0.125 to 0.125
- block_cols: int32 [32, 5], P('row'), may hold values from 0 to 31, as said below
- samples: bfloat16 [16384, 1024], P('row', 'col'), may hold values from -6 to 6
- sketch_matrix: bfloat16 [1024, 256], replicated, may hold values from -0.1875 to 0.1875
Outputs:
- leaf_bases: bfloat16 [16384, 256], P('row')
- top_transfers: bfloat16 [1024, 256], P('row')
Inputs may be any that keep to these rules, and one draw needn't show every extreme that they name: `block_cols`: each row lists 5 different block columns; the first is the row's own index, the second lies in the other half of the 32 block columns (its index differs in the highest bit).
All inputs are finite; a program needn't handle non-finite values.
Results may differ from a plain program's by a relative error of at most 0.035.
Values may be sent and summed in bfloat16 or wider, within the bound.
A program may use at most 128 MiB of HBM per device.

v0:
```python
import math

import jax
import jax.numpy as jnp
from jax import lax
from jax.sharding import PartitionSpec as P


def partner_2(value, axis, stride):
    mask = 2**stride
    pairs = [(source, source ^ mask) for source in range(lax.axis_size(axis))]
    return lax.ppermute(value, axis, pairs)


def cholqr(sketch):
    highest = lax.Precision.HIGHEST
    gram_matrix = jnp.dot(sketch.T, sketch, precision=highest)
    low_factor = jnp.linalg.cholesky(gram_matrix)
    identity = jnp.eye(sketch.shape[1], dtype=sketch.dtype)
    low_inverse = jax.scipy.linalg.solve_triangular(low_factor, identity, lower=True)
    ortho_basis = jnp.dot(sketch, low_inverse.T, precision=highest)
    return (ortho_basis * math.sqrt(sketch.shape[0])).astype(jnp.bfloat16)


def off_products(all_sketched, front_blocks, block_cols, leaf_ids, top_level):
    leaf_total = all_sketched.shape[0] // front_blocks.shape[2]
    gathered_blocks = all_sketched.reshape(
        leaf_total, front_blocks.shape[2], all_sketched.shape[1]
    )[block_cols]
    products = jnp.einsum(
        "nkab,nkbc->nkac", front_blocks, gathered_blocks, preferred_element_type=jnp.float32
    )
    level_ids = jnp.arange(top_level, dtype=jnp.int32)
    outside = (
        jnp.right_shift(leaf_ids[:, None, None], level_ids[None, :, None])
        != jnp.right_shift(block_cols[:, None, :], level_ids[None, :, None])
    ).astype(jnp.float32)
    return jnp.einsum("nlk,nkac->nlac", outside, products, precision=lax.Precision.HIGHEST).astype(
        jnp.bfloat16
    )


def shards(front_blocks, block_cols, samples, sketch_matrix):
    leaf_dev = front_blocks.shape[0]
    leaf_size = front_blocks.shape[2]
    rank_size = sketch_matrix.shape[1]
    cols_dev = samples.shape[1]
    size_rows = lax.axis_size("row")
    row_index = lax.axis_index("row")
    leaf_total = leaf_dev * size_rows
    top_level = leaf_total.bit_length() - 1
    local_levels = leaf_dev.bit_length() - 1
    leaf_ids = row_index * leaf_dev + jnp.arange(leaf_dev, dtype=jnp.int32)
    local_rows = lax.dynamic_slice_in_dim(
        sketch_matrix, lax.axis_index("col") * cols_dev, cols_dev, 0
    )
    partial_sum = jnp.dot(samples, local_rows, preferred_element_type=jnp.float32)
    sketched = lax.psum(partial_sum.astype(jnp.bfloat16), "col")
    all_sketched = lax.all_gather(sketched, "row", axis=0, tiled=True)
    off_samples = off_products(all_sketched, front_blocks, block_cols, leaf_ids, top_level)
    leaf_basis = jax.vmap(cholqr)(off_samples[:, 0].astype(jnp.float32))
    carried = jnp.einsum(
        "nar,nlac->nlrc", leaf_basis, off_samples[:, 1:], preferred_element_type=jnp.float32
    )
    carried = (carried * (1.0 / math.sqrt(leaf_size))).astype(jnp.bfloat16)
    scale_pair = 1.0 / math.sqrt(2 * rank_size)
    transfer = None
    for tree_level in range(1, top_level):
        if carried.shape[0] >= 2:
            node_count = carried.shape[0] // 2
            paired = carried.reshape(node_count, 2, carried.shape[1], rank_size, rank_size)
            stacked = jnp.concatenate([paired[:, 0], paired[:, 1]], axis=2)
        else:
            swap_bit = tree_level - local_levels - 1
            is_left = jnp.right_shift(row_index, swap_bit) % 2 == 0
            partner = partner_2(carried, "row", swap_bit)
            left_part = jnp.where(is_left, carried, partner)
            right_part = jnp.where(is_left, partner, carried)
            stacked = jnp.concatenate([left_part, right_part], axis=2)
        transfer = jax.vmap(cholqr)(stacked[:, 0].astype(jnp.float32))
        if tree_level < top_level - 1:
            moved = jnp.einsum(
                "npr,nlpc->nlrc", transfer, stacked[:, 1:], preferred_element_type=jnp.float32
            )
            carried = (moved * scale_pair).astype(jnp.bfloat16)
    out_rows = 4 * rank_size // size_rows
    offset = row_index % (size_rows // 2) * out_rows
    top_rows = lax.dynamic_slice_in_dim(transfer[0], offset, out_rows, 0)
    return (leaf_basis.reshape(leaf_dev * leaf_size, rank_size), top_rows)


def solution(mesh):
    placed = (P("row", None, None, None), P("row", None), P("row", "col"), P())
    return jax.shard_map(
        shards,
        mesh=mesh,
        in_specs=placed,
        out_specs=(P("row", None), P("row", None)),
        check_vma=False,
    )
```

profile of v0, /device:TPU:0, one launch (start us, length us, event | category | flops | bytes accessed | tf_op | source)
XLA Modules:
  0.0 784.3 jit_solution(8630957988484231931)
XLA Ops:
  7.2 1.2 copy-done
  8.4 2.4 fusion.2
  10.8 56.1 %all-reduce.5.cloned.1.call-done = bf16[2048,256]{0,1:T(8,128)(2,1)} async-done(((bf16[2048,256]{0,1:T(8,128)(2,1)}), bf16[2048,256]{0,1:T(8,128)(2,1)}) %all-reduce.5.cloned.1.call-update) | async-done | bytes 1048592 | tf_op jit(solution)/shard_map/psum | solution.py:58
  69.7 80.9 %all-gather.2.cloned.1.call-done = bf16[16384,256]{0,1:T(8,128)(2,1)} async-done(((bf16[2048,256]{0,1:T(8,128)(2,1)}), bf16[16384,256]{0,1:T(8,128)(2,1)}) %all-gather.2.cloned.1.call-update) | async-done | bytes 8388624 | tf_op jit(solution)/shard_map/all_gather | solution.py:59
  150.6 11.9 %copy.101 = bf16[16384,256]{1,0:T(8,128)(2,1)} copy(bf16[16384,256]{0,1:T(8,128)(2,1)} %all-gather.2.cloned.1.call-done) | data formatting | bytes 16777216 | tf_op jit(solution)/shard_map/reshape | solution.py:27
  162.5 7.5 gather_fusion
  170.0 12.5 %convolution_bitcast_fusion = f32[4,5,512,256]{2,3,1,0:T(8,128)} fusion(bf16[4,5,512,256]{3,2,1,0:T(8,128)(2,1)} %bitcast.353, bf16[4,5,512,512]{3,2,1,0:T(8,128)(2,1)} %param.7), kind=kOutput, calls=%fused_computation.15 | convolution fusion | flops 2684354560 | bytes 26214400 | tf_op jit(solution)/shard_map/nkab,nkbc->nkac/dot_general | solution.py:30
  182.5 17.1 %copy.57 = f32[4,5,512,256]{3,1,2,0:T(8,128)} copy(f32[4,5,512,256]{2,3,1,0:T(8,128)} %convolution_bitcast_fusion) | data formatting | bytes 20971520 | tf_op jit(solution)/shard_map/nkab,nkbc->nkac/dot_general | solution.py:30
  199.6 11.9 %convolution_convert_fusion = bf16[4,5,512,256]{3,1,2,0:T(8,128)(2,1)S(1)} fusion(f32[4,5,512,256]{3,1,2,0:T(8,128)} %copy.57, s32[4,5]{1,0:T(4,128)S(1)} %copy-done.7, s32[4,5]{1,0:T(4,128)S(1)} %iota_shift-right-arithmetic_fusion), kind=kOutput, calls=%fused_computation.11 | convolution fusion | flops 159908032 | bytes 15728800 | tf_op jit(solution)/shard_map/nlk,nkac->nlac/dot_general | solution.py:38
  211.5 1.4 slice.224
  213.0 4.2 slice.225
  218.2 46.9 %custom-call.47 = f32[4,128,128]{2,1,0:T(8,128)S(1)} custom-call(f32[4,128,128]{2,1,0:T(8,128)S(1)} %cholesky.503), custom_call_target="Cholesky" | custom-call | tf_op jit(solution)/shard_map/vmap(jit(cholesky))/cholesky | solution.py:18
  265.1 0.7 select_bitcast_fusion
  265.8 39.3 %custom-call.48 = f32[4,1,128,128]{2,3,1,0:T(8,128)S(1)} custom-call(f32[4,1,128,128]{3,2,1,0:T(8,128)S(1)} %select_bitcast_fusion), custom_call_target="InvertDiagBlocksLowerTriangular" | custom-call | tf_op jit(solution)/shard_map/vmap(jit(cholesky))/cholesky | solution.py:18
  306.3 47.3 %custom-call.49 = f32[4,128,128]{2,1,0:T(8,128)S(1)} custom-call(f32[4,128,128]{2,1,0:T(8,128)S(1)} %convolution_subtract_fusion.2), custom_call_target="Cholesky" | custom-call | tf_op jit(solution)/shard_map/vmap(jit(cholesky))/cholesky | solution.py:18
  353.9 1.0 select_select_fusion
  355.6 5.3 while.8
  356.2 2.1 bitcast_dynamic-update-slice_fusion.13
  358.8 2.1 bitcast_dynamic-update-slice_fusion.13
  360.9 79.4 %custom-call.50 = f32[4,2,128,128]{2,3,1,0:T(8,128)S(1)} custom-call(f32[4,2,128,128]{3,2,1,0:T(8,128)} %bitcast.368), custom_call_target="InvertDiagBlocksLowerTriangular" | custom-call | tf_op jit(solution)/shard_map/vmap(jit(_solve_triangular))/triangular_solve | solution.py:20
  441.0 1.8 convolution_subtract_fusion
  443.4 2.7 multiply_convert_fusion.1
  446.1 1.4 multiply_convert_fusion
  448.3 1.0 copy.70
  449.3 1.1 fusion.46
  450.4 0.8 copy-done.5
  451.2 23.6 %custom-call.51 = f32[2,128,128]{2,1,0:T(8,128)S(1)} custom-call(f32[2,128,128]{2,1,0:T(8,128)S(1)} %cholesky.506), custom_call_target="Cholesky" | custom-call | tf_op jit(solution)/shard_map/vmap(jit(cholesky))/cholesky | solution.py:18
  474.8 1.4 select_bitcast_fusion.1
  476.2 21.1 %custom-call.52 = f32[2,1,128,128]{2,3,1,0:T(8,128)} custom-call(f32[2,1,128,128]{3,2,1,0:T(8,128)} %select_bitcast_fusion.1), custom_call_target="InvertDiagBlocksLowerTriangular" | custom-call | tf_op jit(solution)/shard_map/vmap(jit(cholesky))/cholesky | solution.py:18
  497.3 1.2 constant_dynamic-update-slice_fusion.4
  498.6 2.0 convolution_subtract_fusion.3
  500.5 24.9 %custom-call.53 = f32[2,128,128]{2,1,0:T(8,128)} custom-call(f32[2,128,128]{2,1,0:T(8,128)} %convolution_subtract_fusion.3), custom_call_target="Cholesky" | custom-call | tf_op jit(solution)/shard_map/vmap(jit(cholesky))/cholesky | solution.py:18
  525.4 0.9 select_reduce_fusion.2
  527.1 1.2 select_select_fusion.1
  528.3 6.5 while.9
  529.5 2.0 bitcast_dynamic-update-slice_fusion.14
  532.8 2.0 bitcast_dynamic-update-slice_fusion.14
  534.8 41.1 %custom-call.54 = f32[2,2,128,128]{2,3,1,0:T(8,128)} custom-call(f32[2,2,128,128]{3,2,1,0:T(8,128)} %bitcast.369), custom_call_target="InvertDiagBlocksLowerTriangular" | custom-call | tf_op jit(solution)/shard_map/vmap(jit(_solve_triangular))/triangular_solve | solution.py:20
  575.9 1.4 fusion.76
  577.3 1.3 convolution_subtract_fusion.1
  578.6 1.3 fusion.75
  581.8 11.7 %custom-call.63 = f32[1,128,128]{2,1,0:T(8,128)S(1)} custom-call(f32[1,128,128]{2,1,0:T(8,128)S(1)} %cholesky.509), custom_call_target="Cholesky" | custom-call | tf_op jit(solution)/shard_map/vmap(jit(cholesky))/cholesky | solution.py:18
  593.6 9.8 %custom-call.64 = f32[1,1,128,128]{2,3,1,0:T(8,128)S(1)} custom-call(f32[1,1,128,128]{3,2,1,0:T(8,128)S(1)} %get-tuple-element.120), custom_call_target="InvertDiagBlocksLowerTriangular" | custom-call | tf_op jit(solution)/shard_map/vmap(jit(cholesky))/cholesky | solution.py:18
  603.9 11.9 %custom-call.65 = f32[1,128,128]{2,1,0:T(8,128)S(1)} custom-call(f32[1,128,128]{2,1,0:T(8,128)S(1)} %fusion.28), custom_call_target="Cholesky" | custom-call | tf_op jit(solution)/shard_map/vmap(jit(cholesky))/cholesky | solution.py:18
  618.6 4.1 while.10
  619.2 1.4 bitcast_dynamic-update-slice_fusion.15
  621.2 1.4 bitcast_dynamic-update-slice_fusion.15
  622.7 19.7 %custom-call.66 = f32[1,2,128,128]{2,3,1,0:T(8,128)S(1)} custom-call(f32[1,2,128,128]{3,2,1,0:T(8,128)S(1)} %bitcast.366), custom_call_target="InvertDiagBlocksLowerTriangular" | custom-call | tf_op jit(solution)/shard_map/vmap(jit(_solve_triangular))/triangular_solve | solution.py:20
  644.4 1.3 collective-permute-done
  646.2 11.7 %custom-call.67 = f32[1,128,128]{2,1,0:T(8,128)S(1)} custom-call(f32[1,128,128]{2,1,0:T(8,128)S(1)} %cholesky.512), custom_call_target="Cholesky" | custom-call | tf_op jit(solution)/shard_map/vmap(jit(cholesky))/cholesky | solution.py:18
  657.9 9.8 %custom-call.68 = f32[1,1,128,128]{2,3,1,0:T(8,128)S(1)} custom-call(f32[1,1,128,128]{3,2,1,0:T(8,128)S(1)} %get-tuple-element.116), custom_call_target="InvertDiagBlocksLowerTriangular" | custom-call | tf_op jit(solution)/shard_map/vmap(jit(cholesky))/cholesky | solution.py:18
  668.2 11.7 %custom-call.69 = f32[1,128,128]{2,1,0:T(8,128)S(1)} custom-call(f32[1,128,128]{2,1,0:T(8,128)S(1)} %fusion.29), custom_call_target="Cholesky" | custom-call | tf_op jit(solution)/shard_map/vmap(jit(cholesky))/cholesky | solution.py:18
  682.7 4.1 while.11
  683.3 1.3 bitcast_dynamic-update-slice_fusion.16
  685.4 1.3 bitcast_dynamic-update-slice_fusion.16
  686.7 19.9 %custom-call.70 = f32[1,2,128,128]{2,3,1,0:T(8,128)S(1)} custom-call(f32[1,2,128,128]{3,2,1,0:T(8,128)S(1)} %bitcast.367), custom_call_target="InvertDiagBlocksLowerTriangular" | custom-call | tf_op jit(solution)/shard_map/vmap(jit(_solve_triangular))/triangular_solve | solution.py:20
  708.4 5.6 collective-permute-done.1
  714.5 11.7 %custom-call.71 = f32[1,128,128]{2,1,0:T(8,128)S(1)} custom-call(f32[1,128,128]{2,1,0:T(8,128)S(1)} %cholesky.515), custom_call_target="Cholesky" | custom-call | tf_op jit(solution)/shard_map/vmap(jit(cholesky))/cholesky | solution.py:18
  726.2 9.8 %custom-call.72 = f32[1,1,128,128]{2,3,1,0:T(8,128)S(1)} custom-call(f32[1,1,128,128]{3,2,1,0:T(8,128)S(1)} %get-tuple-element.112), custom_call_target="InvertDiagBlocksLowerTriangular" | custom-call | tf_op jit(solution)/shard_map/vmap(jit(cholesky))/cholesky | solution.py:18
  736.5 11.7 %custom-call.73 = f32[1,128,128]{2,1,0:T(8,128)S(1)} custom-call(f32[1,128,128]{2,1,0:T(8,128)S(1)} %fusion.30), custom_call_target="Cholesky" | custom-call | tf_op jit(solution)/shard_map/vmap(jit(cholesky))/cholesky | solution.py:18
  751.0 4.1 while.12
  751.7 1.4 bitcast_dynamic-update-slice_fusion.17
  753.7 1.4 bitcast_dynamic-update-slice_fusion.17
  755.1 19.9 %custom-call.74 = f32[1,2,128,128]{2,3,1,0:T(8,128)S(1)} custom-call(f32[1,2,128,128]{3,2,1,0:T(8,128)S(1)} %bitcast.365), custom_call_target="InvertDiagBlocksLowerTriangular" | custom-call | tf_op jit(solution)/shard_map/vmap(jit(_solve_triangular))/triangular_solve | solution.py:20
  (142 shorter events, 30.2 us)
Async XLA Ops:
  7.2 1.2 copy-start
  7.2 59.8 %copy-start.7 = (s32[4,5]{1,0:T(4,128)S(1)}, s32[4,5]{1,0:T(4,128)}, u32[]{:S(2)}) copy-start(s32[4,5]{1,0:T(4,128)} %param.8) | copy-start | bytes 244
  7.2 59.8 %all-reduce.5.cloned.1.call-start = ((), (), s32[]{:S(2)}) async-start(), calls=%async_computation | async-start | bytes 2097152 | tf_op jit(solution)/shard_map/psum | solution.py:58
  10.8 139.9 %all-gather.2.cloned.1.call-start = ((), (), s32[]{:S(2)}) async-start(), calls=%async_computation.1 | async-start | bytes 9437184 | tf_op jit(solution)/shard_map/all_gather | solution.py:59
  69.7 370.6 %copy-start.6 = (f32[128,256]{1,0:T(8,128)}, f32[128,256]{1,0:T(8,128)S(1)}, u32[]{:S(2)}) copy-start(f32[128,256]{1,0:T(8,128)S(1)} %get-tuple-element.106) | copy-start | bytes 393220
  213.0 4.2 copy-start.3
  360.9 86.6 %copy-start.9 = (s32[2,2]{1,0:T(2,128)}, s32[2,2]{1,0:T(2,128)S(1)}, u32[]{:S(2)}) copy-start(s32[2,2]{1,0:T(2,128)S(1)} %get-tuple-element.370) | copy-start | bytes 52
  440.3 5.8 copy-start.2
  446.1 1.4 copy-start.8
  450.4 0.8 copy-start.5
  526.3 0.8 copy-start.4
  581.3 37.3 %copy-start.10 = (s32[2,2]{1,0:T(2,128)S(1)}, s32[2,2]{1,0:T(2,128)}, u32[]{:S(2)}) copy-start(s32[2,2]{1,0:T(2,128)} %get-tuple-element.371) | copy-start | bytes 52
  644.1 1.6 collective-permute-start
  707.5 69.5 %copy-start.1 = (bf16[2048,256]{1,0:T(8,128)(2,1)S(1)}, bf16[2048,256]{1,0:T(8,128)(2,1)}, u32[]{:S(2)}) copy-start(bf16[2048,256]{1,0:T(8,128)(2,1)} %param.9) | copy-start | bytes 3145732
  708.2 5.7 collective-permute-start.1
Sparse Core Ops, SparseCore 0:
  11.7 55.2 all-reduce.4
  68.6 82.0 all-gather.1
where the time goes:
time: 793 us; the launch traced here: 784 us
  other arithmetic  497 us (63%)
  waiting for transfers between devices  144 us (18%)
  local copies, waits for them, and re-layouts  72.3 us (9%)
  matrix products  51.1 us (6%)
  between operations  19.2 us (2%)
    another operation x38, other arithmetic, cholqr(): low_factor = jnp.linalg.cholesky(gram_matrix)  311 us
    another operation x12, other arithmetic, cholqr(): jax.scipy.linalg.solve_triangular(low_factor, identity, lower=True)  184 us
    all_gather x1, waiting for transfers between devices, shards(): all_sketched = lax.all_gather(sketched, 'row', axis=0, tiled=True)  80.9 us
    psum x1, waiting for transfers between devices, shards(): sketched = lax.psum(partial_sum.astype(jnp.bfloat16), 'col')  56.1 us
    dot_general x1, local copies, waits for them, and re-layouts, off_products(): jnp.einsum('nkab,nkbc->nkac', front_blocks, gathered_blocks, preferred_el...  17.1 us
  transfers between devices with their start and end apart: 4, of which 4 were waited for; matrix products, arithmetic and copies ran while one was open for 0% of the time, Pallas kernels for 0%

commit v1 on v0

v1 whole, which is shorter than its diff:
```python
import functools
import math

import jax
import jax.numpy as jnp
from jax import lax
from jax.experimental import pallas as pl
from jax.experimental.pallas import tpu as pltpu
from jax.sharding import PartitionSpec as P

PANEL = 32
STEP = 4
NT = (((1,), (1,)), ((), ()))
TN = (((0,), (0,)), ((), ()))


def swap(value, axis, mask):
    pairs = [(source, source ^ mask) for source in range(lax.axis_size(axis))]
    return lax.ppermute(value, axis, pairs)


def split3(value):
    high = value.astype(jnp.bfloat16)
    rest = value - high.astype(jnp.float32)
    mid = rest.astype(jnp.bfloat16)
    low = (rest - mid.astype(jnp.float32)).astype(jnp.bfloat16)
    return high, mid, low


def eliminate_panel(panel, start):
    rows, width = panel.shape
    row_ids = lax.broadcasted_iota(jnp.int32, (rows, 128), 0)
    wide_rows = lax.broadcasted_iota(jnp.int32, (rows, width), 0)
    lanes = lax.broadcasted_iota(jnp.int32, (rows, width), 1)
    pivots = jnp.ones((rows, 128), jnp.float32)
    for first in range(0, rows, STEP):
        cols = [
            jnp.broadcast_to(panel[:, start + first + t : start + first + t + 1], (rows, 128))
            for t in range(STEP)
        ]
        for t in range(STEP):
            j = first + t
            pivot = cols[t][j : j + 1, :]
            pivots = jnp.where(row_ids == j, pivot, pivots)
            factor = jnp.where(row_ids > j, cols[t] * (1.0 / pivot), 0.0)
            for u in range(t + 1, STEP):
                cols[u] = cols[u] - factor * cols[u][j : j + 1, :]
            panel = jnp.where(
                lanes == start + j, jnp.where(wide_rows == j, 1.0, 0.0), panel
            )
            panel = panel - jnp.concatenate([factor] * (width // 128), axis=1) * panel[j : j + 1, :]
    scale = lax.rsqrt(pivots)
    panel = panel * jnp.concatenate([scale] * (width // 128), axis=1)
    corner = (lanes > wide_rows + start) & (lanes < start + rows)
    return jnp.where(corner, 0.0, panel)


def cholqr_kernel(samples_ref, basis_ref, *rest):
    work_ref = rest[-1]
    rank = samples_ref.shape[1]
    count = samples_ref.shape[2]
    work_ref[...] = lax.dot_general(
        samples_ref[0], samples_ref[0], NT, preferred_element_type=jnp.float32
    )
    for start in range(0, rank, PANEL):
        end = start + PANEL
        panel = eliminate_panel(work_ref[start:end, :], start)
        work_ref[start:end, :] = panel
        if end < rank:
            update = lax.dot_general(
                panel, panel, TN, precision=lax.Precision.HIGHEST,
                preferred_element_type=jnp.float32,
            )
            later = work_ref[end:, :]
            lanes = lax.broadcasted_iota(jnp.int32, later.shape, 1)
            done = (lanes >= start) & (lanes < end)
            work_ref[end:, :] = jnp.where(done, 0.0, later) - update[end:, :]
    shape = (rank, rank)
    lower = lax.broadcasted_iota(jnp.int32, shape, 1) <= lax.broadcasted_iota(jnp.int32, shape, 0)
    inverse = jnp.where(lower, work_ref[...], 0.0)
    total = None
    for part in reversed(split3(inverse)):
        term = jnp.dot(part, samples_ref[0], preferred_element_type=jnp.float32)
        total = term if total is None else total + term
    basis = (total * math.sqrt(count)).astype(jnp.bfloat16)
    basis_ref[...] = basis
    if len(rest) > 1:
        moved_ref = rest[0]
        for level in range(moved_ref.shape[0]):
            moved = lax.dot_general(
                samples_ref[level + 1], basis, NT, preferred_element_type=jnp.float32
            )
            moved_ref[level] = (moved * (1.0 / math.sqrt(count))).astype(jnp.bfloat16)


def cholqr_project(samples):
    levels, rank, count = samples.shape
    out_shape = [jax.ShapeDtypeStruct((rank, count), jnp.bfloat16)]
    if levels > 1:
        out_shape.append(jax.ShapeDtypeStruct((levels - 1, rank, rank), jnp.bfloat16))
    vmem = pl.BlockSpec(memory_space=pltpu.VMEM)
    out = pl.pallas_call(
        cholqr_kernel,
        out_shape=out_shape,
        in_specs=[vmem],
        out_specs=[vmem] * len(out_shape),
        scratch_shapes=[pltpu.VMEM((rank, rank), jnp.float32)],
        compiler_params=pltpu.CompilerParams(vmem_limit_bytes=32 * 2**20),
    )(samples)
    return out if levels > 1 else (out[0], None)


def products_kernel(source_ref, depth_ref, blocks_ref, sketched_ref, out_ref):
    leaf = pl.program_id(0)
    slots = blocks_ref.shape[1]
    levels = out_ref.shape[1]
    sums = [jnp.zeros(out_ref.shape[2:], jnp.float32) for _ in range(levels)]
    for slot in range(slots):
        product = lax.dot_general(
            sketched_ref[source_ref[leaf, slot]], blocks_ref[0, slot], NT,
            preferred_element_type=jnp.float32,
        )
        depth = depth_ref[leaf, slot]
        for level in range(levels):
            sums[level] = sums[level] + jnp.where(depth > level, product, 0.0)
    for level in range(levels):
        out_ref[0, level] = sums[level].astype(jnp.bfloat16)


def off_products(front_blocks, sketched, source, depth, levels):
    leaf_dev, slots, size, _ = front_blocks.shape
    ranks = sketched.shape[1]
    grid_spec = pltpu.PrefetchScalarGridSpec(
        num_scalar_prefetch=2,
        grid=(leaf_dev,),
        in_specs=[
            pl.BlockSpec((1, slots, size, size), lambda i, *_: (i, 0, 0, 0)),
            pl.BlockSpec(sketched.shape, lambda i, *_: (0, 0, 0)),
        ],
        out_specs=pl.BlockSpec((1, levels, ranks, size), lambda i, *_: (i, 0, 0, 0)),
    )
    return pl.pallas_call(
        products_kernel,
        grid_spec=grid_spec,
        out_shape=jax.ShapeDtypeStruct((leaf_dev, levels, ranks, size), jnp.bfloat16),
        compiler_params=pltpu.CompilerParams(vmem_limit_bytes=40 * 2**20),
    )(source, depth, front_blocks, sketched)


def shards(front_blocks, block_cols, samples, sketch_matrix):
    leaf_dev, _, leaf_size, _ = front_blocks.shape
    rank = sketch_matrix.shape[1]
    cols_dev = samples.shape[1]
    size_rows, size_cols = lax.axis_size("row"), lax.axis_size("col")
    row, col = lax.axis_index("row"), lax.axis_index("col")
    leaf_total = leaf_dev * size_rows
    top_level = leaf_total.bit_length() - 1
    local_levels = leaf_dev.bit_length() - 1
    chunk = rank // size_cols

    local_rows = lax.dynamic_slice_in_dim(sketch_matrix, col * cols_dev, cols_dev, 0)
    partial = jnp.einsum(
        "kc,lak->lca",
        local_rows,
        samples.reshape(leaf_dev, leaf_size, cols_dev),
        preferred_element_type=jnp.float32,
    ).astype(jnp.bfloat16)

    def chunk_of(owner):
        return lax.dynamic_slice_in_dim(partial, owner * chunk, chunk, 1)

    received = [swap(chunk_of(col ^ mask), "col", mask) for mask in range(1, size_cols)]
    total = chunk_of(col).astype(jnp.float32)
    for term in received:
        total = total + term.astype(jnp.float32)
    sketched = total.astype(jnp.bfloat16)

    even = jnp.stack([sketched] + [swap(sketched, "row", mask) for mask in range(2, size_rows, 2)])
    odd = swap(even, "row", 1)
    held = jnp.concatenate([even, odd]).reshape(leaf_total, chunk, leaf_size)
    leaf_ids = row * leaf_dev + jnp.arange(leaf_dev, dtype=jnp.int32)
    apart = jnp.bitwise_xor(leaf_ids[:, None], block_cols)
    depth = sum((apart >> level > 0).astype(jnp.int32) for level in range(top_level))
    offset = (block_cols // leaf_dev) ^ row
    place = (offset & 1) * (size_rows // 2) + (offset >> 1)
    source = place * leaf_dev + block_cols % leaf_dev

    off = off_products(front_blocks, held, source, depth, top_level)

    def leaf_of(owner):
        return lax.dynamic_index_in_dim(off, owner % leaf_dev, 0, keepdims=False)

    pieces = jnp.stack(
        [leaf_of(col)] + [swap(leaf_of(col ^ mask), "col", mask) for mask in range(1, size_cols)]
    )
    ordered = pieces[jnp.arange(size_cols, dtype=jnp.int32) ^ col]
    stacked = ordered.swapaxes(0, 1).reshape(top_level, rank, leaf_size)

    basis, carried = cholqr_project(stacked)
    own = basis.T
    bases = jnp.stack([own] + [swap(own, "col", mask) for mask in range(1, leaf_dev)])
    bases = bases[jnp.arange(leaf_dev, dtype=jnp.int32) ^ (col % leaf_dev)]

    for tree_level in range(1, top_level):
        bit = tree_level - 1
        if bit < local_levels:
            axis, index = "col", col
        else:
            axis, index, bit = "row", row, bit - local_levels
        is_left = (index >> bit) % 2 == 0
        partner = swap(carried, axis, 2**bit)
        stacked = jnp.concatenate(
            [jnp.where(is_left, carried, partner), jnp.where(is_left, partner, carried)], axis=2
        )
        transfer, carried = cholqr_project(stacked)
    out_rows = 4 * rank // size_rows
    offset = row % (size_rows // 2) * out_rows
    top_rows = lax.dynamic_slice_in_dim(transfer.T, offset, out_rows, 0)
    return (bases.reshape(leaf_dev * leaf_size, rank), top_rows)


def solution(mesh):
    placed = (P("row", None, None, None), P("row", None), P("row", "col"), P())
    return jax.shard_map(
        shards,
        mesh=mesh,
        in_specs=placed,
        out_specs=(P("row", None), P("row", None)),
        check_vma=False,
    )
```

time: 793 us -> 200 us (0.25)
  other arithmetic: 497 us -> 5.84 us
  Pallas kernels: 0 us -> 80.7 us
  waiting for transfers between devices: 144 us -> 67.5 us
  local copies, waits for them, and re-layouts: 72.3 us -> 16.3 us
  matrix products: 51.1 us -> 1.39 us
  starting transfers between devices: 0.46 us -> 24.3 us
  between operations: 19.2 us -> 1.14 us
    another operation x50 -> x3, other arithmetic: 495 us -> 2.51 us  [the longest x1 2.21 us: shards(): jnp.stack([sketched] + [swap(sketched, 'row', mask) for mask in range(2,...]
    all_gather x1 -> x0, waiting for transfers between devices: 80.9 us -> none  [shards(): all_sketched = lax.all_gather(sketched, 'row', axis=0, tiled=True)]
    pallas_call x0 -> x6, Pallas kernels: none -> 80.7 us  [the longest x5 75.6 us: cholqr_project(): pl.pallas_call(cholqr_kernel, out_shape=out_shape, in_specs=[vmem], out_s...]
    ppermute x2 -> x17, waiting for transfers between devices: 6.9 us -> 67.5 us  [swap(): return lax.ppermute(value, axis, pairs)]
    psum x1 -> x0, waiting for transfers between devices: 56.1 us -> none  [shards(): sketched = lax.psum(partial_sum.astype(jnp.bfloat16), 'col')]
    dot_general x17 -> x1, matrix products: 35.7 us -> 1.39 us  [shards(): jnp.einsum('kc,lak->lca', local_rows, samples.reshape(leaf_dev, leaf_size...]
    another operation x45 -> x0, local copies, waits for them, and re-layouts: 25.5 us -> none  [the longest x23 13.5 us: cholqr(): jax.scipy.linalg.solve_triangular(low_factor, identity, lower=True)]
    ppermute x2 -> x17, starting transfers between devices: 0.38 us -> 24.3 us  [swap(): return lax.ppermute(value, axis, pairs)]
  transfers between devices with their start and end apart: 4 -> 17, of which waited for: 4 -> 11; matrix products, arithmetic and copies ran while one was open for 0% -> 2% of each run, Pallas kernels for 0% -> 8%
where the time goes in v1:
time: 200 us; the launch traced here: 197 us
  Pallas kernels  80.7 us (40%)
  waiting for transfers between devices  67.5 us (34%)
  starting transfers between devices  24.3 us (12%)
  local copies, waits for them, and re-layouts  16.3 us (8%)
  other arithmetic  5.84 us (3%)
    pallas_call x5, Pallas kernels, cholqr_project(): pl.pallas_call(cholqr_kernel, out_shape=out_shape, in_specs=[vmem], out_s...  75.6 us
    ppermute x17, waiting for transfers between devices, swap(): return lax.ppermute(value, axis, pairs)  67.5 us
    ppermute x17, starting transfers between devices, swap(): return lax.ppermute(value, axis, pairs)  24.3 us
    unnamed x14, local copies, waits for them, and re-layouts  9.54 us
    pallas_call x1, Pallas kernels, off_products(): pl.pallas_call(products_kernel, grid_spec=grid_spec, out_shape=jax.ShapeD...  5.08 us
  transfers between devices with their start and end apart: 17, of which 11 were waited for; matrix products, arithmetic and copies ran while one was open for 2% of the time, Pallas kernels for 8%

profile of v1, /device:TPU:0, one launch (start us, length us, event | category | flops | bytes accessed | tf_op | source)
XLA Modules:
  0.0 197.2 jit_solution(5918653784205823625)
XLA Ops:
  0.6 0.0 copy-start
  0.7 1.2 copy-done
  1.9 1.4 convolution_convert_fusion
  3.3 0.0 copy-start.2
  3.3 1.0 copy-done.2
  4.2 0.1 dynamic-slice_bitcast_fusion.5
  4.3 0.0 copy-start.4
  4.3 4.0 %collective-permute-start.2 = (bf16[4,64,512]{2,1,0:T(8,128)(2,1)S(1)}, bf16[4,64,512]{2,1,0:T(8,128)(2,1)S(1)}, u32[]{:S(2)}, u32[]{:S(2)}) collective-permute-start(bf16[4,64,512]{2,1,0:T(8,128)(2,1)S(1)} %get-tuple-element.25), channel_id=1, source_target_pairs={{0,3},{1,2},{2,1},{3,0},{4,7},{5,6},{6,5},{7,4},{8,11},{9,10},{10,... | collective-permute-start | bytes 786440 | tf_op jit(solution)/shard_map/ppermute | solution.py:19
  8.3 0.5 collective-permute-start.1
  8.8 0.1 collective-permute-start
  8.9 6.5 %collective-permute-done.2 = bf16[4,64,512]{2,1,0:T(8,128)(2,1)S(1)} collective-permute-done((bf16[4,64,512]{2,1,0:T(8,128)(2,1)S(1)}, bf16[4,64,512]{2,1,0:T(8,128)(2,1)S(1)}, u32[]{:S(2)}, u32[]{:S(2)}) %collective-permute-start.2) | collective-permute-done | bytes 262176 | tf_op jit(solution)/shard_map/ppermute | solution.py:19
  15.4 4.7 %collective-permute-done.1 = bf16[4,64,512]{2,1,0:T(8,128)(2,1)S(1)} collective-permute-done((bf16[4,64,512]{2,1,0:T(8,128)(2,1)S(1)}, bf16[4,64,512]{2,1,0:T(8,128)(2,1)S(1)}, u32[]{:S(2)}, u32[]{:S(2)}) %collective-permute-start.1) | collective-permute-done | bytes 262176 | tf_op jit(solution)/shard_map/ppermute | solution.py:19
  20.2 0.7 copy-done.3
  20.9 1.9 constant_dynamic-update-slice_fusion.4
  22.8 1.8 collective-permute-start.3
  24.6 2.6 %collective-permute-start.4 = (bf16[4,64,512]{2,1,0:T(8,128)(2,1)}, bf16[4,64,512]{2,1,0:T(8,128)(2,1)}, u32[]{:S(2)}, u32[]{:S(2)}) collective-permute-start(bf16[4,64,512]{2,1,0:T(8,128)(2,1)} %get-tuple-element.17), channel_id=1, source_target_pairs={{0,16},{4,20},{8,24},{12,28},{16,0},{20,4},{24,8},{28,12},{1,17},{... | collective-permute-start | bytes 786440 | tf_op jit(solution)/shard_map/ppermute | solution.py:19
  27.2 0.0 collective-permute-start.5
  27.2 9.2 %collective-permute-done.3 = bf16[4,64,512]{2,1,0:T(8,128)(2,1)S(1)} collective-permute-done((bf16[4,64,512]{2,1,0:T(8,128)(2,1)}, bf16[4,64,512]{2,1,0:T(8,128)(2,1)S(1)}, u32[]{:S(2)}, u32[]{:S(2)}) %collective-permute-start.3) | collective-permute-done | bytes 262176 | tf_op jit(solution)/shard_map/ppermute | solution.py:19
  36.4 9.8 %collective-permute-done.4 = bf16[4,64,512]{2,1,0:T(8,128)(2,1)} collective-permute-done((bf16[4,64,512]{2,1,0:T(8,128)(2,1)}, bf16[4,64,512]{2,1,0:T(8,128)(2,1)}, u32[]{:S(2)}, u32[]{:S(2)}) %collective-permute-start.4) | collective-permute-done | bytes 262176 | tf_op jit(solution)/shard_map/ppermute | solution.py:19
  46.2 2.2 %pad_maximum_fusion.1 = bf16[4,4,64,512]{3,2,1,0:T(8,128)(2,1)} fusion(bf16[1,4,64,512]{3,2,1,0:T(8,128)(2,1)} %bitcast.9, bf16[1,4,64,512]{3,2,1,0:T(8,128)(2,1)} %bitcast.8, bf16[1,4,64,512]{3,2,1,0:T(8,128)(2,1)S(1)} %bitcast.63, bf16[1,4,64,512]{3,2,1,0:T(8,128)(2,1)} %bitcast.6), kind=kLoop, calls=%fused_computation.4 | loop fusion | flops 1572864 | bytes 2097152 | tf_op jit(solution)/shard_map/stack | solution.py:178
  48.5 0.1 convert_add_fusion
  48.6 1.0 constant_dynamic-update-slice_fusion.2
  49.5 1.0 constant_dynamic-update-slice_fusion.1
  50.5 0.9 collective-permute-done.6
  51.4 1.3 constant_dynamic-update-slice_fusion
  52.8 0.0 copy-start.1
  52.8 4.0 %copy-done.1 = bf16[4,5,512,512]{3,2,1,0:T(8,128)(2,1)S(1)} copy-done((bf16[4,5,512,512]{3,2,1,0:T(8,128)(2,1)S(1)}, bf16[4,5,512,512]{3,2,1,0:T(8,128)(2,1)}, u32[]{:S(2)}) %copy-start.1) | copy-done | bytes 10485784
  56.7 5.1 %shard_map.59 = bf16[4,5,64,512]{3,2,1,0:T(8,128)(2,1)S(1)} custom-call(s32[4,5]{1,0:T(4,128)S(1)} %get-tuple-element.34.source_ref, s32[4,5]{1,0:T(4,128)S(1)} %get-tuple-element.33.depth_ref, bf16[4,5,512,512]{3,2,1,0:T(8,128)(2,1)S(1)} %copy-done.1, bf16[32,64,512]{2,1,0:T(8,128)(2,1)S(1)} %bitcast.56), custom_call_target="tpu_custom_call" | custom-call | tf_op jit(solution)/shard_map/pallas_call | solution.py:142
  61.8 0.1 constant_dynamic-slice_fusion
  62.0 1.9 collective-permute-start.9
  63.8 1.2 collective-permute-start.8
  65.0 0.5 collective-permute-start.7
  65.5 8.0 %collective-permute-done.9 = bf16[5,64,512]{2,1,0:T(8,128)(2,1)S(1)} collective-permute-done((bf16[5,64,512]{2,1,0:T(8,128)(2,1)S(1)}, bf16[5,64,512]{2,1,0:T(8,128)(2,1)S(1)}, u32[]{:S(2)}, u32[]{:S(2)}) %collective-permute-start.9) | collective-permute-done | bytes 327712 | tf_op jit(solution)/shard_map/ppermute | solution.py:19
  73.5 6.2 %collective-permute-done.8 = bf16[5,64,512]{2,1,0:T(8,128)(2,1)S(1)} collective-permute-done((bf16[5,64,512]{2,1,0:T(8,128)(2,1)S(1)}, bf16[5,64,512]{2,1,0:T(8,128)(2,1)S(1)}, u32[]{:S(2)}, u32[]{:S(2)}) %collective-permute-start.8) | collective-permute-done | bytes 327712 | tf_op jit(solution)/shard_map/ppermute | solution.py:19
  79.7 0.1 collective-permute-done.7
  79.8 0.2 pad_maximum_fusion
  80.0 1.7 gather_fusion
  81.7 1.4 copy.10
  83.1 15.0 %shard_map.60 = (bf16[256,512]{1,0:T(8,128)(2,1)S(1)}, bf16[4,256,256]{2,1,0:T(8,128)(2,1)S(1)}) custom-call(bf16[5,256,512]{2,1,0:T(8,128)(2,1)S(1)} %bitcast.55), custom_call_target="tpu_custom_call" | custom-call | tf_op jit(solution)/shard_map/pallas_call | solution.py:102
  98.1 1.4 collective-permute-start.13
  99.6 12.4 %collective-permute-done.13 = bf16[4,256,256]{2,1,0:T(8,128)(2,1)S(1)} collective-permute-done((bf16[4,256,256]{2,1,0:T(8,128)(2,1)S(1)}, bf16[4,256,256]{2,1,0:T(8,128)(2,1)S(1)}, u32[]{:S(2)}, u32[]{:S(2)}) %collective-permute-start.13) | collective-permute-done | bytes 524320 | tf_op jit(solution)/shard_map/ppermute | solution.py:19
  111.9 0.1 broadcast_select_fusion.1
  112.0 0.1 pad_maximum_fusion.3.samples_ref
  112.1 15.4 %shard_map.61 = (bf16[256,512]{1,0:T(8,128)(2,1)}, bf16[3,256,256]{2,1,0:T(8,128)(2,1)S(1)}) custom-call(bf16[4,256,512]{2,1,0:T(8,128)(2,1)S(1)} %pad_maximum_fusion.3.samples_ref), custom_call_target="tpu_custom_call" | custom-call | tf_op jit(solution)/shard_map/pallas_call | solution.py:102
  127.5 1.5 collective-permute-start.14
  129.1 8.5 %collective-permute-done.14 = bf16[3,256,256]{2,1,0:T(8,128)(2,1)S(1)} collective-permute-done((bf16[3,256,256]{2,1,0:T(8,128)(2,1)S(1)}, bf16[3,256,256]{2,1,0:T(8,128)(2,1)S(1)}, u32[]{:S(2)}, u32[]{:S(2)}) %collective-permute-start.14) | collective-permute-done | bytes 393248 | tf_op jit(solution)/shard_map/ppermute | solution.py:19
  137.6 0.1 broadcast_select_fusion.3
  137.7 0.1 pad_maximum_fusion.4.samples_ref
  137.7 15.2 %shard_map.62 = (bf16[256,512]{1,0:T(8,128)(2,1)}, bf16[2,256,256]{2,1,0:T(8,128)(2,1)S(1)}) custom-call(bf16[3,256,512]{2,1,0:T(8,128)(2,1)S(1)} %pad_maximum_fusion.4.samples_ref), custom_call_target="tpu_custom_call" | custom-call | tf_op jit(solution)/shard_map/pallas_call | solution.py:102
  153.0 0.0 collective-permute-start.15
  153.0 1.8 collective-permute-start.12
  154.8 1.3 collective-permute-start.11
  156.1 0.4 collective-permute-start.10
  156.5 0.0 collective-permute-done.15
  156.6 15.4 %shard_map.63 = (bf16[256,512]{1,0:T(8,128)(2,1)}, bf16[1,256,256]{2,1,0:T(8,128)(2,1)S(1)}) custom-call(bf16[2,256,512]{2,1,0:T(8,128)(2,1)S(1)} %pad_maximum_fusion.5.samples_ref), custom_call_target="tpu_custom_call" | custom-call | tf_op jit(solution)/shard_map/pallas_call | solution.py:102
  172.0 5.3 %collective-permute-start.16 = (bf16[1,256,256]{2,1,0:T(8,128)(2,1)S(1)}, bf16[1,256,256]{2,1,0:T(8,128)(2,1)}, u32[]{:S(2)}, u32[]{:S(2)}) collective-permute-start(bf16[1,256,256]{2,1,0:T(8,128)(2,1)S(1)} %get-tuple-element.11), channel_id=1, source_target_pairs={{0,8},{4,12},{8,0},{12,4},{16,24},{20,28},{24,16},{28,20},{1,9},{5... | collective-permute-start | bytes 393224 | tf_op jit(solution)/shard_map/ppermute | solution.py:19
  177.3 0.0 collective-permute-done.12
  177.3 0.1 pad_maximum_fusion.2
  177.5 0.6 gather_fusion.1
  178.1 1.5 copy.11
  179.6 1.1 collective-permute-done.16
  180.7 0.9 broadcast_select_fusion.7
  181.7 14.5 %shard_map.64 = bf16[256,512]{1,0:T(8,128)(2,1)S(1)} custom-call(bf16[1,256,512]{2,1,0:T(8,128)(2,1)S(1)} %pad_maximum_fusion.6.samples_ref), custom_call_target="tpu_custom_call" | custom-call | tf_op jit(solution)/shard_map/pallas_call | solution.py:102
  196.2 0.7 copy.12
  (17 shorter events, 0.2 us)
Async XLA Ops:
  0.6 1.2 copy-start
  3.3 1.0 copy-start.2
  4.3 44.2 %copy-start.4 = (s32[4,5]{1,0:T(4,128)S(1)}, s32[4,5]{1,0:T(4,128)}, u32[]{:S(2)}) copy-start(s32[4,5]{1,0:T(4,128)} %param.5) | copy-start | bytes 244
  4.3 11.1 %collective-permute-start.2 = (bf16[4,64,512]{2,1,0:T(8,128)(2,1)S(1)}, bf16[4,64,512]{2,1,0:T(8,128)(2,1)S(1)}, u32[]{:S(2)}, u32[]{:S(2)}) collective-permute-start(bf16[4,64,512]{2,1,0:T(8,128)(2,1)S(1)} %get-tuple-element.25), channel_id=1, source_target_pairs={{0,3},{1,2},{2,1},{3,0},{4,7},{5,6},{6,5},{7,4},{8,11},{9,10},{10,... | collective-permute-start | bytes 786440 | tf_op jit(solution)/shard_map/ppermute | solution.py:19
  8.3 11.9 %collective-permute-start.1 = (bf16[4,64,512]{2,1,0:T(8,128)(2,1)S(1)}, bf16[4,64,512]{2,1,0:T(8,128)(2,1)S(1)}, u32[]{:S(2)}, u32[]{:S(2)}) collective-permute-start(bf16[4,64,512]{2,1,0:T(8,128)(2,1)S(1)} %get-tuple-element.26), channel_id=1, source_target_pairs={{0,2},{1,3},{2,0},{3,1},{4,6},{5,7},{6,4},{7,5},{8,10},{9,11},{10,... | collective-permute-start | bytes 786440 | tf_op jit(solution)/shard_map/ppermute | solution.py:19
  8.8 12.1 %collective-permute-start = (bf16[4,64,512]{2,1,0:T(8,128)(2,1)S(1)}, bf16[4,64,512]{2,1,0:T(8,128)(2,1)}, u32[]{:S(2)}, u32[]{:S(2)}) collective-permute-start(bf16[4,64,512]{2,1,0:T(8,128)(2,1)S(1)} %get-tuple-element.24), channel_id=1, source_target_pairs={{0,1},{1,0},{2,3},{3,2},{4,5},{5,4},{6,7},{7,6},{8,9},{9,8},{10,11... | collective-permute-start | bytes 786440 | tf_op jit(solution)/shard_map/ppermute | solution.py:19
  20.2 0.7 copy-start.3
  22.8 13.6 %collective-permute-start.3 = (bf16[4,64,512]{2,1,0:T(8,128)(2,1)}, bf16[4,64,512]{2,1,0:T(8,128)(2,1)S(1)}, u32[]{:S(2)}, u32[]{:S(2)}) collective-permute-start(bf16[4,64,512]{2,1,0:T(8,128)(2,1)} %get-tuple-element.17), channel_id=1, source_target_pairs={{0,8},{4,12},{8,0},{12,4},{16,24},{20,28},{24,16},{28,20},{1,9},{5... | collective-permute-start | bytes 786440 | tf_op jit(solution)/shard_map/ppermute | solution.py:19
  24.6 21.6 %collective-permute-start.4 = (bf16[4,64,512]{2,1,0:T(8,128)(2,1)}, bf16[4,64,512]{2,1,0:T(8,128)(2,1)}, u32[]{:S(2)}, u32[]{:S(2)}) collective-permute-start(bf16[4,64,512]{2,1,0:T(8,128)(2,1)} %get-tuple-element.17), channel_id=1, source_target_pairs={{0,16},{4,20},{8,24},{12,28},{16,0},{20,4},{24,8},{28,12},{1,17},{... | collective-permute-start | bytes 786440 | tf_op jit(solution)/shard_map/ppermute | solution.py:19
  27.2 19.1 %collective-permute-start.5 = (bf16[4,64,512]{2,1,0:T(8,128)(2,1)}, bf16[4,64,512]{2,1,0:T(8,128)(2,1)}, u32[]{:S(2)}, u32[]{:S(2)}) collective-permute-start(bf16[4,64,512]{2,1,0:T(8,128)(2,1)} %get-tuple-element.17), channel_id=1, source_target_pairs={{0,24},{4,28},{8,16},{12,20},{16,8},{20,12},{24,0},{28,4},{1,25},{... | collective-permute-start | bytes 786440 | tf_op jit(solution)/shard_map/ppermute | solution.py:19
  48.4 3.0 %collective-permute-start.6 = (bf16[4,4,64,512]{3,2,1,0:T(8,128)(2,1)}, bf16[4,4,64,512]{3,2,1,0:T(8,128)(2,1)}, u32[]{:S(2)}, u32[]{:S(2)}) collective-permute-start(bf16[4,4,64,512]{3,2,1,0:T(8,128)(2,1)} %pad_maximum_fusion.1), channel_id=1, source_target_pairs={{0,4},{4,0},{8,12},{12,8},{16,20},{20,16},{24,28},{28,24},{1,5},{5... | collective-permute-start | bytes 3145736 | tf_op jit(solution)/shard_map/ppermute | solution.py:19
  52.8 4.0 %copy-start.1 = (bf16[4,5,512,512]{3,2,1,0:T(8,128)(2,1)S(1)}, bf16[4,5,512,512]{3,2,1,0:T(8,128)(2,1)}, u32[]{:S(2)}) copy-start(bf16[4,5,512,512]{3,2,1,0:T(8,128)(2,1)} %blocks_ref.1) | copy-start | bytes 31457284
  62.0 11.6 %collective-permute-start.9 = (bf16[5,64,512]{2,1,0:T(8,128)(2,1)S(1)}, bf16[5,64,512]{2,1,0:T(8,128)(2,1)S(1)}, u32[]{:S(2)}, u32[]{:S(2)}) collective-permute-start(bf16[5,64,512]{2,1,0:T(8,128)(2,1)S(1)} %get-tuple-element.19), channel_id=1, source_target_pairs={{0,3},{1,2},{2,1},{3,0},{4,7},{5,6},{6,5},{7,4},{8,11},{9,10},{10,... | collective-permute-start | bytes 983048 | tf_op jit(solution)/shard_map/ppermute | solution.py:19
  63.8 15.9 %collective-permute-start.8 = (bf16[5,64,512]{2,1,0:T(8,128)(2,1)S(1)}, bf16[5,64,512]{2,1,0:T(8,128)(2,1)S(1)}, u32[]{:S(2)}, u32[]{:S(2)}) collective-permute-start(bf16[5,64,512]{2,1,0:T(8,128)(2,1)S(1)} %get-tuple-element.20), channel_id=1, source_target_pairs={{0,2},{1,3},{2,0},{3,1},{4,6},{5,7},{6,4},{7,5},{8,10},{9,11},{10,... | collective-permute-start | bytes 983048 | tf_op jit(solution)/shard_map/ppermute | solution.py:19
  65.0 14.8 %collective-permute-start.7 = (bf16[5,64,512]{2,1,0:T(8,128)(2,1)S(1)}, bf16[5,64,512]{2,1,0:T(8,128)(2,1)S(1)}, u32[]{:S(2)}, u32[]{:S(2)}) collective-permute-start(bf16[5,64,512]{2,1,0:T(8,128)(2,1)S(1)} %get-tuple-element.21), channel_id=1, source_target_pairs={{0,1},{1,0},{2,3},{3,2},{4,5},{5,4},{6,7},{7,6},{8,9},{9,8},{10,11... | collective-permute-start | bytes 983048 | tf_op jit(solution)/shard_map/ppermute | solution.py:19
  98.1 13.8 %collective-permute-start.13 = (bf16[4,256,256]{2,1,0:T(8,128)(2,1)S(1)}, bf16[4,256,256]{2,1,0:T(8,128)(2,1)S(1)}, u32[]{:S(2)}, u32[]{:S(2)}) collective-permute-start(bf16[4,256,256]{2,1,0:T(8,128)(2,1)S(1)} %get-tuple-element.8), channel_id=1, source_target_pairs={{0,1},{1,0},{2,3},{3,2},{4,5},{5,4},{6,7},{7,6},{8,9},{9,8},{10,11... | collective-permute-start | bytes 1572872 | tf_op jit(solution)/shard_map/ppermute | solution.py:19
  127.5 10.1 %collective-permute-start.14 = (bf16[3,256,256]{2,1,0:T(8,128)(2,1)S(1)}, bf16[3,256,256]{2,1,0:T(8,128)(2,1)S(1)}, u32[]{:S(2)}, u32[]{:S(2)}) collective-permute-start(bf16[3,256,256]{2,1,0:T(8,128)(2,1)S(1)} %get-tuple-element.9), channel_id=1, source_target_pairs={{0,2},{1,3},{2,0},{3,1},{4,6},{5,7},{6,4},{7,5},{8,10},{9,11},{10,... | collective-permute-start | bytes 1179656 | tf_op jit(solution)/shard_map/ppermute | solution.py:19
  153.0 3.6 %collective-permute-start.15 = (bf16[2,256,256]{2,1,0:T(8,128)(2,1)S(1)}, bf16[2,256,256]{2,1,0:T(8,128)(2,1)S(1)}, u32[]{:S(2)}, u32[]{:S(2)}) collective-permute-start(bf16[2,256,256]{2,1,0:T(8,128)(2,1)S(1)} %get-tuple-element.10), channel_id=1, source_target_pairs={{0,4},{4,0},{8,12},{12,8},{16,20},{20,16},{24,28},{28,24},{1,5},{5... | collective-permute-start | bytes 786440 | tf_op jit(solution)/shard_map/ppermute | solution.py:19
  153.0 24.3 %collective-permute-start.12 = (bf16[512,256]{0,1:T(8,128)(2,1)S(1)}, bf16[512,256]{0,1:T(8,128)(2,1)S(1)}, u32[]{:S(2)}, u32[]{:S(2)}) collective-permute-start(bf16[512,256]{0,1:T(8,128)(2,1)S(1)} %bitcast.57), channel_id=1, source_target_pairs={{0,3},{1,2},{2,1},{3,0},{4,7},{5,6},{6,5},{7,4},{8,11},{9,10},{10,... | collective-permute-start | bytes 786440 | tf_op jit(solution)/shard_map/ppermute | solution.py:19
  154.8 22.5 %collective-permute-start.11 = (bf16[512,256]{0,1:T(8,128)(2,1)S(1)}, bf16[512,256]{0,1:T(8,128)(2,1)S(1)}, u32[]{:S(2)}, u32[]{:S(2)}) collective-permute-start(bf16[512,256]{0,1:T(8,128)(2,1)S(1)} %bitcast.58), channel_id=1, source_target_pairs={{0,2},{1,3},{2,0},{3,1},{4,6},{5,7},{6,4},{7,5},{8,10},{9,11},{10,... | collective-permute-start | bytes 786440 | tf_op jit(solution)/shard_map/ppermute | solution.py:19
  156.1 21.2 %collective-permute-start.10 = (bf16[512,256]{0,1:T(8,128)(2,1)S(1)}, bf16[512,256]{0,1:T(8,128)(2,1)S(1)}, u32[]{:S(2)}, u32[]{:S(2)}) collective-permute-start(bf16[512,256]{0,1:T(8,128)(2,1)S(1)} %bitcast.59), channel_id=1, source_target_pairs={{0,1},{1,0},{2,3},{3,2},{4,5},{5,4},{6,7},{7,6},{8,9},{9,8},{10,11... | collective-permute-start | bytes 786440 | tf_op jit(solution)/shard_map/ppermute | solution.py:19
  172.0 8.7 %collective-permute-start.16 = (bf16[1,256,256]{2,1,0:T(8,128)(2,1)S(1)}, bf16[1,256,256]{2,1,0:T(8,128)(2,1)}, u32[]{:S(2)}, u32[]{:S(2)}) collective-permute-start(bf16[1,256,256]{2,1,0:T(8,128)(2,1)S(1)} %get-tuple-element.11), channel_id=1, source_target_pairs={{0,8},{4,12},{8,0},{12,4},{16,24},{20,28},{24,16},{28,20},{1,9},{5... | collective-permute-start | bytes 393224 | tf_op jit(solution)/shard_map/ppermute | solution.py:19

commit v2 on v1

v2 whole, which is shorter than its diff:
```python
import functools
import math

import jax
import jax.numpy as jnp
from jax import lax
from jax.experimental import pallas as pl
from jax.experimental.pallas import tpu as pltpu
from jax.sharding import PartitionSpec as P

PANEL = 32
BUSY = 8 * 10**9
NT = (((1,), (1,)), ((), ()))
TN = (((0,), (0,)), ((), ()))


def swap(value, axis, mask):
    pairs = [(source, source ^ mask) for source in range(lax.axis_size(axis))]
    return lax.ppermute(value, axis, pairs)


def split3(value):
    high = value.astype(jnp.bfloat16)
    rest = value - high.astype(jnp.float32)
    mid = rest.astype(jnp.bfloat16)
    low = (rest - mid.astype(jnp.float32)).astype(jnp.bfloat16)
    return high, mid, low


def reciprocal(value):
    guess = pl.reciprocal(value, approx=True)
    return guess * (2.0 - value * guess)


def wide(value, width):
    return jnp.concatenate([value] * (width // value.shape[1]), axis=1)


def eliminate_panel(panel, start):
    rows, width = panel.shape
    tiles = [panel[8 * i : 8 * i + 8, :] for i in range(rows // 8)]
    lanes = lax.broadcasted_iota(jnp.int32, (8, width), 1)
    row_ids = lax.broadcasted_iota(jnp.int32, (8, width), 0)
    for k in range(len(tiles)):
        base = start + 8 * k
        inside = (lanes >= base) & (lanes < base + 8)
        unit = jnp.where(lanes == base + row_ids, 1.0, 0.0)

        def columns(tile):
            return [
                jnp.broadcast_to(tile[:, base + t : base + t + 1], (8, 128)) for t in range(8)
            ]

        below = {i: columns(tiles[i]) for i in range(k + 1, len(tiles))}
        own = columns(tiles[k])
        values = [
            [jnp.broadcast_to(own[u][t : t + 1, :], (8, 128)) if u >= t else None for u in range(8)]
            for t in range(8)
        ]
        top = jnp.where(inside, unit, tiles[k])
        lines = [jnp.broadcast_to(top[t : t + 1, :], (8, width)) for t in range(8)]
        inverses, new = [], None
        for t in range(8):
            inverse = reciprocal(values[t][t])
            inverses.append(inverse)
            for u in range(t + 1, 8):
                ratio = values[t][u] * inverse
                for v in range(u, 8):
                    values[u][v] = values[u][v] - ratio * values[t][v]
                lines[u] = lines[u] - wide(ratio, width) * lines[t]
            scaled = lines[t] * wide(lax.rsqrt(values[t][t]), width)
            new = scaled if new is None else jnp.where(row_ids == t, scaled, new)
        for i in range(len(tiles)):
            if i == k:
                tiles[i] = new
                continue
            tile = jnp.where(inside, 0.0, tiles[i])
            if i > k:
                cols = below[i]
                for t in range(8):
                    factor = cols[t] * inverses[t]
                    for u in range(t + 1, 8):
                        cols[u] = cols[u] - factor * values[t][u]
                    tile = tile - wide(factor, width) * lines[t]
            tiles[i] = tile
    return jnp.concatenate(tiles, axis=0)


def invert_factor(work_ref):
    rank = work_ref.shape[0]
    for start in range(0, rank, PANEL):
        end = start + PANEL
        panel = eliminate_panel(work_ref[start:end, :], start)
        work_ref[start:end, :] = panel
        if end < rank:
            high, mid, low = split3(panel)
            left = jnp.concatenate([high, high, mid, high, low, mid], axis=0)
            right = jnp.concatenate([high, mid, high, low, high, mid], axis=0)
            first = end // 128 * 128
            update = lax.dot_general(
                left[:, first:], right, TN, preferred_element_type=jnp.float32
            )
            later = work_ref[end:, :]
            lanes = lax.broadcasted_iota(jnp.int32, later.shape, 1)
            done = (lanes >= start) & (lanes < end)
            work_ref[end:, :] = jnp.where(done, 0.0, later) - update[end - first :, :]
    shape = (rank, rank)
    lower = lax.broadcasted_iota(jnp.int32, shape, 1) <= lax.broadcasted_iota(jnp.int32, shape, 0)
    return split3(jnp.where(lower, work_ref[...], 0.0))


def gram(value):
    return lax.dot_general(value, value, NT, preferred_element_type=jnp.float32)


def apply_inverse(parts, value, count):
    total = None
    for part in reversed(parts):
        term = jnp.dot(part, value, preferred_element_type=jnp.float32)
        total = term if total is None else total + term
    return (total * math.sqrt(count)).astype(jnp.bfloat16)


def leaf_kernel(col_ref, *refs):
    pieces, (basis_ref, rows_ref, samples_ref, work_ref) = refs[:-4], refs[-4:]
    chunk, count = pieces[0].shape
    for mask, piece in enumerate(pieces):
        place = pl.multiple_of((col_ref[0] ^ mask) * chunk, chunk)
        samples_ref[pl.ds(place, chunk), :] = piece[...]
    work_ref[...] = gram(samples_ref[...])
    parts = invert_factor(work_ref)
    basis = apply_inverse(parts, samples_ref[...], count)
    basis_ref[...] = basis
    rows_ref[...] = basis.T


def node_kernel(own_ref, partner_ref, *refs):
    outs, work_ref = refs[:-1], refs[-1]
    count = 2 * own_ref.shape[1]
    work_ref[...] = gram(own_ref[...]) + gram(partner_ref[...])
    parts = invert_factor(work_ref)
    for source, out in zip((own_ref, partner_ref), outs):
        out[...] = apply_inverse(parts, source[...], count)


def project_leaf_kernel(col_ref, basis_ref, *refs):
    pieces, (first_ref, rest_ref) = refs[:-2], refs[-2:]
    levels, chunk, count = pieces[0].shape
    for mask, piece in enumerate(pieces):
        place = pl.ds(pl.multiple_of((col_ref[0] ^ mask) * chunk, chunk), chunk)
        for level in range(levels):
            moved = lax.dot_general(
                piece[level], basis_ref[...], NT, preferred_element_type=jnp.float32
            )
            moved = (moved * (1.0 / math.sqrt(count))).astype(jnp.bfloat16)
            if level:
                rest_ref[level - 1, place, :] = moved
            else:
                first_ref[place, :] = moved


def project_node_kernel(own_ref, partner_ref, q_own_ref, q_partner_ref, first_ref, *rest):
    count = 2 * own_ref.shape[2]
    for level in range(own_ref.shape[0]):
        moved = lax.dot_general(
            own_ref[level], q_own_ref[...], NT, preferred_element_type=jnp.float32
        ) + lax.dot_general(
            partner_ref[level], q_partner_ref[...], NT, preferred_element_type=jnp.float32
        )
        moved = (moved * (1.0 / math.sqrt(count))).astype(jnp.bfloat16)
        if level:
            rest[0][level - 1] = moved
        else:
            first_ref[...] = moved


def local_call(kernel, args, shapes, scalars=0, scratch=(), flops=0):
    vmem = pl.BlockSpec(memory_space=pltpu.VMEM)
    smem = pl.BlockSpec(memory_space=pltpu.SMEM)
    return pl.pallas_call(
        kernel,
        out_shape=[jax.ShapeDtypeStruct(shape, jnp.bfloat16) for shape in shapes],
        in_specs=[smem] * scalars + [vmem] * (len(args) - scalars),
        out_specs=[vmem] * len(shapes),
        scratch_shapes=list(scratch),
        cost_estimate=pl.CostEstimate(flops=flops, bytes_accessed=2**20, transcendentals=0),
        compiler_params=pltpu.CompilerParams(vmem_limit_bytes=32 * 2**20),
    )(*args)


def products_kernel(source_ref, depth_ref, blocks_ref, sketched_ref, first_ref, rest_ref):
    leaf = pl.program_id(0)
    slots = blocks_ref.shape[1]
    levels = rest_ref.shape[1] + 1
    sums = [jnp.zeros(first_ref.shape[1:], jnp.float32) for _ in range(levels)]
    for slot in range(slots):
        product = lax.dot_general(
            sketched_ref[source_ref[leaf, slot]], blocks_ref[0, slot], NT,
            preferred_element_type=jnp.float32,
        )
        depth = depth_ref[leaf, slot]
        for level in range(levels):
            sums[level] = sums[level] + jnp.where(depth > level, product, 0.0)
    first_ref[0] = sums[0].astype(jnp.bfloat16)
    for level in range(1, levels):
        rest_ref[0, level - 1] = sums[level].astype(jnp.bfloat16)


def off_products(front_blocks, sketched, source, depth, levels):
    leaf_dev, slots, size, _ = front_blocks.shape
    ranks = sketched.shape[1]
    grid_spec = pltpu.PrefetchScalarGridSpec(
        num_scalar_prefetch=2,
        grid=(leaf_dev,),
        in_specs=[
            pl.BlockSpec((1, slots, size, size), lambda i, *_: (i, 0, 0, 0)),
            pl.BlockSpec(sketched.shape, lambda i, *_: (0, 0, 0)),
        ],
        out_specs=[
            pl.BlockSpec((1, ranks, size), lambda i, *_: (i, 0, 0)),
            pl.BlockSpec((1, levels - 1, ranks, size), lambda i, *_: (i, 0, 0, 0)),
        ],
    )
    return pl.pallas_call(
        products_kernel,
        grid_spec=grid_spec,
        out_shape=[
            jax.ShapeDtypeStruct((leaf_dev, ranks, size), jnp.bfloat16),
            jax.ShapeDtypeStruct((leaf_dev, levels - 1, ranks, size), jnp.bfloat16),
        ],
        compiler_params=pltpu.CompilerParams(vmem_limit_bytes=40 * 2**20),
    )(source, depth, front_blocks, sketched)


def shards(front_blocks, block_cols, samples, sketch_matrix):
    leaf_dev, _, leaf_size, _ = front_blocks.shape
    rank = sketch_matrix.shape[1]
    cols_dev = samples.shape[1]
    size_rows, size_cols = lax.axis_size("row"), lax.axis_size("col")
    row, col = lax.axis_index("row"), lax.axis_index("col")
    leaf_total = leaf_dev * size_rows
    top_level = leaf_total.bit_length() - 1
    local_levels = leaf_dev.bit_length() - 1
    chunk = rank // size_cols

    local_rows = lax.dynamic_slice_in_dim(sketch_matrix, col * cols_dev, cols_dev, 0)
    partial = jnp.einsum(
        "kc,lak->lca",
        local_rows,
        samples.reshape(leaf_dev, leaf_size, cols_dev),
        preferred_element_type=jnp.float32,
    ).astype(jnp.bfloat16)

    def chunk_of(owner):
        return lax.dynamic_slice_in_dim(partial, owner * chunk, chunk, 1)

    received = [swap(chunk_of(col ^ mask), "col", mask) for mask in range(1, size_cols)]
    total = chunk_of(col).astype(jnp.float32)
    for term in received:
        total = total + term.astype(jnp.float32)
    sketched = total.astype(jnp.bfloat16)

    even = jnp.stack([sketched] + [swap(sketched, "row", mask) for mask in range(2, size_rows, 2)])
    odd = swap(even, "row", 1)
    held = jnp.concatenate([even, odd]).reshape(leaf_total, chunk, leaf_size)
    leaf_ids = row * leaf_dev + jnp.arange(leaf_dev, dtype=jnp.int32)
    apart = jnp.bitwise_xor(leaf_ids[:, None], block_cols)
    depth = sum((apart >> level > 0).astype(jnp.int32) for level in range(top_level))
    offset = (block_cols // leaf_dev) ^ row
    place = (offset & 1) * (size_rows // 2) + (offset >> 1)
    source = place * leaf_dev + block_cols % leaf_dev

    off_first, off_rest = off_products(front_blocks, held, source, depth, top_level)

    def leaf_of(off, mask):
        return lax.dynamic_index_in_dim(off, (col ^ mask) % leaf_dev, 0, keepdims=False)

    masks = range(1, size_cols)
    here = col.astype(jnp.int32).reshape(1)
    pieces = [leaf_of(off_first, 0)] + [swap(leaf_of(off_first, m), "col", m) for m in masks]
    pieces, off_rest = lax.optimization_barrier((pieces, off_rest))
    later = [leaf_of(off_rest, 0)] + [swap(leaf_of(off_rest, m), "col", m) for m in masks]
    work = pltpu.VMEM((rank, rank), jnp.float32)
    basis, basis_rows = local_call(
        leaf_kernel, [here, *pieces], [(rank, leaf_size), (leaf_size, rank)], 1,
        [pltpu.VMEM((rank, leaf_size), jnp.bfloat16), work], BUSY,
    )
    first, rest = local_call(
        project_leaf_kernel, [here, basis, *later],
        [(rank, rank), (top_level - 2, rank, rank)], 1,
    )

    square = (rank, rank)
    bases = None
    for tree_level in range(1, top_level):
        bit = tree_level - 1
        axis = "col" if bit < local_levels else "row"
        mask = 2 ** (bit if axis == "col" else bit - local_levels)
        partner = swap(first, axis, mask)
        if tree_level == top_level - 1:
            (transfer,) = local_call(node_kernel, [first, partner], [square], 0, [work], BUSY)
            break
        partner, rest = lax.optimization_barrier((partner, rest))
        partner_rest = swap(rest, axis, mask)
        if axis == "row" and bases is None:
            partner, basis_rows = lax.optimization_barrier((partner, basis_rows))
            groups = [
                list(range(i, i + leaf_dev)) for i in range(0, size_cols, leaf_dev)
            ]
            bases = lax.all_gather(
                basis_rows, "col", axis=0, tiled=True, axis_index_groups=groups
            )
        q_own, q_partner = local_call(
            node_kernel, [first, partner], [square, square], 0, [work], BUSY
        )
        shapes = [square] + [(rest.shape[0] - 1, *square)] * (rest.shape[0] > 1)
        first, *others = local_call(
            project_node_kernel, [rest, partner_rest, q_own, q_partner], shapes
        )
        rest = others[0] if others else None
    out_rows = 4 * rank // size_rows
    top_rows = lax.dynamic_slice_in_dim(transfer, row * out_rows % rank, out_rows, 1).T
    return (bases, top_rows)


def solution(mesh):
    placed = (P("row", None, None, None), P("row", None), P("row", "col"), P())
    return jax.shard_map(
        shards,
        mesh=mesh,
        in_specs=placed,
        out_specs=(P("row", None), P("row", None)),
        check_vma=False,
    )
```

time: 200 us -> 163 us (0.81); the launches traced: 197 us -> 163 us
  Pallas kernels: 80.7 us -> 52.5 us
  waiting for transfers between devices: 67.5 us -> 51.4 us
  between operations: 1.14 us -> 14.3 us
  local copies, waits for them, and re-layouts: 16.3 us -> 13.2 us
    pallas_call x6 -> x10, Pallas kernels: 80.7 us -> 52.5 us  [the longest x9 47.8 us: local_call(): pl.pallas_call(kernel, out_shape=[jax.ShapeDtypeStruct(shape, jnp.bfloat1...]
    ppermute x17 -> x20, waiting for transfers between devices: 67.5 us -> 50.2 us  [swap(): return lax.ppermute(value, axis, pairs)]
    gather x3 -> x0, local copies, waits for them, and re-layouts: 3.86 us -> none  [the longest x2 2.15 us: shards(): bases = bases[jnp.arange(leaf_dev, dtype=jnp.int32) ^ col % leaf_dev]]
    unnamed x14 -> x15, local copies, waits for them, and re-layouts: 9.54 us -> 11.8 us
    ppermute x17 -> x20, starting transfers between devices: 24.3 us -> 25.8 us  [swap(): return lax.ppermute(value, axis, pairs)]
  transfers between devices with their start and end apart: 17 -> 21, of which waited for: 11 -> 13; matrix products, arithmetic and copies ran while one was open for 2% -> 2% of each run, Pallas kernels for 8% -> 28%
where the time goes in v2:
time: 163 us
  Pallas kernels  52.5 us (32%)
  waiting for transfers between devices  51.4 us (32%)
  starting transfers between devices  25.8 us (16%)
  between operations  14.3 us (9%)
  local copies, waits for them, and re-layouts  13.2 us (8%)
  other arithmetic  4.24 us (3%)
    ppermute x20, waiting for transfers between devices, swap(): return lax.ppermute(value, axis, pairs)  50.2 us
    pallas_call x9, Pallas kernels, local_call(): pl.pallas_call(kernel, out_shape=[jax.ShapeDtypeStruct(shape, jnp.bfloat1...  47.8 us
    ppermute x20, starting transfers between devices, swap(): return lax.ppermute(value, axis, pairs)  25.8 us
    unnamed x15, local copies, waits for them, and re-layouts  11.8 us
    pallas_call x1, Pallas kernels, off_products(): pl.pallas_call(products_kernel, grid_spec=grid_spec, out_shape=[jax.Shape...  4.74 us
  transfers between devices with their start and end apart: 21, of which 13 were waited for; matrix products, arithmetic and copies ran while one was open for 2% of the time, Pallas kernels for 28%

profile of v2, /device:TPU:0, one launch (start us, length us, event | category | flops | bytes accessed | tf_op | source)
XLA Modules:
  0.0 162.9 jit_solution(1677531605457659581)
XLA Ops:
  7.2 0.0 copy-start
  7.2 0.0 all-gather.2.cloned.1.call-start
  7.3 1.1 copy-done
  8.4 1.4 convolution_convert_fusion
  9.8 0.0 copy-start.2
  9.8 1.0 copy-done.2
  10.8 0.1 dynamic-slice_bitcast_fusion.6
  10.8 0.0 copy-start.4
  10.8 4.0 %collective-permute-start.2 = (bf16[4,64,512]{2,1,0:T(8,128)(2,1)S(1)}, bf16[4,64,512]{2,1,0:T(8,128)(2,1)S(1)}, u32[]{:S(2)}, u32[]{:S(2)}) collective-permute-start(bf16[4,64,512]{2,1,0:T(8,128)(2,1)S(1)} %get-tuple-element.69), channel_id=1, source_target_pairs={{0,3},{1,2},{2,1},{3,0},{4,7},{5,6},{6,5},{7,4},{8,11},{9,10},{10,... | collective-permute-start | bytes 786440 | tf_op jit(solution)/shard_map/ppermute | solution.py:19
  14.8 0.5 collective-permute-start.1
  15.3 0.1 collective-permute-start
  15.4 6.5 %collective-permute-done.2 = bf16[4,64,512]{2,1,0:T(8,128)(2,1)S(1)} collective-permute-done((bf16[4,64,512]{2,1,0:T(8,128)(2,1)S(1)}, bf16[4,64,512]{2,1,0:T(8,128)(2,1)S(1)}, u32[]{:S(2)}, u32[]{:S(2)}) %collective-permute-start.2) | collective-permute-done | bytes 262176 | tf_op jit(solution)/shard_map/ppermute | solution.py:19
  22.0 4.7 %collective-permute-done.1 = bf16[4,64,512]{2,1,0:T(8,128)(2,1)S(1)} collective-permute-done((bf16[4,64,512]{2,1,0:T(8,128)(2,1)S(1)}, bf16[4,64,512]{2,1,0:T(8,128)(2,1)S(1)}, u32[]{:S(2)}, u32[]{:S(2)}) %collective-permute-start.1) | collective-permute-done | bytes 262176 | tf_op jit(solution)/shard_map/ppermute | solution.py:19
  26.7 0.7 copy-done.3
  27.4 2.0 %constant_dynamic-update-slice_fusion.4 = (bf16[8,4,64,512]{3,2,1,0:T(8,128)(2,1)S(1)}, bf16[4,64,512]{2,1,0:T(8,128)(2,1)}) fusion(bf16[4,64,512]{2,1,0:T(8,128)(2,1)S(1)} %collective-permute-done.2, bf16[4,64,512]{2,1,0:T(8,128)(2,1)} %copy-done.3, bf16[4,64,512]{2,1,0:T(8,128)(2,1)} %collective-permute-done, bf16[256,4,512]{2,0,1:T(8,128)(2,1)} %copy-done.2, ...), kind=kLoop, calls=%fused_computation.24 | loop fusion | flops 1048575 | bytes 1572868
  29.4 1.8 %collective-permute-start.3 = (bf16[4,64,512]{2,1,0:T(8,128)(2,1)}, bf16[4,64,512]{2,1,0:T(8,128)(2,1)S(1)}, u32[]{:S(2)}, u32[]{:S(2)}) collective-permute-start(bf16[4,64,512]{2,1,0:T(8,128)(2,1)} %get-tuple-element.63), channel_id=1, source_target_pairs={{0,8},{4,12},{8,0},{12,4},{16,24},{20,28},{24,16},{28,20},{1,9},{5... | collective-permute-start | bytes 786440 | tf_op jit(solution)/shard_map/ppermute | solution.py:19
  31.1 2.6 %collective-permute-start.4 = (bf16[4,64,512]{2,1,0:T(8,128)(2,1)}, bf16[4,64,512]{2,1,0:T(8,128)(2,1)}, u32[]{:S(2)}, u32[]{:S(2)}) collective-permute-start(bf16[4,64,512]{2,1,0:T(8,128)(2,1)} %get-tuple-element.63), channel_id=1, source_target_pairs={{0,16},{4,20},{8,24},{12,28},{16,0},{20,4},{24,8},{28,12},{1,17},{... | collective-permute-start | bytes 786440 | tf_op jit(solution)/shard_map/ppermute | solution.py:19
  33.7 0.0 collective-permute-start.5
  33.8 9.2 %collective-permute-done.3 = bf16[4,64,512]{2,1,0:T(8,128)(2,1)S(1)} collective-permute-done((bf16[4,64,512]{2,1,0:T(8,128)(2,1)}, bf16[4,64,512]{2,1,0:T(8,128)(2,1)S(1)}, u32[]{:S(2)}, u32[]{:S(2)}) %collective-permute-start.3) | collective-permute-done | bytes 262176 | tf_op jit(solution)/shard_map/ppermute | solution.py:19
  43.0 9.8 %collective-permute-done.4 = bf16[4,64,512]{2,1,0:T(8,128)(2,1)} collective-permute-done((bf16[4,64,512]{2,1,0:T(8,128)(2,1)}, bf16[4,64,512]{2,1,0:T(8,128)(2,1)}, u32[]{:S(2)}, u32[]{:S(2)}) %collective-permute-start.4) | collective-permute-done | bytes 262176 | tf_op jit(solution)/shard_map/ppermute | solution.py:19
  52.8 2.2 %pad_maximum_fusion = bf16[4,4,64,512]{3,2,1,0:T(8,128)(2,1)} fusion(bf16[1,4,64,512]{3,2,1,0:T(8,128)(2,1)} %bitcast.10, bf16[1,4,64,512]{3,2,1,0:T(8,128)(2,1)} %bitcast.9, bf16[1,4,64,512]{3,2,1,0:T(8,128)(2,1)S(1)} %bitcast.51, bf16[1,4,64,512]{3,2,1,0:T(8,128)(2,1)} %bitcast.7), kind=kLoop, calls=%fused_computation.1 | loop fusion | flops 1572864 | bytes 2097152 | tf_op jit(solution)/shard_map/stack | solution.py:263
  55.0 0.1 convert_add_fusion
  55.1 1.0 constant_dynamic-update-slice_fusion.2
  56.1 1.0 constant_dynamic-update-slice_fusion.1
  57.1 0.9 collective-permute-done.6
  58.0 1.3 constant_dynamic-update-slice_fusion
  59.3 0.0 copy-start.1
  59.3 4.0 %copy-done.1 = bf16[4,5,512,512]{3,2,1,0:T(8,128)(2,1)S(1)} copy-done((bf16[4,5,512,512]{3,2,1,0:T(8,128)(2,1)S(1)}, bf16[4,5,512,512]{3,2,1,0:T(8,128)(2,1)}, u32[]{:S(2)}) %copy-start.1) | copy-done | bytes 10485784
  63.3 4.7 %shard_map.59 = (bf16[4,64,512]{2,1,0:T(8,128)(2,1)S(1)}, bf16[4,4,64,512]{3,2,1,0:T(8,128)(2,1)S(1)}) custom-call(s32[4,5]{1,0:T(4,128)S(1)} %get-tuple-element.76.source_ref, s32[4,5]{1,0:T(4,128)S(1)} %get-tuple-element.75.depth_ref, bf16[4,5,512,512]{3,2,1,0:T(8,128)(2,1)S(1)} %copy-done.1, bf16[32,64,512]{2,1,0:T(8,128)(2,1)S(1)} %bitcast.50), custom_call_target="tpu_custom_call" | custom-call | tf_op jit(solution)/shard_map/pallas_call | solution.py:224
  68.1 1.6 collective-permute-start.7
  69.6 0.9 collective-permute-start.8
  70.5 1.1 collective-permute-start.9
  71.6 0.8 collective-permute-done.7.refs_1_
  72.4 2.2 %collective-permute-done.8.refs_2_ = bf16[64,512]{1,0:T(8,128)(2,1)S(1)} collective-permute-done((bf16[64,512]{1,0:T(8,128)(2,1)S(1)}, bf16[64,512]{1,0:T(8,128)(2,1)S(1)}, u32[]{:S(2)}, u32[]{:S(2)}) %collective-permute-start.8) | collective-permute-done | bytes 65568 | tf_op jit(solution)/shard_map/ppermute | solution.py:19
  74.6 1.1 collective-permute-done.9.refs_3_
  75.7 0.1 dynamic-slice_bitcast_fusion
  75.8 1.3 collective-permute-start.10
  77.0 0.5 collective-permute-start.11
  77.5 1.8 %collective-permute-start.12 = (bf16[4,64,512]{2,1,0:T(8,128)(2,1)S(1)}, bf16[4,64,512]{2,1,0:T(8,128)(2,1)S(1)}, u32[]{:S(2)}, u32[]{:S(2)}) collective-permute-start(bf16[4,64,512]{2,1,0:T(8,128)(2,1)S(1)} %get-tuple-element.64), channel_id=1, source_target_pairs={{0,3},{1,2},{2,1},{3,0},{4,7},{5,6},{6,5},{7,4},{8,11},{9,10},{10,... | collective-permute-start | bytes 786440 | tf_op jit(solution)/shard_map/ppermute | solution.py:19
  79.3 9.7 %shard_map.60 = (bf16[256,512]{1,0:T(8,128)(2,1)S(1)}, bf16[512,256]{1,0:T(8,128)(2,1)}) custom-call(s32[1]{0:T(128)} %bitcast.col_ref, bf16[64,512]{1,0:T(8,128)(2,1)S(1)} %get-tuple-element.33.refs_0_, bf16[64,512]{1,0:T(8,128)(2,1)S(1)} %collective-permute-done.7.refs_1_, bf16[64,512]{1,0:T(8,128)(2,1)S(1)} %collective-permute-done.8.refs_2_, ...), custom_call_target="tpu_custom_call" | custom-call | flops 8000000000 | bytes 1048576 | tf_op jit(solution)/shard_map/pallas_call | solution.py:180
  89.0 0.0 collective-permute-done.11.refs_2_
  89.0 1.4 shard_map.61
  90.4 1.2 collective-permute-start.13
  91.7 4.7 %collective-permute-done.13.partner_ref = bf16[256,256]{1,0:T(8,128)(2,1)S(1)} collective-permute-done((bf16[256,256]{1,0:T(8,128)(2,1)S(1)}, bf16[256,256]{1,0:T(8,128)(2,1)S(1)}, u32[]{:S(2)}, u32[]{:S(2)}) %collective-permute-start.13) | collective-permute-done | bytes 131104 | tf_op jit(solution)/shard_map/ppermute | solution.py:19
  96.4 1.3 collective-permute-start.14
  97.7 9.1 %shard_map.62 = (bf16[256,256]{1,0:T(8,128)(2,1)S(1)}, bf16[256,256]{1,0:T(8,128)(2,1)S(1)}) custom-call(bf16[256,256]{1,0:T(8,128)(2,1)S(1)} %get-tuple-element.39.own_ref, bf16[256,256]{1,0:T(8,128)(2,1)S(1)} %collective-permute-done.13.partner_ref), custom_call_target="tpu_custom_call" | custom-call | flops 8000000000 | bytes 1048576 | tf_op jit(solution)/shard_map/pallas_call | solution.py:180
  106.7 0.4 shard_map.63
  107.1 1.0 collective-permute-start.15
  108.2 4.8 %collective-permute-done.15.partner_ref = bf16[256,256]{1,0:T(8,128)(2,1)S(1)} collective-permute-done((bf16[256,256]{1,0:T(8,128)(2,1)S(1)}, bf16[256,256]{1,0:T(8,128)(2,1)S(1)}, u32[]{:S(2)}, u32[]{:S(2)}) %collective-permute-start.15) | collective-permute-done | bytes 131104 | tf_op jit(solution)/shard_map/ppermute | solution.py:19
  113.0 0.6 collective-permute-start.16
  113.6 8.9 %shard_map.64 = (bf16[256,256]{1,0:T(8,128)(2,1)S(1)}, bf16[256,256]{1,0:T(8,128)(2,1)S(1)}) custom-call(bf16[256,256]{1,0:T(8,128)(2,1)S(1)} %get-tuple-element.45.own_ref, bf16[256,256]{1,0:T(8,128)(2,1)S(1)} %collective-permute-done.15.partner_ref), custom_call_target="tpu_custom_call" | custom-call | flops 8000000000 | bytes 1048576 | tf_op jit(solution)/shard_map/pallas_call | solution.py:180
  122.5 0.3 shard_map.65
  122.8 0.1 collective-permute-start.17
  122.9 1.3 collective-permute-done.17.partner_ref
  124.2 0.0 all-gather.2.cloned.1.call-update
  124.2 0.2 collective-permute-start.18
  124.5 9.1 %shard_map.66 = (bf16[256,256]{1,0:T(8,128)(2,1)S(1)}, bf16[256,256]{1,0:T(8,128)(2,1)S(1)}) custom-call(bf16[256,256]{1,0:T(8,128)(2,1)S(1)} %get-tuple-element.51.own_ref, bf16[256,256]{1,0:T(8,128)(2,1)S(1)} %collective-permute-done.17.partner_ref), custom_call_target="tpu_custom_call" | custom-call | flops 8000000000 | bytes 1048576 | tf_op jit(solution)/shard_map/pallas_call | solution.py:180
  133.6 0.3 shard_map.67.own_ref
  133.9 5.2 %collective-permute-start.19 = (bf16[256,256]{1,0:T(8,128)(2,1)S(1)}, bf16[256,256]{1,0:T(8,128)(2,1)S(1)}, u32[]{:S(2)}, u32[]{:S(2)}) collective-permute-start(bf16[256,256]{1,0:T(8,128)(2,1)S(1)} %shard_map.67.own_ref), channel_id=1, source_target_pairs={{0,8},{4,12},{8,0},{12,4},{16,24},{20,28},{24,16},{28,20},{1,9},{5... | collective-permute-start | bytes 393224 | tf_op jit(solution)/shard_map/ppermute | solution.py:19
  139.0 4.0 %collective-permute-done.19.partner_ref = bf16[256,256]{1,0:T(8,128)(2,1)S(1)} collective-permute-done((bf16[256,256]{1,0:T(8,128)(2,1)S(1)}, bf16[256,256]{1,0:T(8,128)(2,1)S(1)}, u32[]{:S(2)}, u32[]{:S(2)}) %collective-permute-start.19) | collective-permute-done | bytes 131104 | tf_op jit(solution)/shard_map/ppermute | solution.py:19
  143.1 8.7 %shard_map.68 = bf16[256,256]{1,0:T(8,128)(2,1)S(1)} custom-call(bf16[256,256]{1,0:T(8,128)(2,1)S(1)} %shard_map.67.own_ref, bf16[256,256]{1,0:T(8,128)(2,1)S(1)} %collective-permute-done.19.partner_ref), custom_call_target="tpu_custom_call" | custom-call | flops 8000000000 | bytes 1048576 | tf_op jit(solution)/shard_map/pallas_call | solution.py:180
  151.8 0.7 copy.7
  152.6 1.2 all-gather.2.cloned.1.call-done
  153.8 2.3 %copy.14 = bf16[2048,256]{1,0:T(8,128)(2,1)} copy(bf16[2048,256]{1,0:T(8,128)(2,1)} %all-gather.2.cloned.1.call-done) | data formatting | bytes 2097152
  (14 shorter events, 0.1 us)
Async XLA Ops:
  7.2 1.2 copy-start
  7.2 146.6 %all-gather.2.cloned.1.call-start = ((), (), s32[]{:S(2)}) async-start(), calls=%async_computation | async-start | bytes 1310720 | tf_op jit(solution)/shard_map/all_gather | solution.py:310
  9.8 1.0 copy-start.2
  10.8 44.2 %copy-start.4 = (s32[4,5]{1,0:T(4,128)S(1)}, s32[4,5]{1,0:T(4,128)}, u32[]{:S(2)}) copy-start(s32[4,5]{1,0:T(4,128)} %param.5) | copy-start | bytes 244
  10.8 11.1 %collective-permute-start.2 = (bf16[4,64,512]{2,1,0:T(8,128)(2,1)S(1)}, bf16[4,64,512]{2,1,0:T(8,128)(2,1)S(1)}, u32[]{:S(2)}, u32[]{:S(2)}) collective-permute-start(bf16[4,64,512]{2,1,0:T(8,128)(2,1)S(1)} %get-tuple-element.69), channel_id=1, source_target_pairs={{0,3},{1,2},{2,1},{3,0},{4,7},{5,6},{6,5},{7,4},{8,11},{9,10},{10,... | collective-permute-start | bytes 786440 | tf_op jit(solution)/shard_map/ppermute | solution.py:19
  14.8 11.9 %collective-permute-start.1 = (bf16[4,64,512]{2,1,0:T(8,128)(2,1)S(1)}, bf16[4,64,512]{2,1,0:T(8,128)(2,1)S(1)}, u32[]{:S(2)}, u32[]{:S(2)}) collective-permute-start(bf16[4,64,512]{2,1,0:T(8,128)(2,1)S(1)} %get-tuple-element.70), channel_id=1, source_target_pairs={{0,2},{1,3},{2,0},{3,1},{4,6},{5,7},{6,4},{7,5},{8,10},{9,11},{10,... | collective-permute-start | bytes 786440 | tf_op jit(solution)/shard_map/ppermute | solution.py:19
  15.3 12.1 %collective-permute-start = (bf16[4,64,512]{2,1,0:T(8,128)(2,1)S(1)}, bf16[4,64,512]{2,1,0:T(8,128)(2,1)}, u32[]{:S(2)}, u32[]{:S(2)}) collective-permute-start(bf16[4,64,512]{2,1,0:T(8,128)(2,1)S(1)} %get-tuple-element.68), channel_id=1, source_target_pairs={{0,1},{1,0},{2,3},{3,2},{4,5},{5,4},{6,7},{7,6},{8,9},{9,8},{10,11... | collective-permute-start | bytes 786440 | tf_op jit(solution)/shard_map/ppermute | solution.py:19
  26.7 0.7 copy-start.3
  29.4 13.6 %collective-permute-start.3 = (bf16[4,64,512]{2,1,0:T(8,128)(2,1)}, bf16[4,64,512]{2,1,0:T(8,128)(2,1)S(1)}, u32[]{:S(2)}, u32[]{:S(2)}) collective-permute-start(bf16[4,64,512]{2,1,0:T(8,128)(2,1)} %get-tuple-element.63), channel_id=1, source_target_pairs={{0,8},{4,12},{8,0},{12,4},{16,24},{20,28},{24,16},{28,20},{1,9},{5... | collective-permute-start | bytes 786440 | tf_op jit(solution)/shard_map/ppermute | solution.py:19
  31.1 21.6 %collective-permute-start.4 = (bf16[4,64,512]{2,1,0:T(8,128)(2,1)}, bf16[4,64,512]{2,1,0:T(8,128)(2,1)}, u32[]{:S(2)}, u32[]{:S(2)}) collective-permute-start(bf16[4,64,512]{2,1,0:T(8,128)(2,1)} %get-tuple-element.63), channel_id=1, source_target_pairs={{0,16},{4,20},{8,24},{12,28},{16,0},{20,4},{24,8},{28,12},{1,17},{... | collective-permute-start | bytes 786440 | tf_op jit(solution)/shard_map/ppermute | solution.py:19
  33.7 19.1 %collective-permute-start.5 = (bf16[4,64,512]{2,1,0:T(8,128)(2,1)}, bf16[4,64,512]{2,1,0:T(8,128)(2,1)}, u32[]{:S(2)}, u32[]{:S(2)}) collective-permute-start(bf16[4,64,512]{2,1,0:T(8,128)(2,1)} %get-tuple-element.63), channel_id=1, source_target_pairs={{0,24},{4,28},{8,16},{12,20},{16,8},{20,12},{24,0},{28,4},{1,25},{... | collective-permute-start | bytes 786440 | tf_op jit(solution)/shard_map/ppermute | solution.py:19
  55.0 3.0 %collective-permute-start.6 = (bf16[4,4,64,512]{3,2,1,0:T(8,128)(2,1)}, bf16[4,4,64,512]{3,2,1,0:T(8,128)(2,1)}, u32[]{:S(2)}, u32[]{:S(2)}) collective-permute-start(bf16[4,4,64,512]{3,2,1,0:T(8,128)(2,1)} %pad_maximum_fusion), channel_id=1, source_target_pairs={{0,4},{4,0},{8,12},{12,8},{16,20},{20,16},{24,28},{28,24},{1,5},{5... | collective-permute-start | bytes 3145736 | tf_op jit(solution)/shard_map/ppermute | solution.py:19
  59.3 4.0 %copy-start.1 = (bf16[4,5,512,512]{3,2,1,0:T(8,128)(2,1)S(1)}, bf16[4,5,512,512]{3,2,1,0:T(8,128)(2,1)}, u32[]{:S(2)}) copy-start(bf16[4,5,512,512]{3,2,1,0:T(8,128)(2,1)} %blocks_ref.1) | copy-start | bytes 31457284
  68.1 4.3 %collective-permute-start.7 = (bf16[64,512]{1,0:T(8,128)(2,1)S(1)}, bf16[64,512]{1,0:T(8,128)(2,1)S(1)}, u32[]{:S(2)}, u32[]{:S(2)}) collective-permute-start(bf16[64,512]{1,0:T(8,128)(2,1)S(1)} %get-tuple-element.73), channel_id=1, source_target_pairs={{0,1},{1,0},{2,3},{3,2},{4,5},{5,4},{6,7},{7,6},{8,9},{9,8},{10,11... | collective-permute-start | bytes 196616 | tf_op jit(solution)/shard_map/ppermute | solution.py:19
  69.6 5.0 %collective-permute-start.8 = (bf16[64,512]{1,0:T(8,128)(2,1)S(1)}, bf16[64,512]{1,0:T(8,128)(2,1)S(1)}, u32[]{:S(2)}, u32[]{:S(2)}) collective-permute-start(bf16[64,512]{1,0:T(8,128)(2,1)S(1)} %get-tuple-element.72), channel_id=1, source_target_pairs={{0,2},{1,3},{2,0},{3,1},{4,6},{5,7},{6,4},{7,5},{8,10},{9,11},{10,... | collective-permute-start | bytes 196616 | tf_op jit(solution)/shard_map/ppermute | solution.py:19
  70.5 5.2 %collective-permute-start.9 = (bf16[64,512]{1,0:T(8,128)(2,1)S(1)}, bf16[64,512]{1,0:T(8,128)(2,1)S(1)}, u32[]{:S(2)}, u32[]{:S(2)}) collective-permute-start(bf16[64,512]{1,0:T(8,128)(2,1)S(1)} %get-tuple-element.71), channel_id=1, source_target_pairs={{0,3},{1,2},{2,1},{3,0},{4,7},{5,6},{6,5},{7,4},{8,11},{9,10},{10,... | collective-permute-start | bytes 196616 | tf_op jit(solution)/shard_map/ppermute | solution.py:19
  75.8 13.2 %collective-permute-start.10 = (bf16[4,64,512]{2,1,0:T(8,128)(2,1)S(1)}, bf16[4,64,512]{2,1,0:T(8,128)(2,1)S(1)}, u32[]{:S(2)}, u32[]{:S(2)}) collective-permute-start(bf16[4,64,512]{2,1,0:T(8,128)(2,1)S(1)} %get-tuple-element.66), channel_id=1, source_target_pairs={{0,1},{1,0},{2,3},{3,2},{4,5},{5,4},{6,7},{7,6},{8,9},{9,8},{10,11... | collective-permute-start | bytes 786440 | tf_op jit(solution)/shard_map/ppermute | solution.py:19
  77.0 12.0 %collective-permute-start.11 = (bf16[4,64,512]{2,1,0:T(8,128)(2,1)S(1)}, bf16[4,64,512]{2,1,0:T(8,128)(2,1)S(1)}, u32[]{:S(2)}, u32[]{:S(2)}) collective-permute-start(bf16[4,64,512]{2,1,0:T(8,128)(2,1)S(1)} %get-tuple-element.65), channel_id=1, source_target_pairs={{0,2},{1,3},{2,0},{3,1},{4,6},{5,7},{6,4},{7,5},{8,10},{9,11},{10,... | collective-permute-start | bytes 786440 | tf_op jit(solution)/shard_map/ppermute | solution.py:19
  77.5 11.5 %collective-permute-start.12 = (bf16[4,64,512]{2,1,0:T(8,128)(2,1)S(1)}, bf16[4,64,512]{2,1,0:T(8,128)(2,1)S(1)}, u32[]{:S(2)}, u32[]{:S(2)}) collective-permute-start(bf16[4,64,512]{2,1,0:T(8,128)(2,1)S(1)} %get-tuple-element.64), channel_id=1, source_target_pairs={{0,3},{1,2},{2,1},{3,0},{4,7},{5,6},{6,5},{7,4},{8,11},{9,10},{10,... | collective-permute-start | bytes 786440 | tf_op jit(solution)/shard_map/ppermute | solution.py:19
  90.4 6.0 %collective-permute-start.13 = (bf16[256,256]{1,0:T(8,128)(2,1)S(1)}, bf16[256,256]{1,0:T(8,128)(2,1)S(1)}, u32[]{:S(2)}, u32[]{:S(2)}) collective-permute-start(bf16[256,256]{1,0:T(8,128)(2,1)S(1)} %get-tuple-element.39.own_ref), channel_id=1, source_target_pairs={{0,1},{1,0},{2,3},{3,2},{4,5},{5,4},{6,7},{7,6},{8,9},{9,8},{10,11... | collective-permute-start | bytes 393224 | tf_op jit(solution)/shard_map/ppermute | solution.py:19
  96.4 10.4 %collective-permute-start.14 = (bf16[3,256,256]{2,1,0:T(8,128)(2,1)S(1)}, bf16[3,256,256]{2,1,0:T(8,128)(2,1)S(1)}, u32[]{:S(2)}, u32[]{:S(2)}) collective-permute-start(bf16[3,256,256]{2,1,0:T(8,128)(2,1)S(1)} %get-tuple-element.41.own_ref), channel_id=1, source_target_pairs={{0,1},{1,0},{2,3},{3,2},{4,5},{5,4},{6,7},{7,6},{8,9},{9,8},{10,11... | collective-permute-start | bytes 1179656 | tf_op jit(solution)/shard_map/ppermute | solution.py:19
  107.1 5.8 %collective-permute-start.15 = (bf16[256,256]{1,0:T(8,128)(2,1)S(1)}, bf16[256,256]{1,0:T(8,128)(2,1)S(1)}, u32[]{:S(2)}, u32[]{:S(2)}) collective-permute-start(bf16[256,256]{1,0:T(8,128)(2,1)S(1)} %get-tuple-element.45.own_ref), channel_id=1, source_target_pairs={{0,2},{1,3},{2,0},{3,1},{4,6},{5,7},{6,4},{7,5},{8,10},{9,11},{10,... | collective-permute-start | bytes 393224 | tf_op jit(solution)/shard_map/ppermute | solution.py:19
  113.0 9.5 %collective-permute-start.16 = (bf16[2,256,256]{2,1,0:T(8,128)(2,1)S(1)}, bf16[2,256,256]{2,1,0:T(8,128)(2,1)S(1)}, u32[]{:S(2)}, u32[]{:S(2)}) collective-permute-start(bf16[2,256,256]{2,1,0:T(8,128)(2,1)S(1)} %get-tuple-element.47.own_ref), channel_id=1, source_target_pairs={{0,2},{1,3},{2,0},{3,1},{4,6},{5,7},{6,4},{7,5},{8,10},{9,11},{10,... | collective-permute-start | bytes 786440 | tf_op jit(solution)/shard_map/ppermute | solution.py:19
  122.8 1.4 collective-permute-start.17
  124.2 9.3 %collective-permute-start.18 = (bf16[1,256,256]{2,1,0:T(8,128)(2,1)S(1)}, bf16[1,256,256]{2,1,0:T(8,128)(2,1)S(1)}, u32[]{:S(2)}, u32[]{:S(2)}) collective-permute-start(bf16[1,256,256]{2,1,0:T(8,128)(2,1)S(1)} %get-tuple-element.56.own_ref), channel_id=1, source_target_pairs={{0,4},{4,0},{8,12},{12,8},{16,20},{20,16},{24,28},{28,24},{1,5},{5... | collective-permute-start | bytes 393224 | tf_op jit(solution)/shard_map/ppermute | solution.py:19
  133.9 9.2 %collective-permute-start.19 = (bf16[256,256]{1,0:T(8,128)(2,1)S(1)}, bf16[256,256]{1,0:T(8,128)(2,1)S(1)}, u32[]{:S(2)}, u32[]{:S(2)}) collective-permute-start(bf16[256,256]{1,0:T(8,128)(2,1)S(1)} %shard_map.67.own_ref), channel_id=1, source_target_pairs={{0,8},{4,12},{8,0},{12,4},{16,24},{20,28},{24,16},{28,20},{1,9},{5... | collective-permute-start | bytes 393224 | tf_op jit(solution)/shard_map/ppermute | solution.py:19
Sparse Core Ops, SparseCore 0:
  124.4 29.3 all-gather.1

commit v3 on v2

--- a/solution.py
+++ b/solution.py
@@ -304,12 +304,9 @@
         partner_rest = swap(rest, axis, mask)
         if axis == "row" and bases is None:
             partner, basis_rows = lax.optimization_barrier((partner, basis_rows))
-            groups = [
-                list(range(i, i + leaf_dev)) for i in range(0, size_cols, leaf_dev)
-            ]
-            bases = lax.all_gather(
-                basis_rows, "col", axis=0, tiled=True, axis_index_groups=groups
-            )
+            bases = [basis_rows] + [swap(basis_rows, "col", m) for m in range(1, leaf_dev)]
+            order = jnp.arange(leaf_dev, dtype=jnp.int32) ^ (col % leaf_dev)
+            bases = jnp.stack(bases)[order].reshape(leaf_dev * leaf_size, rank)
         q_own, q_partner = local_call(
             node_kernel, [first, partner], [square, square], 0, [work], BUSY
         )

time: 163 us -> 150 us (0.920)
  between operations: 14.3 us -> 0.93 us
  starting transfers between devices: 25.8 us -> 29 us
  waiting for transfers between devices: 51.4 us -> 49 us
    ppermute x20 -> x23, starting transfers between devices: 25.8 us -> 29 us  [swap(): return lax.ppermute(value, axis, pairs)]
    unnamed x15 -> x14, local copies, waits for them, and re-layouts: 11.8 us -> 9.54 us
    ppermute x20 -> x23, waiting for transfers between devices: 50.2 us -> 49 us  [swap(): return lax.ppermute(value, axis, pairs)]
  transfers between devices with their start and end apart: 21 -> 23, of which waited for: 13 -> 13; matrix products, arithmetic and copies ran while one was open for 2% -> 3% of each run, Pallas kernels for 28% -> 24%
where the time goes in v3:
time: 150 us; the launch traced here: 149 us
  Pallas kernels  51.8 us (35%)
  waiting for transfers between devices  49 us (33%)
  starting transfers between devices  29 us (19%)
  local copies, waits for them, and re-layouts  12.6 us (8%)
  other arithmetic  4.39 us (3%)
    ppermute x23, waiting for transfers between devices, swap(): return lax.ppermute(value, axis, pairs)  49 us
    pallas_call x9, Pallas kernels, local_call(): pl.pallas_call(kernel, out_shape=[jax.ShapeDtypeStruct(shape, jnp.bfloat1...  47.1 us
    ppermute x23, starting transfers between devices, swap(): return lax.ppermute(value, axis, pairs)  29 us
    unnamed x14, local copies, waits for them, and re-layouts  9.54 us
    pallas_call x1, Pallas kernels, off_products(): pl.pallas_call(products_kernel, grid_spec=grid_spec, out_shape=[jax.Shape...  4.74 us
  transfers between devices with their start and end apart: 23, of which 13 were waited for; matrix products, arithmetic and copies ran while one was open for 3% of the time, Pallas kernels for 24%

profile of v3, /device:TPU:0, one launch (start us, length us, event | category | flops | bytes accessed | tf_op | source)
XLA Modules:
  0.0 149.2 jit_solution(14352170696285779501)
XLA Ops:
  0.6 0.0 copy-start
  0.7 1.2 copy-done
  1.9 1.4 convolution_convert_fusion
  3.3 0.0 copy-start.2
  3.3 1.0 copy-done.2
  4.2 0.1 dynamic-slice_bitcast_fusion.6
  4.3 0.0 copy-start.4
  4.3 4.0 %collective-permute-start.2 = (bf16[4,64,512]{2,1,0:T(8,128)(2,1)S(1)}, bf16[4,64,512]{2,1,0:T(8,128)(2,1)S(1)}, u32[]{:S(2)}, u32[]{:S(2)}) collective-permute-start(bf16[4,64,512]{2,1,0:T(8,128)(2,1)S(1)} %get-tuple-element.69), channel_id=1, source_target_pairs={{0,3},{1,2},{2,1},{3,0},{4,7},{5,6},{6,5},{7,4},{8,11},{9,10},{10,... | collective-permute-start | bytes 786440 | tf_op jit(solution)/shard_map/ppermute | solution.py:19
  8.3 0.5 collective-permute-start.1
  8.8 0.1 collective-permute-start
  8.9 6.5 %collective-permute-done.2 = bf16[4,64,512]{2,1,0:T(8,128)(2,1)S(1)} collective-permute-done((bf16[4,64,512]{2,1,0:T(8,128)(2,1)S(1)}, bf16[4,64,512]{2,1,0:T(8,128)(2,1)S(1)}, u32[]{:S(2)}, u32[]{:S(2)}) %collective-permute-start.2) | collective-permute-done | bytes 262176 | tf_op jit(solution)/shard_map/ppermute | solution.py:19
  15.4 4.7 %collective-permute-done.1 = bf16[4,64,512]{2,1,0:T(8,128)(2,1)S(1)} collective-permute-done((bf16[4,64,512]{2,1,0:T(8,128)(2,1)S(1)}, bf16[4,64,512]{2,1,0:T(8,128)(2,1)S(1)}, u32[]{:S(2)}, u32[]{:S(2)}) %collective-permute-start.1) | collective-permute-done | bytes 262176 | tf_op jit(solution)/shard_map/ppermute | solution.py:19
  20.2 0.7 copy-done.3
  20.9 2.0 %constant_dynamic-update-slice_fusion.4 = (bf16[8,4,64,512]{3,2,1,0:T(8,128)(2,1)S(1)}, bf16[4,64,512]{2,1,0:T(8,128)(2,1)}) fusion(bf16[4,64,512]{2,1,0:T(8,128)(2,1)S(1)} %collective-permute-done.2, bf16[4,64,512]{2,1,0:T(8,128)(2,1)} %copy-done.3, bf16[4,64,512]{2,1,0:T(8,128)(2,1)} %collective-permute-done, bf16[256,4,512]{2,0,1:T(8,128)(2,1)} %copy-done.2, ...), kind=kLoop, calls=%fused_computation.26 | loop fusion | flops 1048575 | bytes 1572868
  22.8 1.8 %collective-permute-start.3 = (bf16[4,64,512]{2,1,0:T(8,128)(2,1)}, bf16[4,64,512]{2,1,0:T(8,128)(2,1)S(1)}, u32[]{:S(2)}, u32[]{:S(2)}) collective-permute-start(bf16[4,64,512]{2,1,0:T(8,128)(2,1)} %get-tuple-element.63), channel_id=1, source_target_pairs={{0,8},{4,12},{8,0},{12,4},{16,24},{20,28},{24,16},{28,20},{1,9},{5... | collective-permute-start | bytes 786440 | tf_op jit(solution)/shard_map/ppermute | solution.py:19
  24.6 2.6 %collective-permute-start.4 = (bf16[4,64,512]{2,1,0:T(8,128)(2,1)}, bf16[4,64,512]{2,1,0:T(8,128)(2,1)}, u32[]{:S(2)}, u32[]{:S(2)}) collective-permute-start(bf16[4,64,512]{2,1,0:T(8,128)(2,1)} %get-tuple-element.63), channel_id=1, source_target_pairs={{0,16},{4,20},{8,24},{12,28},{16,0},{20,4},{24,8},{28,12},{1,17},{... | collective-permute-start | bytes 786440 | tf_op jit(solution)/shard_map/ppermute | solution.py:19
  27.2 0.0 collective-permute-start.5
  27.2 9.2 %collective-permute-done.3 = bf16[4,64,512]{2,1,0:T(8,128)(2,1)S(1)} collective-permute-done((bf16[4,64,512]{2,1,0:T(8,128)(2,1)}, bf16[4,64,512]{2,1,0:T(8,128)(2,1)S(1)}, u32[]{:S(2)}, u32[]{:S(2)}) %collective-permute-start.3) | collective-permute-done | bytes 262176 | tf_op jit(solution)/shard_map/ppermute | solution.py:19
  36.4 9.8 %collective-permute-done.4 = bf16[4,64,512]{2,1,0:T(8,128)(2,1)} collective-permute-done((bf16[4,64,512]{2,1,0:T(8,128)(2,1)}, bf16[4,64,512]{2,1,0:T(8,128)(2,1)}, u32[]{:S(2)}, u32[]{:S(2)}) %collective-permute-start.4) | collective-permute-done | bytes 262176 | tf_op jit(solution)/shard_map/ppermute | solution.py:19
  46.3 2.2 %pad_maximum_fusion = bf16[4,4,64,512]{3,2,1,0:T(8,128)(2,1)} fusion(bf16[1,4,64,512]{3,2,1,0:T(8,128)(2,1)} %bitcast.10, bf16[1,4,64,512]{3,2,1,0:T(8,128)(2,1)} %bitcast.9, bf16[1,4,64,512]{3,2,1,0:T(8,128)(2,1)S(1)} %bitcast.60, bf16[1,4,64,512]{3,2,1,0:T(8,128)(2,1)} %bitcast.7), kind=kLoop, calls=%fused_computation.2 | loop fusion | flops 1572864 | bytes 2097152 | tf_op jit(solution)/shard_map/stack | solution.py:263
  48.5 0.1 convert_add_fusion
  48.6 1.0 constant_dynamic-update-slice_fusion.2
  49.5 1.0 constant_dynamic-update-slice_fusion.1
  50.5 0.9 collective-permute-done.6
  51.5 1.3 constant_dynamic-update-slice_fusion
  52.8 0.0 copy-start.1
  52.8 4.0 %copy-done.1 = bf16[4,5,512,512]{3,2,1,0:T(8,128)(2,1)S(1)} copy-done((bf16[4,5,512,512]{3,2,1,0:T(8,128)(2,1)S(1)}, bf16[4,5,512,512]{3,2,1,0:T(8,128)(2,1)}, u32[]{:S(2)}) %copy-start.1) | copy-done | bytes 10485784
  56.8 4.7 %shard_map.59 = (bf16[4,64,512]{2,1,0:T(8,128)(2,1)S(1)}, bf16[4,4,64,512]{3,2,1,0:T(8,128)(2,1)S(1)}) custom-call(s32[4,5]{1,0:T(4,128)S(1)} %get-tuple-element.76.source_ref, s32[4,5]{1,0:T(4,128)S(1)} %get-tuple-element.75.depth_ref, bf16[4,5,512,512]{3,2,1,0:T(8,128)(2,1)S(1)} %copy-done.1, bf16[32,64,512]{2,1,0:T(8,128)(2,1)S(1)} %bitcast.57), custom_call_target="tpu_custom_call" | custom-call | tf_op jit(solution)/shard_map/pallas_call | solution.py:224
  61.6 1.6 %collective-permute-start.7 = (bf16[64,512]{1,0:T(8,128)(2,1)S(1)}, bf16[64,512]{1,0:T(8,128)(2,1)S(1)}, u32[]{:S(2)}, u32[]{:S(2)}) collective-permute-start(bf16[64,512]{1,0:T(8,128)(2,1)S(1)} %get-tuple-element.73), channel_id=1, source_target_pairs={{0,1},{1,0},{2,3},{3,2},{4,5},{5,4},{6,7},{7,6},{8,9},{9,8},{10,11... | collective-permute-start | bytes 196616 | tf_op jit(solution)/shard_map/ppermute | solution.py:19
  63.1 0.9 collective-permute-start.8
  64.0 1.1 collective-permute-start.9
  65.1 0.8 collective-permute-done.7.refs_1_
  65.9 2.2 %collective-permute-done.8.refs_2_ = bf16[64,512]{1,0:T(8,128)(2,1)S(1)} collective-permute-done((bf16[64,512]{1,0:T(8,128)(2,1)S(1)}, bf16[64,512]{1,0:T(8,128)(2,1)S(1)}, u32[]{:S(2)}, u32[]{:S(2)}) %collective-permute-start.8) | collective-permute-done | bytes 65568 | tf_op jit(solution)/shard_map/ppermute | solution.py:19
  68.1 1.1 collective-permute-done.9.refs_3_
  69.2 0.1 dynamic-slice_bitcast_fusion
  69.2 1.3 collective-permute-start.10
  70.5 0.5 collective-permute-start.11
  71.0 1.8 %collective-permute-start.12 = (bf16[4,64,512]{2,1,0:T(8,128)(2,1)S(1)}, bf16[4,64,512]{2,1,0:T(8,128)(2,1)S(1)}, u32[]{:S(2)}, u32[]{:S(2)}) collective-permute-start(bf16[4,64,512]{2,1,0:T(8,128)(2,1)S(1)} %get-tuple-element.64), channel_id=1, source_target_pairs={{0,3},{1,2},{2,1},{3,0},{4,7},{5,6},{6,5},{7,4},{8,11},{9,10},{10,... | collective-permute-start | bytes 786440 | tf_op jit(solution)/shard_map/ppermute | solution.py:19
  72.8 9.0 %shard_map.60 = (bf16[256,512]{1,0:T(8,128)(2,1)S(1)}, bf16[512,256]{1,0:T(8,128)(2,1)S(1)}) custom-call(s32[1]{0:T(128)} %bitcast.col_ref, bf16[64,512]{1,0:T(8,128)(2,1)S(1)} %get-tuple-element.33.refs_0_, bf16[64,512]{1,0:T(8,128)(2,1)S(1)} %collective-permute-done.7.refs_1_, bf16[64,512]{1,0:T(8,128)(2,1)S(1)} %collective-permute-done.8.refs_2_, ...), custom_call_target="tpu_custom_call" | custom-call | flops 8000000000 | bytes 1048576 | tf_op jit(solution)/shard_map/pallas_call | solution.py:180
  81.8 0.7 collective-permute-done.11.refs_2_
  82.5 1.4 shard_map.61
  83.9 1.0 collective-permute-start.13
  84.9 5.3 %collective-permute-done.13.partner_ref = bf16[256,256]{1,0:T(8,128)(2,1)S(1)} collective-permute-done((bf16[256,256]{1,0:T(8,128)(2,1)S(1)}, bf16[256,256]{1,0:T(8,128)(2,1)S(1)}, u32[]{:S(2)}, u32[]{:S(2)}) %collective-permute-start.13) | collective-permute-done | bytes 131104 | tf_op jit(solution)/shard_map/ppermute | solution.py:19
  90.2 1.0 collective-permute-start.14
  91.2 9.1 %shard_map.62 = (bf16[256,256]{1,0:T(8,128)(2,1)S(1)}, bf16[256,256]{1,0:T(8,128)(2,1)S(1)}) custom-call(bf16[256,256]{1,0:T(8,128)(2,1)S(1)} %get-tuple-element.39.own_ref, bf16[256,256]{1,0:T(8,128)(2,1)S(1)} %collective-permute-done.13.partner_ref), custom_call_target="tpu_custom_call" | custom-call | flops 8000000000 | bytes 1048576 | tf_op jit(solution)/shard_map/pallas_call | solution.py:180
  100.3 0.4 shard_map.63
  100.7 1.1 collective-permute-start.15
  101.8 3.9 %collective-permute-done.15.partner_ref = bf16[256,256]{1,0:T(8,128)(2,1)S(1)} collective-permute-done((bf16[256,256]{1,0:T(8,128)(2,1)S(1)}, bf16[256,256]{1,0:T(8,128)(2,1)S(1)}, u32[]{:S(2)}, u32[]{:S(2)}) %collective-permute-start.15) | collective-permute-done | bytes 131104 | tf_op jit(solution)/shard_map/ppermute | solution.py:19
  105.7 1.1 collective-permute-start.16
  106.9 8.9 %shard_map.64 = (bf16[256,256]{1,0:T(8,128)(2,1)S(1)}, bf16[256,256]{1,0:T(8,128)(2,1)S(1)}) custom-call(bf16[256,256]{1,0:T(8,128)(2,1)S(1)} %get-tuple-element.45.own_ref, bf16[256,256]{1,0:T(8,128)(2,1)S(1)} %collective-permute-done.15.partner_ref), custom_call_target="tpu_custom_call" | custom-call | flops 8000000000 | bytes 1048576 | tf_op jit(solution)/shard_map/pallas_call | solution.py:180
  115.8 0.3 shard_map.65
  116.1 0.1 collective-permute-start.17
  116.2 1.3 collective-permute-done.17.partner_ref
  117.5 1.5 %collective-permute-start.20 = (bf16[512,256]{1,0:T(8,128)(2,1)S(1)}, bf16[512,256]{1,0:T(8,128)(2,1)S(1)}, u32[]{:S(2)}, u32[]{:S(2)}) collective-permute-start(bf16[512,256]{1,0:T(8,128)(2,1)S(1)} %get-tuple-element.55), channel_id=1, source_target_pairs={{0,3},{1,2},{2,1},{3,0},{4,7},{5,6},{6,5},{7,4},{8,11},{9,10},{10,... | collective-permute-start | bytes 786440 | tf_op jit(solution)/shard_map/ppermute | solution.py:19
  119.0 1.0 collective-permute-start.19
  120.0 1.0 collective-permute-start.18
  121.0 9.1 %shard_map.66 = (bf16[256,256]{1,0:T(8,128)(2,1)S(1)}, bf16[256,256]{1,0:T(8,128)(2,1)S(1)}) custom-call(bf16[256,256]{1,0:T(8,128)(2,1)S(1)} %get-tuple-element.51.own_ref, bf16[256,256]{1,0:T(8,128)(2,1)S(1)} %collective-permute-done.17.partner_ref), custom_call_target="tpu_custom_call" | custom-call | flops 8000000000 | bytes 1048576 | tf_op jit(solution)/shard_map/pallas_call | solution.py:180
  130.1 0.3 shard_map.67.own_ref
  130.4 5.1 %collective-permute-start.22 = (bf16[256,256]{1,0:T(8,128)(2,1)S(1)}, bf16[256,256]{1,0:T(8,128)(2,1)S(1)}, u32[]{:S(2)}, u32[]{:S(2)}) collective-permute-start(bf16[256,256]{1,0:T(8,128)(2,1)S(1)} %shard_map.67.own_ref), channel_id=1, source_target_pairs={{0,8},{4,12},{8,0},{12,4},{16,24},{20,28},{24,16},{28,20},{1,9},{5... | collective-permute-start | bytes 393224 | tf_op jit(solution)/shard_map/ppermute | solution.py:19
  135.5 0.1 pad_maximum_fusion.1
  135.6 1.6 %gather_fusion = bf16[4,512,256]{2,1,0:T(8,128)(2,1)} fusion(bf16[4,512,256]{2,1,0:T(8,128)(2,1)S(1)} %pad_maximum_fusion.1, s32[1024]{0:T(1024)S(1)} %pad_clamp_fusion), kind=kCustom, calls=%fused_computation | custom fusion | bytes 2097168 | tf_op jit(solution)/shard_map/gather | solution.py:309
  137.2 2.4 %collective-permute-done.22.partner_ref = bf16[256,256]{1,0:T(8,128)(2,1)S(1)} collective-permute-done((bf16[256,256]{1,0:T(8,128)(2,1)S(1)}, bf16[256,256]{1,0:T(8,128)(2,1)S(1)}, u32[]{:S(2)}, u32[]{:S(2)}) %collective-permute-start.22) | collective-permute-done | bytes 131104 | tf_op jit(solution)/shard_map/ppermute | solution.py:19
  139.6 8.7 %shard_map.68 = bf16[256,256]{1,0:T(8,128)(2,1)S(1)} custom-call(bf16[256,256]{1,0:T(8,128)(2,1)S(1)} %shard_map.67.own_ref, bf16[256,256]{1,0:T(8,128)(2,1)S(1)} %collective-permute-done.22.partner_ref), custom_call_target="tpu_custom_call" | custom-call | flops 8000000000 | bytes 1048576 | tf_op jit(solution)/shard_map/pallas_call | solution.py:180
  148.4 0.7 copy.7
  (20 shorter events, 0.1 us)
Async XLA Ops:
  0.6 1.2 copy-start
  3.3 1.0 copy-start.2
  4.3 44.2 %copy-start.4 = (s32[4,5]{1,0:T(4,128)S(1)}, s32[4,5]{1,0:T(4,128)}, u32[]{:S(2)}) copy-start(s32[4,5]{1,0:T(4,128)} %param.5) | copy-start | bytes 244
  4.3 11.1 %collective-permute-start.2 = (bf16[4,64,512]{2,1,0:T(8,128)(2,1)S(1)}, bf16[4,64,512]{2,1,0:T(8,128)(2,1)S(1)}, u32[]{:S(2)}, u32[]{:S(2)}) collective-permute-start(bf16[4,64,512]{2,1,0:T(8,128)(2,1)S(1)} %get-tuple-element.69), channel_id=1, source_target_pairs={{0,3},{1,2},{2,1},{3,0},{4,7},{5,6},{6,5},{7,4},{8,11},{9,10},{10,... | collective-permute-start | bytes 786440 | tf_op jit(solution)/shard_map/ppermute | solution.py:19
  8.3 11.9 %collective-permute-start.1 = (bf16[4,64,512]{2,1,0:T(8,128)(2,1)S(1)}, bf16[4,64,512]{2,1,0:T(8,128)(2,1)S(1)}, u32[]{:S(2)}, u32[]{:S(2)}) collective-permute-start(bf16[4,64,512]{2,1,0:T(8,128)(2,1)S(1)} %get-tuple-element.70), channel_id=1, source_target_pairs={{0,2},{1,3},{2,0},{3,1},{4,6},{5,7},{6,4},{7,5},{8,10},{9,11},{10,... | collective-permute-start | bytes 786440 | tf_op jit(solution)/shard_map/ppermute | solution.py:19
  8.8 12.1 %collective-permute-start = (bf16[4,64,512]{2,1,0:T(8,128)(2,1)S(1)}, bf16[4,64,512]{2,1,0:T(8,128)(2,1)}, u32[]{:S(2)}, u32[]{:S(2)}) collective-permute-start(bf16[4,64,512]{2,1,0:T(8,128)(2,1)S(1)} %get-tuple-element.68), channel_id=1, source_target_pairs={{0,1},{1,0},{2,3},{3,2},{4,5},{5,4},{6,7},{7,6},{8,9},{9,8},{10,11... | collective-permute-start | bytes 786440 | tf_op jit(solution)/shard_map/ppermute | solution.py:19
  20.2 0.7 copy-start.3
  22.8 13.6 %collective-permute-start.3 = (bf16[4,64,512]{2,1,0:T(8,128)(2,1)}, bf16[4,64,512]{2,1,0:T(8,128)(2,1)S(1)}, u32[]{:S(2)}, u32[]{:S(2)}) collective-permute-start(bf16[4,64,512]{2,1,0:T(8,128)(2,1)} %get-tuple-element.63), channel_id=1, source_target_pairs={{0,8},{4,12},{8,0},{12,4},{16,24},{20,28},{24,16},{28,20},{1,9},{5... | collective-permute-start | bytes 786440 | tf_op jit(solution)/shard_map/ppermute | solution.py:19
  24.6 21.6 %collective-permute-start.4 = (bf16[4,64,512]{2,1,0:T(8,128)(2,1)}, bf16[4,64,512]{2,1,0:T(8,128)(2,1)}, u32[]{:S(2)}, u32[]{:S(2)}) collective-permute-start(bf16[4,64,512]{2,1,0:T(8,128)(2,1)} %get-tuple-element.63), channel_id=1, source_target_pairs={{0,16},{4,20},{8,24},{12,28},{16,0},{20,4},{24,8},{28,12},{1,17},{... | collective-permute-start | bytes 786440 | tf_op jit(solution)/shard_map/ppermute | solution.py:19
  27.2 19.1 %collective-permute-start.5 = (bf16[4,64,512]{2,1,0:T(8,128)(2,1)}, bf16[4,64,512]{2,1,0:T(8,128)(2,1)}, u32[]{:S(2)}, u32[]{:S(2)}) collective-permute-start(bf16[4,64,512]{2,1,0:T(8,128)(2,1)} %get-tuple-element.63), channel_id=1, source_target_pairs={{0,24},{4,28},{8,16},{12,20},{16,8},{20,12},{24,0},{28,4},{1,25},{... | collective-permute-start | bytes 786440 | tf_op jit(solution)/shard_map/ppermute | solution.py:19
  48.5 3.0 %collective-permute-start.6 = (bf16[4,4,64,512]{3,2,1,0:T(8,128)(2,1)}, bf16[4,4,64,512]{3,2,1,0:T(8,128)(2,1)}, u32[]{:S(2)}, u32[]{:S(2)}) collective-permute-start(bf16[4,4,64,512]{3,2,1,0:T(8,128)(2,1)} %pad_maximum_fusion), channel_id=1, source_target_pairs={{0,4},{4,0},{8,12},{12,8},{16,20},{20,16},{24,28},{28,24},{1,5},{5... | collective-permute-start | bytes 3145736 | tf_op jit(solution)/shard_map/ppermute | solution.py:19
  52.8 4.0 %copy-start.1 = (bf16[4,5,512,512]{3,2,1,0:T(8,128)(2,1)S(1)}, bf16[4,5,512,512]{3,2,1,0:T(8,128)(2,1)}, u32[]{:S(2)}) copy-start(bf16[4,5,512,512]{3,2,1,0:T(8,128)(2,1)} %blocks_ref.1) | copy-start | bytes 31457284
  61.6 4.3 %collective-permute-start.7 = (bf16[64,512]{1,0:T(8,128)(2,1)S(1)}, bf16[64,512]{1,0:T(8,128)(2,1)S(1)}, u32[]{:S(2)}, u32[]{:S(2)}) collective-permute-start(bf16[64,512]{1,0:T(8,128)(2,1)S(1)} %get-tuple-element.73), channel_id=1, source_target_pairs={{0,1},{1,0},{2,3},{3,2},{4,5},{5,4},{6,7},{7,6},{8,9},{9,8},{10,11... | collective-permute-start | bytes 196616 | tf_op jit(solution)/shard_map/ppermute | solution.py:19
  63.1 5.0 %collective-permute-start.8 = (bf16[64,512]{1,0:T(8,128)(2,1)S(1)}, bf16[64,512]{1,0:T(8,128)(2,1)S(1)}, u32[]{:S(2)}, u32[]{:S(2)}) collective-permute-start(bf16[64,512]{1,0:T(8,128)(2,1)S(1)} %get-tuple-element.72), channel_id=1, source_target_pairs={{0,2},{1,3},{2,0},{3,1},{4,6},{5,7},{6,4},{7,5},{8,10},{9,11},{10,... | collective-permute-start | bytes 196616 | tf_op jit(solution)/shard_map/ppermute | solution.py:19
  64.0 5.2 %collective-permute-start.9 = (bf16[64,512]{1,0:T(8,128)(2,1)S(1)}, bf16[64,512]{1,0:T(8,128)(2,1)S(1)}, u32[]{:S(2)}, u32[]{:S(2)}) collective-permute-start(bf16[64,512]{1,0:T(8,128)(2,1)S(1)} %get-tuple-element.71), channel_id=1, source_target_pairs={{0,3},{1,2},{2,1},{3,0},{4,7},{5,6},{6,5},{7,4},{8,11},{9,10},{10,... | collective-permute-start | bytes 196616 | tf_op jit(solution)/shard_map/ppermute | solution.py:19
  69.2 12.5 %collective-permute-start.10 = (bf16[4,64,512]{2,1,0:T(8,128)(2,1)S(1)}, bf16[4,64,512]{2,1,0:T(8,128)(2,1)S(1)}, u32[]{:S(2)}, u32[]{:S(2)}) collective-permute-start(bf16[4,64,512]{2,1,0:T(8,128)(2,1)S(1)} %get-tuple-element.66), channel_id=1, source_target_pairs={{0,1},{1,0},{2,3},{3,2},{4,5},{5,4},{6,7},{7,6},{8,9},{9,8},{10,11... | collective-permute-start | bytes 786440 | tf_op jit(solution)/shard_map/ppermute | solution.py:19
  70.5 12.0 %collective-permute-start.11 = (bf16[4,64,512]{2,1,0:T(8,128)(2,1)S(1)}, bf16[4,64,512]{2,1,0:T(8,128)(2,1)S(1)}, u32[]{:S(2)}, u32[]{:S(2)}) collective-permute-start(bf16[4,64,512]{2,1,0:T(8,128)(2,1)S(1)} %get-tuple-element.65), channel_id=1, source_target_pairs={{0,2},{1,3},{2,0},{3,1},{4,6},{5,7},{6,4},{7,5},{8,10},{9,11},{10,... | collective-permute-start | bytes 786440 | tf_op jit(solution)/shard_map/ppermute | solution.py:19
  71.0 11.5 %collective-permute-start.12 = (bf16[4,64,512]{2,1,0:T(8,128)(2,1)S(1)}, bf16[4,64,512]{2,1,0:T(8,128)(2,1)S(1)}, u32[]{:S(2)}, u32[]{:S(2)}) collective-permute-start(bf16[4,64,512]{2,1,0:T(8,128)(2,1)S(1)} %get-tuple-element.64), channel_id=1, source_target_pairs={{0,3},{1,2},{2,1},{3,0},{4,7},{5,6},{6,5},{7,4},{8,11},{9,10},{10,... | collective-permute-start | bytes 786440 | tf_op jit(solution)/shard_map/ppermute | solution.py:19
  83.9 6.3 %collective-permute-start.13 = (bf16[256,256]{1,0:T(8,128)(2,1)S(1)}, bf16[256,256]{1,0:T(8,128)(2,1)S(1)}, u32[]{:S(2)}, u32[]{:S(2)}) collective-permute-start(bf16[256,256]{1,0:T(8,128)(2,1)S(1)} %get-tuple-element.39.own_ref), channel_id=1, source_target_pairs={{0,1},{1,0},{2,3},{3,2},{4,5},{5,4},{6,7},{7,6},{8,9},{9,8},{10,11... | collective-permute-start | bytes 393224 | tf_op jit(solution)/shard_map/ppermute | solution.py:19
  90.2 10.1 %collective-permute-start.14 = (bf16[3,256,256]{2,1,0:T(8,128)(2,1)S(1)}, bf16[3,256,256]{2,1,0:T(8,128)(2,1)S(1)}, u32[]{:S(2)}, u32[]{:S(2)}) collective-permute-start(bf16[3,256,256]{2,1,0:T(8,128)(2,1)S(1)} %get-tuple-element.41.own_ref), channel_id=1, source_target_pairs={{0,1},{1,0},{2,3},{3,2},{4,5},{5,4},{6,7},{7,6},{8,9},{9,8},{10,11... | collective-permute-start | bytes 1179656 | tf_op jit(solution)/shard_map/ppermute | solution.py:19
  100.7 5.0 %collective-permute-start.15 = (bf16[256,256]{1,0:T(8,128)(2,1)S(1)}, bf16[256,256]{1,0:T(8,128)(2,1)S(1)}, u32[]{:S(2)}, u32[]{:S(2)}) collective-permute-start(bf16[256,256]{1,0:T(8,128)(2,1)S(1)} %get-tuple-element.45.own_ref), channel_id=1, source_target_pairs={{0,2},{1,3},{2,0},{3,1},{4,6},{5,7},{6,4},{7,5},{8,10},{9,11},{10,... | collective-permute-start | bytes 393224 | tf_op jit(solution)/shard_map/ppermute | solution.py:19
  105.7 10.0 %collective-permute-start.16 = (bf16[2,256,256]{2,1,0:T(8,128)(2,1)S(1)}, bf16[2,256,256]{2,1,0:T(8,128)(2,1)S(1)}, u32[]{:S(2)}, u32[]{:S(2)}) collective-permute-start(bf16[2,256,256]{2,1,0:T(8,128)(2,1)S(1)} %get-tuple-element.47.own_ref), channel_id=1, source_target_pairs={{0,2},{1,3},{2,0},{3,1},{4,6},{5,7},{6,4},{7,5},{8,10},{9,11},{10,... | collective-permute-start | bytes 786440 | tf_op jit(solution)/shard_map/ppermute | solution.py:19
  116.1 1.4 collective-permute-start.17
  117.5 18.0 %collective-permute-start.20 = (bf16[512,256]{1,0:T(8,128)(2,1)S(1)}, bf16[512,256]{1,0:T(8,128)(2,1)S(1)}, u32[]{:S(2)}, u32[]{:S(2)}) collective-permute-start(bf16[512,256]{1,0:T(8,128)(2,1)S(1)} %get-tuple-element.55), channel_id=1, source_target_pairs={{0,3},{1,2},{2,1},{3,0},{4,7},{5,6},{6,5},{7,4},{8,11},{9,10},{10,... | collective-permute-start | bytes 786440 | tf_op jit(solution)/shard_map/ppermute | solution.py:19
  119.0 16.5 %collective-permute-start.19 = (bf16[512,256]{1,0:T(8,128)(2,1)S(1)}, bf16[512,256]{1,0:T(8,128)(2,1)S(1)}, u32[]{:S(2)}, u32[]{:S(2)}) collective-permute-start(bf16[512,256]{1,0:T(8,128)(2,1)S(1)} %get-tuple-element.55), channel_id=1, source_target_pairs={{0,2},{1,3},{2,0},{3,1},{4,6},{5,7},{6,4},{7,5},{8,10},{9,11},{10,... | collective-permute-start | bytes 786440 | tf_op jit(solution)/shard_map/ppermute | solution.py:19
  120.0 15.5 %collective-permute-start.18 = (bf16[512,256]{1,0:T(8,128)(2,1)S(1)}, bf16[512,256]{1,0:T(8,128)(2,1)S(1)}, u32[]{:S(2)}, u32[]{:S(2)}) collective-permute-start(bf16[512,256]{1,0:T(8,128)(2,1)S(1)} %get-tuple-element.55), channel_id=1, source_target_pairs={{0,1},{1,0},{2,3},{3,2},{4,5},{5,4},{6,7},{7,6},{8,9},{9,8},{10,11... | collective-permute-start | bytes 786440 | tf_op jit(solution)/shard_map/ppermute | solution.py:19
  121.0 9.1 %collective-permute-start.21 = (bf16[1,256,256]{2,1,0:T(8,128)(2,1)S(1)}, bf16[1,256,256]{2,1,0:T(8,128)(2,1)S(1)}, u32[]{:S(2)}, u32[]{:S(2)}) collective-permute-start(bf16[1,256,256]{2,1,0:T(8,128)(2,1)S(1)} %get-tuple-element.56.own_ref), channel_id=1, source_target_pairs={{0,4},{4,0},{8,12},{12,8},{16,20},{20,16},{24,28},{28,24},{1,5},{5... | collective-permute-start | bytes 393224 | tf_op jit(solution)/shard_map/ppermute | solution.py:19
  130.4 9.2 %collective-permute-start.22 = (bf16[256,256]{1,0:T(8,128)(2,1)S(1)}, bf16[256,256]{1,0:T(8,128)(2,1)S(1)}, u32[]{:S(2)}, u32[]{:S(2)}) collective-permute-start(bf16[256,256]{1,0:T(8,128)(2,1)S(1)} %shard_map.67.own_ref), channel_id=1, source_target_pairs={{0,8},{4,12},{8,0},{12,4},{16,24},{20,28},{24,16},{28,20},{1,9},{5... | collective-permute-start | bytes 393224 | tf_op jit(solution)/shard_map/ppermute | solution.py:19

commit v4 on v3

--- a/solution.py
+++ b/solution.py
@@ -232,6 +232,145 @@
     )(source, depth, front_blocks, sketched)
 
 
+def front_kernel(sketch_ref, samples_ref, held_ref, part_ref, got_ref, *sems):
+    sum_send, sum_recv, chain_send, gather_recv = sems
+    row, col = lax.axis_index("row"), lax.axis_index("col")
+    size_cols = got_ref.shape[0] + 1
+    size_z = held_ref.shape[0] // 2
+    leaf_dev, _, cols_dev = samples_ref.shape
+    chunk = held_ref.shape[2]
+    z = row // 2
+    below, above = z > 0, z < size_z - 1
+
+    def signal(where):
+        pl.semaphore_signal(
+            barrier, inc=1, device_id=where, device_id_type=pl.DeviceIdType.MESH
+        )
+
+    barrier = pltpu.get_barrier_semaphore()
+    for mask in range(1, size_cols):
+        signal({"col": col ^ mask})
+    signal({"row": row ^ 1})
+
+    @pl.when(below)
+    def _():
+        signal({"row": row - 2})
+
+    @pl.when(above)
+    def _():
+        signal({"row": row + 2})
+
+    pl.semaphore_wait(barrier, size_cols + below.astype(jnp.int32) + above.astype(jnp.int32))
+
+    def sum_copy(mask, leaf):
+        peer = col ^ mask
+        return pltpu.make_async_remote_copy(
+            src_ref=part_ref.at[leaf, pl.ds(pl.multiple_of(peer * chunk, chunk), chunk)],
+            dst_ref=got_ref.at[mask - 1, leaf],
+            send_sem=sum_send.at[mask - 1, leaf],
+            recv_sem=sum_recv.at[mask - 1, leaf],
+            device_id={"col": peer},
+            device_id_type=pl.DeviceIdType.MESH,
+        )
+
+    def gather_copy(way, slot, source, leaf, where):
+        return pltpu.make_async_remote_copy(
+            src_ref=held_ref.at[source, leaf],
+            dst_ref=held_ref.at[source, leaf],
+            send_sem=chain_send.at[way, slot, leaf],
+            recv_sem=gather_recv.at[source, leaf],
+            device_id={"row": where},
+            device_id_type=pl.DeviceIdType.MESH,
+        )
+
+    def up(distance, leaf):
+        return gather_copy(0, distance, row - 2 * distance, leaf, row + 2)
+
+    def down(distance, leaf):
+        return gather_copy(1, distance, row + 2 * distance, leaf, row - 2)
+
+    def across(offset, leaf):
+        return gather_copy(2, offset % size_z, row + 2 * offset, leaf, row ^ 1)
+
+    matrix = sketch_ref[pl.ds(pl.multiple_of(col * cols_dev, cols_dev), cols_dev), :].T
+    for leaf in range(leaf_dev):
+        part_ref[leaf] = lax.dot_general(
+            matrix, samples_ref[leaf], NT, preferred_element_type=jnp.float32
+        ).astype(jnp.bfloat16)
+        for mask in range(1, size_cols):
+            sum_copy(mask, leaf).start()
+
+    own = pl.ds(pl.multiple_of(col * chunk, chunk), chunk)
+    for leaf in range(leaf_dev):
+        total = part_ref[leaf, own].astype(jnp.float32)
+        for mask in range(1, size_cols):
+            sum_copy(mask, leaf).wait_recv()
+            total = total + got_ref[mask - 1, leaf].astype(jnp.float32)
+        held_ref[row, leaf] = total.astype(jnp.bfloat16)
+        pl.when(above)(lambda: up(0, leaf).start())
+        pl.when(below)(lambda: down(0, leaf).start())
+        across(0, leaf).start()
+
+    for distance in range(1, size_z):
+        for leaf in range(leaf_dev):
+
+            @pl.when(z >= distance)
+            def _():
+                up(distance, leaf).wait_recv()
+                pl.when(above)(lambda: up(distance, leaf).start())
+                across(-distance, leaf).start()
+
+            @pl.when(z + distance < size_z)
+            def _():
+                down(distance, leaf).wait_recv()
+                pl.when(below)(lambda: down(distance, leaf).start())
+                across(distance, leaf).start()
+
+    for leaf in range(leaf_dev):
+        for mask in range(1, size_cols):
+            sum_copy(mask, leaf).wait_send()
+        for other in range(size_z):
+            gather_copy(2, 0, 2 * other + 1 - row % 2, leaf, row ^ 1).wait_recv()
+        pl.when(above)(lambda: up(0, leaf).wait_send())
+        pl.when(below)(lambda: down(0, leaf).wait_send())
+        across(0, leaf).wait_send()
+        for distance in range(1, size_z):
+
+            @pl.when(z >= distance)
+            def _():
+                pl.when(above)(lambda: up(distance, leaf).wait_send())
+                across(-distance, leaf).wait_send()
+
+            @pl.when(z + distance < size_z)
+            def _():
+                pl.when(below)(lambda: down(distance, leaf).wait_send())
+                across(distance, leaf).wait_send()
+
+
+def gathered_sketch(sketch_matrix, samples, size_rows, size_cols):
+    leaf_dev, size, _ = samples.shape
+    rank = sketch_matrix.shape[1]
+    chunk = rank // size_cols
+    vmem = pl.BlockSpec(memory_space=pltpu.VMEM)
+    return pl.pallas_call(
+        front_kernel,
+        out_shape=jax.ShapeDtypeStruct((size_rows, leaf_dev, chunk, size), jnp.bfloat16),
+        in_specs=[vmem, vmem],
+        out_specs=vmem,
+        scratch_shapes=[
+            pltpu.VMEM((leaf_dev, rank, size), jnp.bfloat16),
+            pltpu.VMEM((size_cols - 1, leaf_dev, chunk, size), jnp.bfloat16),
+            pltpu.SemaphoreType.DMA((size_cols - 1, leaf_dev)),
+            pltpu.SemaphoreType.DMA((size_cols - 1, leaf_dev)),
+            pltpu.SemaphoreType.DMA((3, size_rows // 2, leaf_dev)),
+            pltpu.SemaphoreType.DMA((size_rows, leaf_dev)),
+        ],
+        compiler_params=pltpu.CompilerParams(
+            collective_id=0, has_side_effects=True, vmem_limit_bytes=32 * 2**20
+        ),
+    )(sketch_matrix, samples)
+
+
 def shards(front_blocks, block_cols, samples, sketch_matrix):
     leaf_dev, _, leaf_size, _ = front_blocks.shape
     rank = sketch_matrix.shape[1]
@@ -241,36 +380,13 @@
     leaf_total = leaf_dev * size_rows
     top_level = leaf_total.bit_length() - 1
     local_levels = leaf_dev.bit_length() - 1
-    chunk = rank // size_cols
-
-    local_rows = lax.dynamic_slice_in_dim(sketch_matrix, col * cols_dev, cols_dev, 0)
-    partial = jnp.einsum(
-        "kc,lak->lca",
-        local_rows,
-        samples.reshape(leaf_dev, leaf_size, cols_dev),
-        preferred_element_type=jnp.float32,
-    ).astype(jnp.bfloat16)
-
-    def chunk_of(owner):
-        return lax.dynamic_slice_in_dim(partial, owner * chunk, chunk, 1)
-
-    received = [swap(chunk_of(col ^ mask), "col", mask) for mask in range(1, size_cols)]
-    total = chunk_of(col).astype(jnp.float32)
-    for term in received:
-        total = total + term.astype(jnp.float32)
-    sketched = total.astype(jnp.bfloat16)
-
-    even = jnp.stack([sketched] + [swap(sketched, "row", mask) for mask in range(2, size_rows, 2)])
-    odd = swap(even, "row", 1)
-    held = jnp.concatenate([even, odd]).reshape(leaf_total, chunk, leaf_size)
+    held = gathered_sketch(
+        sketch_matrix, samples.reshape(leaf_dev, leaf_size, cols_dev), size_rows, size_cols
+    ).reshape(leaf_total, rank // size_cols, leaf_size)
     leaf_ids = row * leaf_dev + jnp.arange(leaf_dev, dtype=jnp.int32)
     apart = jnp.bitwise_xor(leaf_ids[:, None], block_cols)
     depth = sum((apart >> level > 0).astype(jnp.int32) for level in range(top_level))
-    offset = (block_cols // leaf_dev) ^ row
-    place = (offset & 1) * (size_rows // 2) + (offset >> 1)
-    source = place * leaf_dev + block_cols % leaf_dev
-
-    off_first, off_rest = off_products(front_blocks, held, source, depth, top_level)
+    off_first, off_rest = off_products(front_blocks, held, block_cols, depth, top_level)
 
     def leaf_of(off, mask):
         return lax.dynamic_index_in_dim(off, (col ^ mask) % leaf_dev, 0, keepdims=False)

time: 150 us -> 129 us (0.86)
  Pallas kernels: 51.8 us -> 85.2 us
  waiting for transfers between devices: 49 us -> 17.1 us
  starting transfers between devices: 29 us -> 15.3 us
  other arithmetic: 4.39 us -> 0.91 us
  local copies, waits for them, and re-layouts: 12.6 us -> 9.36 us
    pallas_call x0 -> x1, Pallas kernels: none -> 33.7 us  [gathered_sketch(): pl.pallas_call(front_kernel, out_shape=jax.ShapeDtypeStruct((size_rows, l...]
    ppermute x23 -> x16, waiting for transfers between devices: 49 us -> 17.1 us  [swap(): return lax.ppermute(value, axis, pairs)]
    ppermute x23 -> x16, starting transfers between devices: 29 us -> 15.3 us  [swap(): return lax.ppermute(value, axis, pairs)]
    another operation x1 -> x0, other arithmetic: 2.21 us -> none  [shards(): jnp.stack([sketched] + [swap(sketched, 'row', mask) for mask in range(2,...]
    unnamed x1 -> x0, other arithmetic: 1.95 us -> none
    unnamed x14 -> x9, local copies, waits for them, and re-layouts: 9.54 us -> 7.66 us
  transfers between devices with their start and end apart: 23 -> 16, of which waited for: 13 -> 8; matrix products, arithmetic and copies ran while one was open for 3% -> 1% of each run, Pallas kernels for 24% -> 35%
where the time goes in v4:
time: 129 us
  Pallas kernels  85.2 us (66%)
  waiting for transfers between devices  17.1 us (13%)
  starting transfers between devices  15.3 us (12%)
  local copies, waits for them, and re-layouts  9.36 us (7%)
    pallas_call x9, Pallas kernels, local_call(): pl.pallas_call(kernel, out_shape=[jax.ShapeDtypeStruct(shape, jnp.bfloat1...  47 us
    pallas_call x1, Pallas kernels, gathered_sketch(): pl.pallas_call(front_kernel, out_shape=jax.ShapeDtypeStruct((size_rows, l...  33.7 us
    ppermute x16, waiting for transfers between devices, swap(): return lax.ppermute(value, axis, pairs)  17.1 us
    ppermute x16, starting transfers between devices, swap(): return lax.ppermute(value, axis, pairs)  15.3 us
    unnamed x9, local copies, waits for them, and re-layouts  7.66 us
    pallas_call x1, Pallas kernels, off_products(): pl.pallas_call(products_kernel, grid_spec=grid_spec, out_shape=[jax.Shape...  4.56 us
  transfers between devices with their start and end apart: 16, of which 8 were waited for; matrix products, arithmetic and copies ran while one was open for 1% of the time, Pallas kernels for 35%

profile of v4, /device:TPU:0, one launch (start us, length us, event | category | flops | bytes accessed | tf_op | source)
XLA Modules:
  0.0 128.8 jit_solution(1261234842177589938)
XLA Ops:
  0.7 0.8 convert_add_fusion.depth_ref
  1.5 0.0 copy-start.1
  1.5 1.2 copy-done.1
  2.7 0.0 copy-start.2
  2.7 1.0 copy-done.2
  3.7 33.7 %shard_map.59 = bf16[8,4,64,512]{3,2,1,0:T(8,128)(2,1)S(1)} custom-call(bf16[1024,256]{1,0:T(8,128)(2,1)S(1)} %copy-done.2, bf16[4,512,256]{2,1,0:T(8,128)(2,1)S(1)} %bitcast.29), custom_call_target="tpu_custom_call" | custom-call | tf_op jit(solution)/shard_map/pallas_call | solution.py:355
  37.4 0.0 copy-start
  37.4 4.0 %copy-done = bf16[4,5,512,512]{3,2,1,0:T(8,128)(2,1)S(1)} copy-done((bf16[4,5,512,512]{3,2,1,0:T(8,128)(2,1)S(1)}, bf16[4,5,512,512]{3,2,1,0:T(8,128)(2,1)}, u32[]{:S(2)}) %copy-start) | copy-done | bytes 10485784
  41.4 0.0 copy-start.3
  41.4 0.7 copy-done.3
  42.1 4.6 %shard_map.60 = (bf16[4,64,512]{2,1,0:T(8,128)(2,1)S(1)}, bf16[4,4,64,512]{3,2,1,0:T(8,128)(2,1)S(1)}) custom-call(s32[4,5]{1,0:T(4,128)S(1)} %copy-done.3, s32[4,5]{1,0:T(4,128)S(1)} %convert_add_fusion.depth_ref, bf16[4,5,512,512]{3,2,1,0:T(8,128)(2,1)S(1)} %copy-done, bf16[32,64,512]{2,1,0:T(8,128)(2,1)S(1)} %bitcast.28), custom_call_target="tpu_custom_call" | custom-call | tf_op jit(solution)/shard_map/pallas_call | solution.py:224
  46.7 0.6 collective-permute-start
  47.3 1.4 %collective-permute-start.1 = (bf16[64,512]{1,0:T(8,128)(2,1)S(1)}, bf16[64,512]{1,0:T(8,128)(2,1)S(1)}, u32[]{:S(2)}, u32[]{:S(2)}) collective-permute-start(bf16[64,512]{1,0:T(8,128)(2,1)S(1)} %get-tuple-element.67), channel_id=1, source_target_pairs={{0,2},{1,3},{2,0},{3,1},{4,6},{5,7},{6,4},{7,5},{8,10},{9,11},{10,... | collective-permute-start | bytes 196616 | tf_op jit(solution)/shard_map/ppermute | solution.py:19
  48.7 1.6 %collective-permute-start.2 = (bf16[64,512]{1,0:T(8,128)(2,1)S(1)}, bf16[64,512]{1,0:T(8,128)(2,1)S(1)}, u32[]{:S(2)}, u32[]{:S(2)}) collective-permute-start(bf16[64,512]{1,0:T(8,128)(2,1)S(1)} %get-tuple-element.66), channel_id=1, source_target_pairs={{0,3},{1,2},{2,1},{3,0},{4,7},{5,6},{6,5},{7,4},{8,11},{9,10},{10,... | collective-permute-start | bytes 196616 | tf_op jit(solution)/shard_map/ppermute | solution.py:19
  50.3 0.9 collective-permute-done.refs_1_
  51.1 0.5 collective-permute-done.1.refs_2_
  51.6 2.3 %collective-permute-done.2.refs_3_ = bf16[64,512]{1,0:T(8,128)(2,1)S(1)} collective-permute-done((bf16[64,512]{1,0:T(8,128)(2,1)S(1)}, bf16[64,512]{1,0:T(8,128)(2,1)S(1)}, u32[]{:S(2)}, u32[]{:S(2)}) %collective-permute-start.2) | collective-permute-done | bytes 65568 | tf_op jit(solution)/shard_map/ppermute | solution.py:19
  53.9 0.1 dynamic-slice_bitcast_fusion
  53.9 0.7 collective-permute-start.3
  54.6 1.5 %collective-permute-start.4 = (bf16[4,64,512]{2,1,0:T(8,128)(2,1)S(1)}, bf16[4,64,512]{2,1,0:T(8,128)(2,1)S(1)}, u32[]{:S(2)}, u32[]{:S(2)}) collective-permute-start(bf16[4,64,512]{2,1,0:T(8,128)(2,1)S(1)} %get-tuple-element.63), channel_id=1, source_target_pairs={{0,2},{1,3},{2,0},{3,1},{4,6},{5,7},{6,4},{7,5},{8,10},{9,11},{10,... | collective-permute-start | bytes 786440 | tf_op jit(solution)/shard_map/ppermute | solution.py:19
  56.1 1.3 %collective-permute-start.5 = (bf16[4,64,512]{2,1,0:T(8,128)(2,1)S(1)}, bf16[4,64,512]{2,1,0:T(8,128)(2,1)S(1)}, u32[]{:S(2)}, u32[]{:S(2)}) collective-permute-start(bf16[4,64,512]{2,1,0:T(8,128)(2,1)S(1)} %get-tuple-element.62), channel_id=1, source_target_pairs={{0,3},{1,2},{2,1},{3,0},{4,7},{5,6},{6,5},{7,4},{8,11},{9,10},{10,... | collective-permute-start | bytes 786440 | tf_op jit(solution)/shard_map/ppermute | solution.py:19
  57.5 9.0 %shard_map.61 = (bf16[256,512]{1,0:T(8,128)(2,1)S(1)}, bf16[512,256]{1,0:T(8,128)(2,1)S(1)}) custom-call(s32[1]{0:T(128)} %bitcast.col_ref, bf16[64,512]{1,0:T(8,128)(2,1)S(1)} %get-tuple-element.33.refs_0_, bf16[64,512]{1,0:T(8,128)(2,1)S(1)} %collective-permute-done.refs_1_, bf16[64,512]{1,0:T(8,128)(2,1)S(1)} %collective-permute-done.1.refs_2_, ...), custom_call_target="tpu_custom_call" | custom-call | flops 8000000000 | bytes 1048576 | tf_op jit(solution)/shard_map/pallas_call | solution.py:180
  66.5 0.0 collective-permute-done.3.refs_1_
  66.5 0.4 collective-permute-done.4.refs_2_
  66.9 0.0 collective-permute-done.5.refs_3_
  66.9 1.4 %shard_map.62 = (bf16[256,256]{1,0:T(8,128)(2,1)S(1)}, bf16[3,256,256]{2,1,0:T(8,128)(2,1)S(1)}) custom-call(s32[1]{0:T(128)} %bitcast.col_ref, bf16[256,512]{1,0:T(8,128)(2,1)S(1)} %get-tuple-element.37.basis_ref, bf16[4,64,512]{2,1,0:T(8,128)(2,1)S(1)} %get-tuple-element.65.refs_0_, bf16[4,64,512]{2,1,0:T(8,128)(2,1)S(1)} %collective-permute-done.3.refs_1_, ...), custom_call_target="tpu_custom_call" | custom-call | bytes 1048576 | tf_op jit(solution)/shard_map/pallas_call | solution.py:180
  68.3 1.4 %collective-permute-start.6 = (bf16[256,256]{1,0:T(8,128)(2,1)S(1)}, bf16[256,256]{1,0:T(8,128)(2,1)S(1)}, u32[]{:S(2)}, u32[]{:S(2)}) collective-permute-start(bf16[256,256]{1,0:T(8,128)(2,1)S(1)} %get-tuple-element.39.own_ref), channel_id=1, source_target_pairs={{0,1},{1,0},{2,3},{3,2},{4,5},{5,4},{6,7},{7,6},{8,9},{9,8},{10,11... | collective-permute-start | bytes 393224 | tf_op jit(solution)/shard_map/ppermute | solution.py:19
  69.7 4.7 %collective-permute-done.6.partner_ref = bf16[256,256]{1,0:T(8,128)(2,1)S(1)} collective-permute-done((bf16[256,256]{1,0:T(8,128)(2,1)S(1)}, bf16[256,256]{1,0:T(8,128)(2,1)S(1)}, u32[]{:S(2)}, u32[]{:S(2)}) %collective-permute-start.6) | collective-permute-done | bytes 131104 | tf_op jit(solution)/shard_map/ppermute | solution.py:19
  74.4 1.4 %collective-permute-start.7 = (bf16[3,256,256]{2,1,0:T(8,128)(2,1)S(1)}, bf16[3,256,256]{2,1,0:T(8,128)(2,1)S(1)}, u32[]{:S(2)}, u32[]{:S(2)}) collective-permute-start(bf16[3,256,256]{2,1,0:T(8,128)(2,1)S(1)} %get-tuple-element.41.own_ref), channel_id=1, source_target_pairs={{0,1},{1,0},{2,3},{3,2},{4,5},{5,4},{6,7},{7,6},{8,9},{9,8},{10,11... | collective-permute-start | bytes 1179656 | tf_op jit(solution)/shard_map/ppermute | solution.py:19
  75.7 9.0 %shard_map.63 = (bf16[256,256]{1,0:T(8,128)(2,1)S(1)}, bf16[256,256]{1,0:T(8,128)(2,1)S(1)}) custom-call(bf16[256,256]{1,0:T(8,128)(2,1)S(1)} %get-tuple-element.39.own_ref, bf16[256,256]{1,0:T(8,128)(2,1)S(1)} %collective-permute-done.6.partner_ref), custom_call_target="tpu_custom_call" | custom-call | flops 8000000000 | bytes 1048576 | tf_op jit(solution)/shard_map/pallas_call | solution.py:180
  84.8 0.0 collective-permute-done.7.partner_ref
  84.8 0.4 shard_map.64
  85.2 0.8 collective-permute-start.8
  86.0 4.9 %collective-permute-done.8.partner_ref = bf16[256,256]{1,0:T(8,128)(2,1)S(1)} collective-permute-done((bf16[256,256]{1,0:T(8,128)(2,1)S(1)}, bf16[256,256]{1,0:T(8,128)(2,1)S(1)}, u32[]{:S(2)}, u32[]{:S(2)}) %collective-permute-start.8) | collective-permute-done | bytes 131104 | tf_op jit(solution)/shard_map/ppermute | solution.py:19
  90.9 0.8 collective-permute-start.9
  91.6 8.9 %shard_map.65 = (bf16[256,256]{1,0:T(8,128)(2,1)S(1)}, bf16[256,256]{1,0:T(8,128)(2,1)S(1)}) custom-call(bf16[256,256]{1,0:T(8,128)(2,1)S(1)} %get-tuple-element.45.own_ref, bf16[256,256]{1,0:T(8,128)(2,1)S(1)} %collective-permute-done.8.partner_ref), custom_call_target="tpu_custom_call" | custom-call | flops 8000000000 | bytes 1048576 | tf_op jit(solution)/shard_map/pallas_call | solution.py:180
  100.5 0.0 collective-permute-done.9.partner_ref
  100.5 0.3 shard_map.66
  100.8 0.1 collective-permute-start.10
  100.9 1.3 %collective-permute-done.10.partner_ref = bf16[256,256]{1,0:T(8,128)(2,1)S(1)} collective-permute-done((bf16[256,256]{1,0:T(8,128)(2,1)S(1)}, bf16[256,256]{1,0:T(8,128)(2,1)S(1)}, u32[]{:S(2)}, u32[]{:S(2)}) %collective-permute-start.10) | collective-permute-done | bytes 131104 | tf_op jit(solution)/shard_map/ppermute | solution.py:19
  102.3 0.1 collective-permute-start.14
  102.4 9.1 %shard_map.67 = (bf16[256,256]{1,0:T(8,128)(2,1)S(1)}, bf16[256,256]{1,0:T(8,128)(2,1)S(1)}) custom-call(bf16[256,256]{1,0:T(8,128)(2,1)S(1)} %get-tuple-element.51.own_ref, bf16[256,256]{1,0:T(8,128)(2,1)S(1)} %collective-permute-done.10.partner_ref), custom_call_target="tpu_custom_call" | custom-call | flops 8000000000 | bytes 1048576 | tf_op jit(solution)/shard_map/pallas_call | solution.py:180
  111.5 0.0 collective-permute-done.14.partner_ref
  111.5 0.3 shard_map.68.own_ref
  111.8 0.1 collective-permute-start.15
  111.9 1.6 %collective-permute-start.13 = (bf16[512,256]{1,0:T(8,128)(2,1)S(1)}, bf16[512,256]{1,0:T(8,128)(2,1)S(1)}, u32[]{:S(2)}, u32[]{:S(2)}) collective-permute-start(bf16[512,256]{1,0:T(8,128)(2,1)S(1)} %get-tuple-element.55), channel_id=1, source_target_pairs={{0,3},{1,2},{2,1},{3,0},{4,7},{5,6},{6,5},{7,4},{8,11},{9,10},{10,... | collective-permute-start | bytes 786440 | tf_op jit(solution)/shard_map/ppermute | solution.py:19
  113.5 1.1 collective-permute-start.12
  114.6 0.9 collective-permute-start.11
  115.5 2.1 %collective-permute-done.15.partner_ref = bf16[256,256]{1,0:T(8,128)(2,1)S(1)} collective-permute-done((bf16[256,256]{1,0:T(8,128)(2,1)S(1)}, bf16[256,256]{1,0:T(8,128)(2,1)S(1)}, u32[]{:S(2)}, u32[]{:S(2)}) %collective-permute-start.15) | collective-permute-done | bytes 131104 | tf_op jit(solution)/shard_map/ppermute | solution.py:19
  117.6 8.7 %shard_map.69 = bf16[256,256]{1,0:T(8,128)(2,1)S(1)} custom-call(bf16[256,256]{1,0:T(8,128)(2,1)S(1)} %shard_map.68.own_ref, bf16[256,256]{1,0:T(8,128)(2,1)S(1)} %collective-permute-done.15.partner_ref), custom_call_target="tpu_custom_call" | custom-call | flops 8000000000 | bytes 1048576 | tf_op jit(solution)/shard_map/pallas_call | solution.py:180
  126.4 0.7 copy.6
  127.1 0.0 collective-permute-done.13
  127.1 0.0 collective-permute-done.12
  127.1 0.0 collective-permute-done.11
  127.1 0.1 pad_maximum_fusion
  127.3 1.6 %gather_fusion = bf16[4,512,256]{2,1,0:T(8,128)(2,1)} fusion(bf16[4,512,256]{2,1,0:T(8,128)(2,1)S(1)} %pad_maximum_fusion, s32[1024]{0:T(1024)S(1)} %pad_clamp_fusion), kind=kCustom, calls=%fused_computation | custom fusion | bytes 2097168 | tf_op jit(solution)/shard_map/gather | solution.py:425
  (5 shorter events, 0.1 us)
Async XLA Ops:
  1.5 1.2 copy-start.1
  2.7 1.0 copy-start.2
  37.4 4.0 %copy-start = (bf16[4,5,512,512]{3,2,1,0:T(8,128)(2,1)S(1)}, bf16[4,5,512,512]{3,2,1,0:T(8,128)(2,1)}, u32[]{:S(2)}) copy-start(bf16[4,5,512,512]{3,2,1,0:T(8,128)(2,1)} %blocks_ref.1) | copy-start | bytes 31457284
  41.4 0.7 copy-start.3
  46.7 4.4 %collective-permute-start = (bf16[64,512]{1,0:T(8,128)(2,1)S(1)}, bf16[64,512]{1,0:T(8,128)(2,1)S(1)}, u32[]{:S(2)}, u32[]{:S(2)}) collective-permute-start(bf16[64,512]{1,0:T(8,128)(2,1)S(1)} %get-tuple-element.68), channel_id=1, source_target_pairs={{0,1},{1,0},{2,3},{3,2},{4,5},{5,4},{6,7},{7,6},{8,9},{9,8},{10,11... | collective-permute-start | bytes 196616 | tf_op jit(solution)/shard_map/ppermute | solution.py:19
  47.3 4.3 %collective-permute-start.1 = (bf16[64,512]{1,0:T(8,128)(2,1)S(1)}, bf16[64,512]{1,0:T(8,128)(2,1)S(1)}, u32[]{:S(2)}, u32[]{:S(2)}) collective-permute-start(bf16[64,512]{1,0:T(8,128)(2,1)S(1)} %get-tuple-element.67), channel_id=1, source_target_pairs={{0,2},{1,3},{2,0},{3,1},{4,6},{5,7},{6,4},{7,5},{8,10},{9,11},{10,... | collective-permute-start | bytes 196616 | tf_op jit(solution)/shard_map/ppermute | solution.py:19
  48.7 5.2 %collective-permute-start.2 = (bf16[64,512]{1,0:T(8,128)(2,1)S(1)}, bf16[64,512]{1,0:T(8,128)(2,1)S(1)}, u32[]{:S(2)}, u32[]{:S(2)}) collective-permute-start(bf16[64,512]{1,0:T(8,128)(2,1)S(1)} %get-tuple-element.66), channel_id=1, source_target_pairs={{0,3},{1,2},{2,1},{3,0},{4,7},{5,6},{6,5},{7,4},{8,11},{9,10},{10,... | collective-permute-start | bytes 196616 | tf_op jit(solution)/shard_map/ppermute | solution.py:19
  53.9 12.5 %collective-permute-start.3 = (bf16[4,64,512]{2,1,0:T(8,128)(2,1)S(1)}, bf16[4,64,512]{2,1,0:T(8,128)(2,1)S(1)}, u32[]{:S(2)}, u32[]{:S(2)}) collective-permute-start(bf16[4,64,512]{2,1,0:T(8,128)(2,1)S(1)} %get-tuple-element.64), channel_id=1, source_target_pairs={{0,1},{1,0},{2,3},{3,2},{4,5},{5,4},{6,7},{7,6},{8,9},{9,8},{10,11... | collective-permute-start | bytes 786440 | tf_op jit(solution)/shard_map/ppermute | solution.py:19
  54.6 12.3 %collective-permute-start.4 = (bf16[4,64,512]{2,1,0:T(8,128)(2,1)S(1)}, bf16[4,64,512]{2,1,0:T(8,128)(2,1)S(1)}, u32[]{:S(2)}, u32[]{:S(2)}) collective-permute-start(bf16[4,64,512]{2,1,0:T(8,128)(2,1)S(1)} %get-tuple-element.63), channel_id=1, source_target_pairs={{0,2},{1,3},{2,0},{3,1},{4,6},{5,7},{6,4},{7,5},{8,10},{9,11},{10,... | collective-permute-start | bytes 786440 | tf_op jit(solution)/shard_map/ppermute | solution.py:19
  56.1 10.8 %collective-permute-start.5 = (bf16[4,64,512]{2,1,0:T(8,128)(2,1)S(1)}, bf16[4,64,512]{2,1,0:T(8,128)(2,1)S(1)}, u32[]{:S(2)}, u32[]{:S(2)}) collective-permute-start(bf16[4,64,512]{2,1,0:T(8,128)(2,1)S(1)} %get-tuple-element.62), channel_id=1, source_target_pairs={{0,3},{1,2},{2,1},{3,0},{4,7},{5,6},{6,5},{7,4},{8,11},{9,10},{10,... | collective-permute-start | bytes 786440 | tf_op jit(solution)/shard_map/ppermute | solution.py:19
  68.3 6.1 %collective-permute-start.6 = (bf16[256,256]{1,0:T(8,128)(2,1)S(1)}, bf16[256,256]{1,0:T(8,128)(2,1)S(1)}, u32[]{:S(2)}, u32[]{:S(2)}) collective-permute-start(bf16[256,256]{1,0:T(8,128)(2,1)S(1)} %get-tuple-element.39.own_ref), channel_id=1, source_target_pairs={{0,1},{1,0},{2,3},{3,2},{4,5},{5,4},{6,7},{7,6},{8,9},{9,8},{10,11... | collective-permute-start | bytes 393224 | tf_op jit(solution)/shard_map/ppermute | solution.py:19
  74.4 10.4 %collective-permute-start.7 = (bf16[3,256,256]{2,1,0:T(8,128)(2,1)S(1)}, bf16[3,256,256]{2,1,0:T(8,128)(2,1)S(1)}, u32[]{:S(2)}, u32[]{:S(2)}) collective-permute-start(bf16[3,256,256]{2,1,0:T(8,128)(2,1)S(1)} %get-tuple-element.41.own_ref), channel_id=1, source_target_pairs={{0,1},{1,0},{2,3},{3,2},{4,5},{5,4},{6,7},{7,6},{8,9},{9,8},{10,11... | collective-permute-start | bytes 1179656 | tf_op jit(solution)/shard_map/ppermute | solution.py:19
  85.2 5.7 %collective-permute-start.8 = (bf16[256,256]{1,0:T(8,128)(2,1)S(1)}, bf16[256,256]{1,0:T(8,128)(2,1)S(1)}, u32[]{:S(2)}, u32[]{:S(2)}) collective-permute-start(bf16[256,256]{1,0:T(8,128)(2,1)S(1)} %get-tuple-element.45.own_ref), channel_id=1, source_target_pairs={{0,2},{1,3},{2,0},{3,1},{4,6},{5,7},{6,4},{7,5},{8,10},{9,11},{10,... | collective-permute-start | bytes 393224 | tf_op jit(solution)/shard_map/ppermute | solution.py:19
  90.9 9.6 %collective-permute-start.9 = (bf16[2,256,256]{2,1,0:T(8,128)(2,1)S(1)}, bf16[2,256,256]{2,1,0:T(8,128)(2,1)S(1)}, u32[]{:S(2)}, u32[]{:S(2)}) collective-permute-start(bf16[2,256,256]{2,1,0:T(8,128)(2,1)S(1)} %get-tuple-element.47.own_ref), channel_id=1, source_target_pairs={{0,2},{1,3},{2,0},{3,1},{4,6},{5,7},{6,4},{7,5},{8,10},{9,11},{10,... | collective-permute-start | bytes 786440 | tf_op jit(solution)/shard_map/ppermute | solution.py:19
  100.8 1.4 %collective-permute-start.10 = (bf16[256,256]{1,0:T(8,128)(2,1)S(1)}, bf16[256,256]{1,0:T(8,128)(2,1)S(1)}, u32[]{:S(2)}, u32[]{:S(2)}) collective-permute-start(bf16[256,256]{1,0:T(8,128)(2,1)S(1)} %get-tuple-element.51.own_ref), channel_id=1, source_target_pairs={{0,4},{4,0},{8,12},{12,8},{16,20},{20,16},{24,28},{28,24},{1,5},{5... | collective-permute-start | bytes 393224 | tf_op jit(solution)/shard_map/ppermute | solution.py:19
  102.3 9.2 %collective-permute-start.14 = (bf16[1,256,256]{2,1,0:T(8,128)(2,1)S(1)}, bf16[1,256,256]{2,1,0:T(8,128)(2,1)S(1)}, u32[]{:S(2)}, u32[]{:S(2)}) collective-permute-start(bf16[1,256,256]{2,1,0:T(8,128)(2,1)S(1)} %get-tuple-element.56.own_ref), channel_id=1, source_target_pairs={{0,4},{4,0},{8,12},{12,8},{16,20},{20,16},{24,28},{28,24},{1,5},{5... | collective-permute-start | bytes 393224 | tf_op jit(solution)/shard_map/ppermute | solution.py:19
  111.8 5.8 %collective-permute-start.15 = (bf16[256,256]{1,0:T(8,128)(2,1)S(1)}, bf16[256,256]{1,0:T(8,128)(2,1)S(1)}, u32[]{:S(2)}, u32[]{:S(2)}) collective-permute-start(bf16[256,256]{1,0:T(8,128)(2,1)S(1)} %shard_map.68.own_ref), channel_id=1, source_target_pairs={{0,8},{4,12},{8,0},{12,4},{16,24},{20,28},{24,16},{28,20},{1,9},{5... | collective-permute-start | bytes 393224 | tf_op jit(solution)/shard_map/ppermute | solution.py:19
  111.9 15.2 %collective-permute-start.13 = (bf16[512,256]{1,0:T(8,128)(2,1)S(1)}, bf16[512,256]{1,0:T(8,128)(2,1)S(1)}, u32[]{:S(2)}, u32[]{:S(2)}) collective-permute-start(bf16[512,256]{1,0:T(8,128)(2,1)S(1)} %get-tuple-element.55), channel_id=1, source_target_pairs={{0,3},{1,2},{2,1},{3,0},{4,7},{5,6},{6,5},{7,4},{8,11},{9,10},{10,... | collective-permute-start | bytes 786440 | tf_op jit(solution)/shard_map/ppermute | solution.py:19
  113.5 13.7 %collective-permute-start.12 = (bf16[512,256]{1,0:T(8,128)(2,1)S(1)}, bf16[512,256]{1,0:T(8,128)(2,1)S(1)}, u32[]{:S(2)}, u32[]{:S(2)}) collective-permute-start(bf16[512,256]{1,0:T(8,128)(2,1)S(1)} %get-tuple-element.55), channel_id=1, source_target_pairs={{0,2},{1,3},{2,0},{3,1},{4,6},{5,7},{6,4},{7,5},{8,10},{9,11},{10,... | collective-permute-start | bytes 786440 | tf_op jit(solution)/shard_map/ppermute | solution.py:19
  114.6 12.5 %collective-permute-start.11 = (bf16[512,256]{1,0:T(8,128)(2,1)S(1)}, bf16[512,256]{1,0:T(8,128)(2,1)S(1)}, u32[]{:S(2)}, u32[]{:S(2)}) collective-permute-start(bf16[512,256]{1,0:T(8,128)(2,1)S(1)} %get-tuple-element.55), channel_id=1, source_target_pairs={{0,1},{1,0},{2,3},{3,2},{4,5},{5,4},{6,7},{7,6},{8,9},{9,8},{10,11... | collective-permute-start | bytes 786440 | tf_op jit(solution)/shard_map/ppermute | solution.py:19

commit v5 on v4

--- a/solution.py
+++ b/solution.py
@@ -228,7 +228,7 @@
             jax.ShapeDtypeStruct((leaf_dev, ranks, size), jnp.bfloat16),
             jax.ShapeDtypeStruct((leaf_dev, levels - 1, ranks, size), jnp.bfloat16),
         ],
-        compiler_params=pltpu.CompilerParams(vmem_limit_bytes=40 * 2**20),
+        compiler_params=pltpu.CompilerParams(vmem_limit_bytes=24 * 2**20),
     )(source, depth, front_blocks, sketched)
 
 
@@ -366,7 +366,7 @@
             pltpu.SemaphoreType.DMA((size_rows, leaf_dev)),
         ],
         compiler_params=pltpu.CompilerParams(
-            collective_id=0, has_side_effects=True, vmem_limit_bytes=32 * 2**20
+            collective_id=0, has_side_effects=True, vmem_limit_bytes=12 * 2**20
         ),
     )(sketch_matrix, samples)
 

time: 129 us -> 129 us (level)
  no operation moved by 1% of the time
where the time goes in v5:
time: 129 us
  Pallas kernels  85.2 us (66%)
  waiting for transfers between devices  17.1 us (13%)
  starting transfers between devices  15.3 us (12%)
  local copies, waits for them, and re-layouts  9.36 us (7%)
    pallas_call x9, Pallas kernels, local_call(): pl.pallas_call(kernel, out_shape=[jax.ShapeDtypeStruct(shape, jnp.bfloat1...  47 us
    pallas_call x1, Pallas kernels, gathered_sketch(): pl.pallas_call(front_kernel, out_shape=jax.ShapeDtypeStruct((size_rows, l...  33.7 us
    ppermute x16, waiting for transfers between devices, swap(): return lax.ppermute(value, axis, pairs)  17.1 us
    ppermute x16, starting transfers between devices, swap(): return lax.ppermute(value, axis, pairs)  15.3 us
    unnamed x9, local copies, waits for them, and re-layouts  7.66 us
    pallas_call x1, Pallas kernels, off_products(): pl.pallas_call(products_kernel, grid_spec=grid_spec, out_shape=[jax.Shape...  4.56 us
  transfers between devices with their start and end apart: 16, of which 8 were waited for; matrix products, arithmetic and copies ran while one was open for 1% of the time, Pallas kernels for 35%

profile of v5, /device:TPU:0, one launch (start us, length us, event | category | flops | bytes accessed | tf_op | source)
XLA Modules:
  0.0 128.8 jit_solution(13439295382194601188)
XLA Ops:
  0.7 0.8 convert_add_fusion.depth_ref
  1.5 0.0 copy-start.1
  1.5 1.2 copy-done.1
  2.7 0.0 copy-start.2
  2.7 1.0 copy-done.2
  3.7 33.7 %shard_map.59 = bf16[8,4,64,512]{3,2,1,0:T(8,128)(2,1)S(1)} custom-call(bf16[1024,256]{1,0:T(8,128)(2,1)S(1)} %copy-done.2, bf16[4,512,256]{2,1,0:T(8,128)(2,1)S(1)} %bitcast.29), custom_call_target="tpu_custom_call" | custom-call | tf_op jit(solution)/shard_map/pallas_call | solution.py:355
  37.4 0.0 copy-start
  37.4 4.0 %copy-done = bf16[4,5,512,512]{3,2,1,0:T(8,128)(2,1)S(1)} copy-done((bf16[4,5,512,512]{3,2,1,0:T(8,128)(2,1)S(1)}, bf16[4,5,512,512]{3,2,1,0:T(8,128)(2,1)}, u32[]{:S(2)}) %copy-start) | copy-done | bytes 10485784
  41.4 0.0 copy-start.3
  41.4 0.7 copy-done.3
  42.1 4.6 %shard_map.60 = (bf16[4,64,512]{2,1,0:T(8,128)(2,1)S(1)}, bf16[4,4,64,512]{3,2,1,0:T(8,128)(2,1)S(1)}) custom-call(s32[4,5]{1,0:T(4,128)S(1)} %copy-done.3, s32[4,5]{1,0:T(4,128)S(1)} %convert_add_fusion.depth_ref, bf16[4,5,512,512]{3,2,1,0:T(8,128)(2,1)S(1)} %copy-done, bf16[32,64,512]{2,1,0:T(8,128)(2,1)S(1)} %bitcast.28), custom_call_target="tpu_custom_call" | custom-call | tf_op jit(solution)/shard_map/pallas_call | solution.py:224
  46.7 0.6 collective-permute-start
  47.3 1.4 %collective-permute-start.1 = (bf16[64,512]{1,0:T(8,128)(2,1)S(1)}, bf16[64,512]{1,0:T(8,128)(2,1)S(1)}, u32[]{:S(2)}, u32[]{:S(2)}) collective-permute-start(bf16[64,512]{1,0:T(8,128)(2,1)S(1)} %get-tuple-element.67), channel_id=1, source_target_pairs={{0,2},{1,3},{2,0},{3,1},{4,6},{5,7},{6,4},{7,5},{8,10},{9,11},{10,... | collective-permute-start | bytes 196616 | tf_op jit(solution)/shard_map/ppermute | solution.py:19
  48.7 1.6 %collective-permute-start.2 = (bf16[64,512]{1,0:T(8,128)(2,1)S(1)}, bf16[64,512]{1,0:T(8,128)(2,1)S(1)}, u32[]{:S(2)}, u32[]{:S(2)}) collective-permute-start(bf16[64,512]{1,0:T(8,128)(2,1)S(1)} %get-tuple-element.66), channel_id=1, source_target_pairs={{0,3},{1,2},{2,1},{3,0},{4,7},{5,6},{6,5},{7,4},{8,11},{9,10},{10,... | collective-permute-start | bytes 196616 | tf_op jit(solution)/shard_map/ppermute | solution.py:19
  50.3 0.9 collective-permute-done.refs_1_
  51.1 0.5 collective-permute-done.1.refs_2_
  51.6 2.3 %collective-permute-done.2.refs_3_ = bf16[64,512]{1,0:T(8,128)(2,1)S(1)} collective-permute-done((bf16[64,512]{1,0:T(8,128)(2,1)S(1)}, bf16[64,512]{1,0:T(8,128)(2,1)S(1)}, u32[]{:S(2)}, u32[]{:S(2)}) %collective-permute-start.2) | collective-permute-done | bytes 65568 | tf_op jit(solution)/shard_map/ppermute | solution.py:19
  53.9 0.1 dynamic-slice_bitcast_fusion
  53.9 0.7 collective-permute-start.3
  54.6 1.5 %collective-permute-start.4 = (bf16[4,64,512]{2,1,0:T(8,128)(2,1)S(1)}, bf16[4,64,512]{2,1,0:T(8,128)(2,1)S(1)}, u32[]{:S(2)}, u32[]{:S(2)}) collective-permute-start(bf16[4,64,512]{2,1,0:T(8,128)(2,1)S(1)} %get-tuple-element.63), channel_id=1, source_target_pairs={{0,2},{1,3},{2,0},{3,1},{4,6},{5,7},{6,4},{7,5},{8,10},{9,11},{10,... | collective-permute-start | bytes 786440 | tf_op jit(solution)/shard_map/ppermute | solution.py:19
  56.1 1.3 %collective-permute-start.5 = (bf16[4,64,512]{2,1,0:T(8,128)(2,1)S(1)}, bf16[4,64,512]{2,1,0:T(8,128)(2,1)S(1)}, u32[]{:S(2)}, u32[]{:S(2)}) collective-permute-start(bf16[4,64,512]{2,1,0:T(8,128)(2,1)S(1)} %get-tuple-element.62), channel_id=1, source_target_pairs={{0,3},{1,2},{2,1},{3,0},{4,7},{5,6},{6,5},{7,4},{8,11},{9,10},{10,... | collective-permute-start | bytes 786440 | tf_op jit(solution)/shard_map/ppermute | solution.py:19
  57.5 9.0 %shard_map.61 = (bf16[256,512]{1,0:T(8,128)(2,1)S(1)}, bf16[512,256]{1,0:T(8,128)(2,1)S(1)}) custom-call(s32[1]{0:T(128)} %bitcast.col_ref, bf16[64,512]{1,0:T(8,128)(2,1)S(1)} %get-tuple-element.33.refs_0_, bf16[64,512]{1,0:T(8,128)(2,1)S(1)} %collective-permute-done.refs_1_, bf16[64,512]{1,0:T(8,128)(2,1)S(1)} %collective-permute-done.1.refs_2_, ...), custom_call_target="tpu_custom_call" | custom-call | flops 8000000000 | bytes 1048576 | tf_op jit(solution)/shard_map/pallas_call | solution.py:180
  66.5 0.0 collective-permute-done.3.refs_1_
  66.5 0.4 collective-permute-done.4.refs_2_
  66.9 0.0 collective-permute-done.5.refs_3_
  66.9 1.4 %shard_map.62 = (bf16[256,256]{1,0:T(8,128)(2,1)S(1)}, bf16[3,256,256]{2,1,0:T(8,128)(2,1)S(1)}) custom-call(s32[1]{0:T(128)} %bitcast.col_ref, bf16[256,512]{1,0:T(8,128)(2,1)S(1)} %get-tuple-element.37.basis_ref, bf16[4,64,512]{2,1,0:T(8,128)(2,1)S(1)} %get-tuple-element.65.refs_0_, bf16[4,64,512]{2,1,0:T(8,128)(2,1)S(1)} %collective-permute-done.3.refs_1_, ...), custom_call_target="tpu_custom_call" | custom-call | bytes 1048576 | tf_op jit(solution)/shard_map/pallas_call | solution.py:180
  68.3 1.4 %collective-permute-start.6 = (bf16[256,256]{1,0:T(8,128)(2,1)S(1)}, bf16[256,256]{1,0:T(8,128)(2,1)S(1)}, u32[]{:S(2)}, u32[]{:S(2)}) collective-permute-start(bf16[256,256]{1,0:T(8,128)(2,1)S(1)} %get-tuple-element.39.own_ref), channel_id=1, source_target_pairs={{0,1},{1,0},{2,3},{3,2},{4,5},{5,4},{6,7},{7,6},{8,9},{9,8},{10,11... | collective-permute-start | bytes 393224 | tf_op jit(solution)/shard_map/ppermute | solution.py:19
  69.7 4.7 %collective-permute-done.6.partner_ref = bf16[256,256]{1,0:T(8,128)(2,1)S(1)} collective-permute-done((bf16[256,256]{1,0:T(8,128)(2,1)S(1)}, bf16[256,256]{1,0:T(8,128)(2,1)S(1)}, u32[]{:S(2)}, u32[]{:S(2)}) %collective-permute-start.6) | collective-permute-done | bytes 131104 | tf_op jit(solution)/shard_map/ppermute | solution.py:19
  74.4 1.4 %collective-permute-start.7 = (bf16[3,256,256]{2,1,0:T(8,128)(2,1)S(1)}, bf16[3,256,256]{2,1,0:T(8,128)(2,1)S(1)}, u32[]{:S(2)}, u32[]{:S(2)}) collective-permute-start(bf16[3,256,256]{2,1,0:T(8,128)(2,1)S(1)} %get-tuple-element.41.own_ref), channel_id=1, source_target_pairs={{0,1},{1,0},{2,3},{3,2},{4,5},{5,4},{6,7},{7,6},{8,9},{9,8},{10,11... | collective-permute-start | bytes 1179656 | tf_op jit(solution)/shard_map/ppermute | solution.py:19
  75.7 9.0 %shard_map.63 = (bf16[256,256]{1,0:T(8,128)(2,1)S(1)}, bf16[256,256]{1,0:T(8,128)(2,1)S(1)}) custom-call(bf16[256,256]{1,0:T(8,128)(2,1)S(1)} %get-tuple-element.39.own_ref, bf16[256,256]{1,0:T(8,128)(2,1)S(1)} %collective-permute-done.6.partner_ref), custom_call_target="tpu_custom_call" | custom-call | flops 8000000000 | bytes 1048576 | tf_op jit(solution)/shard_map/pallas_call | solution.py:180
  84.8 0.0 collective-permute-done.7.partner_ref
  84.8 0.4 shard_map.64
  85.2 0.8 collective-permute-start.8
  86.0 4.9 %collective-permute-done.8.partner_ref = bf16[256,256]{1,0:T(8,128)(2,1)S(1)} collective-permute-done((bf16[256,256]{1,0:T(8,128)(2,1)S(1)}, bf16[256,256]{1,0:T(8,128)(2,1)S(1)}, u32[]{:S(2)}, u32[]{:S(2)}) %collective-permute-start.8) | collective-permute-done | bytes 131104 | tf_op jit(solution)/shard_map/ppermute | solution.py:19
  90.9 0.8 collective-permute-start.9
  91.6 8.9 %shard_map.65 = (bf16[256,256]{1,0:T(8,128)(2,1)S(1)}, bf16[256,256]{1,0:T(8,128)(2,1)S(1)}) custom-call(bf16[256,256]{1,0:T(8,128)(2,1)S(1)} %get-tuple-element.45.own_ref, bf16[256,256]{1,0:T(8,128)(2,1)S(1)} %collective-permute-done.8.partner_ref), custom_call_target="tpu_custom_call" | custom-call | flops 8000000000 | bytes 1048576 | tf_op jit(solution)/shard_map/pallas_call | solution.py:180
  100.5 0.0 collective-permute-done.9.partner_ref
  100.5 0.3 shard_map.66
  100.8 0.1 collective-permute-start.10
  100.9 1.3 %collective-permute-done.10.partner_ref = bf16[256,256]{1,0:T(8,128)(2,1)S(1)} collective-permute-done((bf16[256,256]{1,0:T(8,128)(2,1)S(1)}, bf16[256,256]{1,0:T(8,128)(2,1)S(1)}, u32[]{:S(2)}, u32[]{:S(2)}) %collective-permute-start.10) | collective-permute-done | bytes 131104 | tf_op jit(solution)/shard_map/ppermute | solution.py:19
  102.3 0.1 collective-permute-start.14
  102.4 9.1 %shard_map.67 = (bf16[256,256]{1,0:T(8,128)(2,1)S(1)}, bf16[256,256]{1,0:T(8,128)(2,1)S(1)}) custom-call(bf16[256,256]{1,0:T(8,128)(2,1)S(1)} %get-tuple-element.51.own_ref, bf16[256,256]{1,0:T(8,128)(2,1)S(1)} %collective-permute-done.10.partner_ref), custom_call_target="tpu_custom_call" | custom-call | flops 8000000000 | bytes 1048576 | tf_op jit(solution)/shard_map/pallas_call | solution.py:180
  111.5 0.0 collective-permute-done.14.partner_ref
  111.5 0.3 shard_map.68.own_ref
  111.8 0.1 collective-permute-start.15
  111.9 1.6 %collective-permute-start.13 = (bf16[512,256]{1,0:T(8,128)(2,1)S(1)}, bf16[512,256]{1,0:T(8,128)(2,1)S(1)}, u32[]{:S(2)}, u32[]{:S(2)}) collective-permute-start(bf16[512,256]{1,0:T(8,128)(2,1)S(1)} %get-tuple-element.55), channel_id=1, source_target_pairs={{0,3},{1,2},{2,1},{3,0},{4,7},{5,6},{6,5},{7,4},{8,11},{9,10},{10,... | collective-permute-start | bytes 786440 | tf_op jit(solution)/shard_map/ppermute | solution.py:19
  113.5 1.1 collective-permute-start.12
  114.6 0.9 collective-permute-start.11
  115.5 2.1 %collective-permute-done.15.partner_ref = bf16[256,256]{1,0:T(8,128)(2,1)S(1)} collective-permute-done((bf16[256,256]{1,0:T(8,128)(2,1)S(1)}, bf16[256,256]{1,0:T(8,128)(2,1)S(1)}, u32[]{:S(2)}, u32[]{:S(2)}) %collective-permute-start.15) | collective-permute-done | bytes 131104 | tf_op jit(solution)/shard_map/ppermute | solution.py:19
  117.6 8.7 %shard_map.69 = bf16[256,256]{1,0:T(8,128)(2,1)S(1)} custom-call(bf16[256,256]{1,0:T(8,128)(2,1)S(1)} %shard_map.68.own_ref, bf16[256,256]{1,0:T(8,128)(2,1)S(1)} %collective-permute-done.15.partner_ref), custom_call_target="tpu_custom_call" | custom-call | flops 8000000000 | bytes 1048576 | tf_op jit(solution)/shard_map/pallas_call | solution.py:180
  126.4 0.7 copy.6
  127.1 0.0 collective-permute-done.13
  127.1 0.0 collective-permute-done.12
  127.1 0.0 collective-permute-done.11
  127.1 0.1 pad_maximum_fusion
  127.3 1.6 %gather_fusion = bf16[4,512,256]{2,1,0:T(8,128)(2,1)} fusion(bf16[4,512,256]{2,1,0:T(8,128)(2,1)S(1)} %pad_maximum_fusion, s32[1024]{0:T(1024)S(1)} %pad_clamp_fusion), kind=kCustom, calls=%fused_computation | custom fusion | bytes 2097168 | tf_op jit(solution)/shard_map/gather | solution.py:425
  (5 shorter events, 0.1 us)
Async XLA Ops:
  1.5 1.2 copy-start.1
  2.7 1.0 copy-start.2
  37.4 4.0 %copy-start = (bf16[4,5,512,512]{3,2,1,0:T(8,128)(2,1)S(1)}, bf16[4,5,512,512]{3,2,1,0:T(8,128)(2,1)}, u32[]{:S(2)}) copy-start(bf16[4,5,512,512]{3,2,1,0:T(8,128)(2,1)} %blocks_ref.1) | copy-start | bytes 31457284
  41.4 0.7 copy-start.3
  46.7 4.4 %collective-permute-start = (bf16[64,512]{1,0:T(8,128)(2,1)S(1)}, bf16[64,512]{1,0:T(8,128)(2,1)S(1)}, u32[]{:S(2)}, u32[]{:S(2)}) collective-permute-start(bf16[64,512]{1,0:T(8,128)(2,1)S(1)} %get-tuple-element.68), channel_id=1, source_target_pairs={{0,1},{1,0},{2,3},{3,2},{4,5},{5,4},{6,7},{7,6},{8,9},{9,8},{10,11... | collective-permute-start | bytes 196616 | tf_op jit(solution)/shard_map/ppermute | solution.py:19
  47.3 4.3 %collective-permute-start.1 = (bf16[64,512]{1,0:T(8,128)(2,1)S(1)}, bf16[64,512]{1,0:T(8,128)(2,1)S(1)}, u32[]{:S(2)}, u32[]{:S(2)}) collective-permute-start(bf16[64,512]{1,0:T(8,128)(2,1)S(1)} %get-tuple-element.67), channel_id=1, source_target_pairs={{0,2},{1,3},{2,0},{3,1},{4,6},{5,7},{6,4},{7,5},{8,10},{9,11},{10,... | collective-permute-start | bytes 196616 | tf_op jit(solution)/shard_map/ppermute | solution.py:19
  48.7 5.2 %collective-permute-start.2 = (bf16[64,512]{1,0:T(8,128)(2,1)S(1)}, bf16[64,512]{1,0:T(8,128)(2,1)S(1)}, u32[]{:S(2)}, u32[]{:S(2)}) collective-permute-start(bf16[64,512]{1,0:T(8,128)(2,1)S(1)} %get-tuple-element.66), channel_id=1, source_target_pairs={{0,3},{1,2},{2,1},{3,0},{4,7},{5,6},{6,5},{7,4},{8,11},{9,10},{10,... | collective-permute-start | bytes 196616 | tf_op jit(solution)/shard_map/ppermute | solution.py:19
  53.9 12.5 %collective-permute-start.3 = (bf16[4,64,512]{2,1,0:T(8,128)(2,1)S(1)}, bf16[4,64,512]{2,1,0:T(8,128)(2,1)S(1)}, u32[]{:S(2)}, u32[]{:S(2)}) collective-permute-start(bf16[4,64,512]{2,1,0:T(8,128)(2,1)S(1)} %get-tuple-element.64), channel_id=1, source_target_pairs={{0,1},{1,0},{2,3},{3,2},{4,5},{5,4},{6,7},{7,6},{8,9},{9,8},{10,11... | collective-permute-start | bytes 786440 | tf_op jit(solution)/shard_map/ppermute | solution.py:19
  54.6 12.3 %collective-permute-start.4 = (bf16[4,64,512]{2,1,0:T(8,128)(2,1)S(1)}, bf16[4,64,512]{2,1,0:T(8,128)(2,1)S(1)}, u32[]{:S(2)}, u32[]{:S(2)}) collective-permute-start(bf16[4,64,512]{2,1,0:T(8,128)(2,1)S(1)} %get-tuple-element.63), channel_id=1, source_target_pairs={{0,2},{1,3},{2,0},{3,1},{4,6},{5,7},{6,4},{7,5},{8,10},{9,11},{10,... | collective-permute-start | bytes 786440 | tf_op jit(solution)/shard_map/ppermute | solution.py:19
  56.1 10.8 %collective-permute-start.5 = (bf16[4,64,512]{2,1,0:T(8,128)(2,1)S(1)}, bf16[4,64,512]{2,1,0:T(8,128)(2,1)S(1)}, u32[]{:S(2)}, u32[]{:S(2)}) collective-permute-start(bf16[4,64,512]{2,1,0:T(8,128)(2,1)S(1)} %get-tuple-element.62), channel_id=1, source_target_pairs={{0,3},{1,2},{2,1},{3,0},{4,7},{5,6},{6,5},{7,4},{8,11},{9,10},{10,... | collective-permute-start | bytes 786440 | tf_op jit(solution)/shard_map/ppermute | solution.py:19
  68.3 6.1 %collective-permute-start.6 = (bf16[256,256]{1,0:T(8,128)(2,1)S(1)}, bf16[256,256]{1,0:T(8,128)(2,1)S(1)}, u32[]{:S(2)}, u32[]{:S(2)}) collective-permute-start(bf16[256,256]{1,0:T(8,128)(2,1)S(1)} %get-tuple-element.39.own_ref), channel_id=1, source_target_pairs={{0,1},{1,0},{2,3},{3,2},{4,5},{5,4},{6,7},{7,6},{8,9},{9,8},{10,11... | collective-permute-start | bytes 393224 | tf_op jit(solution)/shard_map/ppermute | solution.py:19
  74.4 10.4 %collective-permute-start.7 = (bf16[3,256,256]{2,1,0:T(8,128)(2,1)S(1)}, bf16[3,256,256]{2,1,0:T(8,128)(2,1)S(1)}, u32[]{:S(2)}, u32[]{:S(2)}) collective-permute-start(bf16[3,256,256]{2,1,0:T(8,128)(2,1)S(1)} %get-tuple-element.41.own_ref), channel_id=1, source_target_pairs={{0,1},{1,0},{2,3},{3,2},{4,5},{5,4},{6,7},{7,6},{8,9},{9,8},{10,11... | collective-permute-start | bytes 1179656 | tf_op jit(solution)/shard_map/ppermute | solution.py:19
  85.2 5.7 %collective-permute-start.8 = (bf16[256,256]{1,0:T(8,128)(2,1)S(1)}, bf16[256,256]{1,0:T(8,128)(2,1)S(1)}, u32[]{:S(2)}, u32[]{:S(2)}) collective-permute-start(bf16[256,256]{1,0:T(8,128)(2,1)S(1)} %get-tuple-element.45.own_ref), channel_id=1, source_target_pairs={{0,2},{1,3},{2,0},{3,1},{4,6},{5,7},{6,4},{7,5},{8,10},{9,11},{10,... | collective-permute-start | bytes 393224 | tf_op jit(solution)/shard_map/ppermute | solution.py:19
  90.9 9.6 %collective-permute-start.9 = (bf16[2,256,256]{2,1,0:T(8,128)(2,1)S(1)}, bf16[2,256,256]{2,1,0:T(8,128)(2,1)S(1)}, u32[]{:S(2)}, u32[]{:S(2)}) collective-permute-start(bf16[2,256,256]{2,1,0:T(8,128)(2,1)S(1)} %get-tuple-element.47.own_ref), channel_id=1, source_target_pairs={{0,2},{1,3},{2,0},{3,1},{4,6},{5,7},{6,4},{7,5},{8,10},{9,11},{10,... | collective-permute-start | bytes 786440 | tf_op jit(solution)/shard_map/ppermute | solution.py:19
  100.8 1.4 %collective-permute-start.10 = (bf16[256,256]{1,0:T(8,128)(2,1)S(1)}, bf16[256,256]{1,0:T(8,128)(2,1)S(1)}, u32[]{:S(2)}, u32[]{:S(2)}) collective-permute-start(bf16[256,256]{1,0:T(8,128)(2,1)S(1)} %get-tuple-element.51.own_ref), channel_id=1, source_target_pairs={{0,4},{4,0},{8,12},{12,8},{16,20},{20,16},{24,28},{28,24},{1,5},{5... | collective-permute-start | bytes 393224 | tf_op jit(solution)/shard_map/ppermute | solution.py:19
  102.3 9.2 %collective-permute-start.14 = (bf16[1,256,256]{2,1,0:T(8,128)(2,1)S(1)}, bf16[1,256,256]{2,1,0:T(8,128)(2,1)S(1)}, u32[]{:S(2)}, u32[]{:S(2)}) collective-permute-start(bf16[1,256,256]{2,1,0:T(8,128)(2,1)S(1)} %get-tuple-element.56.own_ref), channel_id=1, source_target_pairs={{0,4},{4,0},{8,12},{12,8},{16,20},{20,16},{24,28},{28,24},{1,5},{5... | collective-permute-start | bytes 393224 | tf_op jit(solution)/shard_map/ppermute | solution.py:19
  111.8 5.8 %collective-permute-start.15 = (bf16[256,256]{1,0:T(8,128)(2,1)S(1)}, bf16[256,256]{1,0:T(8,128)(2,1)S(1)}, u32[]{:S(2)}, u32[]{:S(2)}) collective-permute-start(bf16[256,256]{1,0:T(8,128)(2,1)S(1)} %shard_map.68.own_ref), channel_id=1, source_target_pairs={{0,8},{4,12},{8,0},{12,4},{16,24},{20,28},{24,16},{28,20},{1,9},{5... | collective-permute-start | bytes 393224 | tf_op jit(solution)/shard_map/ppermute | solution.py:19
  111.9 15.2 %collective-permute-start.13 = (bf16[512,256]{1,0:T(8,128)(2,1)S(1)}, bf16[512,256]{1,0:T(8,128)(2,1)S(1)}, u32[]{:S(2)}, u32[]{:S(2)}) collective-permute-start(bf16[512,256]{1,0:T(8,128)(2,1)S(1)} %get-tuple-element.55), channel_id=1, source_target_pairs={{0,3},{1,2},{2,1},{3,0},{4,7},{5,6},{6,5},{7,4},{8,11},{9,10},{10,... | collective-permute-start | bytes 786440 | tf_op jit(solution)/shard_map/ppermute | solution.py:19
  113.5 13.7 %collective-permute-start.12 = (bf16[512,256]{1,0:T(8,128)(2,1)S(1)}, bf16[512,256]{1,0:T(8,128)(2,1)S(1)}, u32[]{:S(2)}, u32[]{:S(2)}) collective-permute-start(bf16[512,256]{1,0:T(8,128)(2,1)S(1)} %get-tuple-element.55), channel_id=1, source_target_pairs={{0,2},{1,3},{2,0},{3,1},{4,6},{5,7},{6,4},{7,5},{8,10},{9,11},{10,... | collective-permute-start | bytes 786440 | tf_op jit(solution)/shard_map/ppermute | solution.py:19
  114.6 12.5 %collective-permute-start.11 = (bf16[512,256]{1,0:T(8,128)(2,1)S(1)}, bf16[512,256]{1,0:T(8,128)(2,1)S(1)}, u32[]{:S(2)}, u32[]{:S(2)}) collective-permute-start(bf16[512,256]{1,0:T(8,128)(2,1)S(1)} %get-tuple-element.55), channel_id=1, source_target_pairs={{0,1},{1,0},{2,3},{3,2},{4,5},{5,4},{6,7},{7,6},{8,9},{9,8},{10,11... | collective-permute-start | bytes 786440 | tf_op jit(solution)/shard_map/ppermute | solution.py:19
